TPU v7x, 256 devices: a whole 4x4x8 slice. The times are simulated.
256 devices in a mesh: lat: 16 (over z_hi, x, core), lev: 16 (over y, z_lo).
Axes of the slice: x: 4, y: 4, z: 8 (z_hi: 2, z_lo: 4; z = z_hi * 4 + z_lo), core: 2. Of those that a mesh axis runs over, the one named last changes fastest.
Arguments:
- tracers: float32 [9, 256, 32, 1152], P(None, 'lat', 'lev'), may hold values from -6 to 6
- thickness: float32 [256, 32, 1152], P('lat', 'lev'), may hold values from 0.5 to 2
- courant_x: float32 [256, 32, 1152], P('lat', 'lev'), may hold values from -0.24 to 0.24
- courant_y: float32 [256, 32, 1152], P('lat', 'lev'), may hold values from -0.24 to 0.24
- level_index: int32 [31, 256, 1152], P(None, 'lat', 'lev'), may hold values from 0 to 31, as said below
- level_offset: int32 [31, 256, 1152], P(None, 'lat', 'lev'), may hold values from 0 to 31, as said below
- level_phase: float32 [31, 256, 1152], P(None, 'lat', 'lev'), may hold values from 0 to 1
Outputs:
- layer_mass: float32 [10, 256, 32, 1152], P(None, 'lat', 'lev')
Inputs may be any that keep to these rules, and one draw needn't show every extreme that they name: Along the interfaces of a column, 32 level_index + level_offset rises strictly; each column follows a stretched target grid of its own. `level_offset`: see level_index.
All inputs are finite; a program needn't handle non-finite values.
Results may differ from a plain program's by a relative error of at most 0.0003.
Values sent between devices are 32-bit elements; how exact they have to be, the bound alone decides.
No kernel may reach another device: no remote copies, remote signals or barrier semaphores. Data moves between devices by JAX's collectives and lax.ppermute only.
A program may use at most 128 MiB of HBM per device.

v0:
```python
import jax
import jax.numpy as jnp
from jax import lax
from jax.sharding import PartitionSpec as P

sub_units = 32.0


def extended_2(block, sides, width):
    for axis, dim in sides:
        count = lax.axis_size(axis)
        forward = [(i, i + 1) for i in range(count - 1)]
        backward = [(target, source) for source, target in forward]
        low = lax.ppermute(
            lax.slice_in_dim(block, block.shape[dim] - width, None, axis=dim), axis, forward
        )
        high = lax.ppermute(lax.slice_in_dim(block, 0, width, axis=dim), axis, backward)
        block = jnp.concatenate([low, block, high], axis=dim)
    return block


def face_values(courant, q_low, slope_low, q_high, slope_high):
    return jnp.where(
        courant > 0,
        q_low + 0.5 * (1.0 - courant) * slope_low,
        q_high - 0.5 * (1.0 + courant) * slope_high,
    )


def remap_columns(m, selector, frac):
    width, levels, columns = m.shape
    left = jnp.concatenate([m[:, :1], 0.5 * (m[:, :-1] + m[:, 1:])], 1)
    right = jnp.concatenate([left[:, 1:], m[:, -1:]], 1)
    slope = right - left
    curve = 6.0 * (m - 0.5 * (left + right))
    below = jnp.cumsum(m, axis=1) - m
    stacked = jnp.stack([below, left, slope, curve], 1).reshape(width * 4, levels, columns)
    picked = jnp.einsum("flc,nlc->fnc", stacked, selector, precision=lax.Precision.HIGHEST)
    picked = picked.reshape(width, 4, selector.shape[0], columns)
    part = picked[:, 1] * frac
    part = part + picked[:, 2] * frac * frac * 0.5
    part = part + picked[:, 3] * (frac * frac * 0.5 - frac * frac * frac / 3.0)
    inner = picked[:, 0] + part
    total = below[:, -1:] + m[:, -1:]
    edges = jnp.concatenate([jnp.zeros_like(total), inner, total], 1)
    return edges[:, 1:] - edges[:, :-1]


def shards(tracers, thickness, courant_x, courant_y, level_index, level_offset, level_phase):
    count, latd, levd, nlon = tracers.shape
    groups = lax.axis_size("lev")
    lond = nlon // groups
    stack = jnp.concatenate([tracers, thickness[None], courant_y[None]], 0)
    extended = extended_2(stack, (("lat", 1),), 2)
    near = extended[:, 1:-1]
    slope_y = (extended[:count, 2:] - extended[:count, :-2]) * 0.5
    q_rows = near[:count]
    dp_rows = near[count]
    global_row = lax.axis_index("lat") * latd + jnp.arange(latd + 1)
    faces_y = jnp.where((global_row > 0)[:, None, None], near[count + 1, 1:], 0.0)
    mass_y = jnp.where(faces_y > 0, faces_y * dp_rows[:-1], faces_y * dp_rows[1:])
    west = jnp.roll(thickness, 1, axis=2)
    mass_x = jnp.where(courant_x > 0, courant_x * west, courant_x * thickness)
    air = thickness + mass_x - jnp.roll(mass_x, -1, axis=2) + mass_y[:-1] - mass_y[1:]
    slope_x = (jnp.roll(tracers, -1, axis=3) - jnp.roll(tracers, 1, axis=3)) * 0.5
    flux_x = mass_x[None] * face_values(
        courant_x[None],
        jnp.roll(tracers, 1, axis=3),
        jnp.roll(slope_x, 1, axis=3),
        tracers,
        slope_x,
    )
    flux_y = mass_y[None] * face_values(
        faces_y[None], q_rows[:, :-1], slope_y[:, :-1], q_rows[:, 1:], slope_y[:, 1:]
    )
    mass = (
        thickness[None] * tracers
        + flux_x
        - jnp.roll(flux_x, -1, axis=3)
        + flux_y[:, :-1]
        - flux_y[:, 1:]
    )
    fields = jnp.concatenate([mass, air[None]], 0)
    width = fields.shape[0]
    ordered = (
        fields.reshape(width, latd, levd, groups, lond)
        .transpose(0, 3, 2, 1, 4)
        .reshape(width, groups, levd, latd * lond)
    )
    interfaces = level_index.shape[0]
    index_cols = level_index.reshape(interfaces, latd * lond)
    offset_cols = level_offset.reshape(interfaces, latd * lond)
    phase_cols = level_phase.reshape(interfaces, latd * lond)
    levels_all = groups * levd
    selector = (
        index_cols[:, None, :] == jnp.arange(levels_all, dtype=jnp.int32)[None, :, None]
    ).astype(jnp.float32)
    frac = (offset_cols.astype(jnp.float32) + phase_cols) / sub_units
    columns = lax.all_to_all(ordered, "lev", split_axis=1, concat_axis=2, tiled=True)
    layers = remap_columns(columns[:, 0], selector, frac)[:, None]
    returned = lax.all_to_all(layers, "lev", split_axis=2, concat_axis=1, tiled=True)
    result = returned.reshape(width, groups, levd, latd, lond).transpose(0, 3, 2, 1, 4)
    return result.reshape(width, latd, levd, nlon)


def solution(mesh):
    in_specs = (
        P(None, "lat", "lev", None),
        P("lat", "lev", None),
        P("lat", "lev", None),
        P("lat", "lev", None),
        P(None, "lat", "lev"),
        P(None, "lat", "lev"),
        P(None, "lat", "lev"),
    )
    out_specs = P(None, "lat", "lev", None)
    return jax.shard_map(shards, mesh=mesh, in_specs=in_specs, out_specs=out_specs, check_vma=False)
```

profile of v0, /device:TPU:2, one launch (start us, length us, event | category | flops | bytes accessed | tf_op | source)
XLA Modules:
  0.0 227.6 jit_solution(2990740967895079912)
XLA Ops:
  0.0 2.1 pad_maximum_fusion.5
  2.1 1.9 collective-permute-start
  4.0 2.4 %collective-permute-start.1 = (f32[11,2,2,1152]{3,2,1,0:T(2,128)}, f32[11,2,2,1152]{3,2,1,0:T(2,128)S(1)}, u32[]{:S(2)}, u32[]{:S(2)}) collective-permute-start(f32[11,2,2,1152]{3,2,1,0:T(2,128)} %get-tuple-element.22), channel_id=1, source_target_pairs={{0,16},{16,32},{32,48},{48,64},{64,80},{80,96},{96,112},{112,128},... | collective-permute-start | bytes 608264 | tf_op jit(solution)/shard_map/ppermute | solution.py:14
  6.4 0.0 copy-done.3
  6.5 0.1 slice.146
  6.5 1.8 fusion.29
  8.4 0.2 fusion.30
  8.6 0.0 copy-start.11
  8.6 2.8 %broadcast_multiply_fusion = f32[9,16,2,1152]{3,2,1,0:T(2,128)S(1)} fusion(f32[9,16,2,1151]{3,2,1,0:T(2,128)S(1)} %get-tuple-element.25, f32[9,16,2,1]{3,2,1,0:T(2,128)S(1)} %get-tuple-element.27, f32[9,16,2,1]{3,2,1,0:T(2,128)S(1)} %get-tuple-element.26, f32[9,16,2,1151]{3,2,1,0:T(2,128)S(1)} %get-tuple-element.24), kind=kLoop, calls=%fused_computation.48 | loop fusion | flops 1327104 | bytes 3981312 | tf_op jit(solution)/shard_map/mul | solution.py:65
  11.4 0.2 slice.184
  11.6 0.1 broadcast_compare_fusion.1
  11.7 0.3 subtract_multiply_fusion
  12.0 3.8 %fusion.22 = f32[9,16,2,1152]{3,2,1,0:T(2,128)S(1)} fusion(f32[9,16,2,1151]{3,2,1,0:T(2,128)S(1)} %bitcast.104, f32[9,16,2,1]{3,2,1,0:T(2,128)S(1)} %slice.184, f32[9,16,2,1152]{3,2,1,0:T(2,128)S(1)} %copy-done, pred[16,2,1152]{2,1,0:T(4,128)(4,1)S(1)} %broadcast_compare_fusion.1, f32[16,2,1152]{2,1,0:T(2,128)S(1)} %get-tuple-element.32, ...), kind=kLoop, calls=%fused_computation.46 | loop fusion | flops 3317760 | bytes 7114752 | tf_op jit(solution)/shard_map/mul | solution.py:66
  15.8 0.0 copy-start.1
  15.8 0.0 copy-start.5
  15.9 1.1 slice.196
  16.9 2.5 %slice.186 = f32[9,16,2,1151]{3,2,1,0:T(2,128)} slice(f32[9,16,2,1152]{3,2,1,0:T(2,128)S(1)} %fusion.22), slice={[0:9], [0:16], [0:2], [1:1152]} | slice | bytes 2651904 | tf_op jit(solution)/shard_map/jit(_roll_static)/slice | solution.py:79
  19.5 0.0 collective-permute-done
  19.5 0.0 collective-permute-done.1
  19.5 0.0 copy-done.5
  19.5 0.0 copy-start.7
  19.5 0.9 select_bitcast_fusion
  20.4 0.0 copy-done.1
  20.4 0.8 fusion.26
  21.2 0.9 multiply_bitcast_fusion.1
  22.2 0.2 compare_select_fusion
  22.4 0.2 slice_subtract_fusion.2
  22.6 0.3 concatenate.105
  22.9 0.2 copy.46
  23.0 3.1 %pad_maximum_fusion.3 = (f32[11,18,2,1152]{3,2,1,0:T(2,128)S(1)}, f32[11,18,2,1152]{3,2,1,0:T(2,128)S(1)}) fusion(f32[11,2,2,1152]{3,2,1,0:T(2,128)} %copy-done.6, f32[1,16,2,1152]{3,2,1,0:T(2,128)S(1)} %bitcast.108, f32[1,16,2,1152]{3,2,1,0:T(2,128)S(1)} %bitcast.103, f32[9,16,2,1152]{3,2,1,0:T(2,128)S(1)} %copy-done, f32[11,2,2,1152]{3,2,1,0:T(2,128)} %copy-done.7), kind=kLoop, calls=%fused_computation.29 | loop fusion | flops 2737152 | bytes 5677056 | tf_op jit(solution)/shard_map/concatenate | solution.py:18
  26.2 1.0 fusion.15
  27.2 0.0 copy-done.10
  27.2 0.1 copy-done.13
  27.3 1.8 fusion.18
  29.1 2.8 %slice_subtract_fusion.1 = f32[9,16,2,1152]{3,2,1,0:T(2,128)} fusion(f32[9,17,2,1152]{3,2,1,0:T(2,128)S(1)} %fusion.18, f32[9,16,2,1]{3,2,1,0:T(2,128)S(1)} %slice-done, f32[9,16,2,1151]{3,2,1,0:T(2,128)S(1)} %copy-done.4, f32[9,16,2,1152]{3,2,1,0:T(2,128)S(1)} %copy-done.2, f32[9,16,2,1152]{3,2,1,0:T(2,128)S(1)} %copy-done, f32[16,2,1152]{2,1,0:T(2,128)S(1)} %copy-done.3), kind=kLoop, calls=%fused_computation.39 | loop fusion | flops 1990656 | bytes 8110080 | tf_op jit(solution)/shard_map/sub | solution.py:77
  31.9 3.9 %concatenate.103 = f32[9,16,2,16,72]{4,3,2,1,0:T(8,128)S(1)} reshape(f32[9,16,2,1152]{3,2,1,0:T(2,128)} %slice_subtract_fusion.1) | data formatting | bytes 2654208 | tf_op jit(solution)/shard_map/concatenate | solution.py:83
  35.8 1.4 copy.45
  37.2 0.2 maximum_bitcast_fusion
  37.4 2.5 %reshape.218 = f32[10,16,2,1152]{3,1,2,0:T(8,128)} reshape(f32[10,16,2,16,72]{4,3,1,2,0:T(8,128)S(1)} %maximum_bitcast_fusion) | data formatting | bytes 2949120 | tf_op jit(solution)/shard_map/reshape | solution.py:88
  39.9 3.3 %copy.47 = f32[10,16,2,1152]{3,2,0,1:T(2,128)} copy(f32[10,16,2,1152]{3,1,2,0:T(8,128)} %reshape.218) | data formatting | bytes 2949120 | tf_op jit(solution)/shard_map/reshape | solution.py:88
  43.2 8.8 %all-to-all-start = ((f32[10,16,2,1152]{3,2,0,1:T(2,128)}), f32[10,16,2,1152]{3,2,0,1:T(2,128)S(1)}, u32[]{:S(2)}, u32[]{:S(2)}) async-start(f32[10,16,2,1152]{3,2,0,1:T(2,128)} %copy.47), calls=%async_computation | async-start | bytes 2949120 | tf_op jit(solution)/shard_map/all_to_all | solution.py:99
  52.0 0.3 copy.61
  52.3 0.2 div.16
  52.5 41.6 %all-to-all-done = f32[10,16,2,1152]{3,2,0,1:T(2,128)S(1)} async-done(((f32[10,16,2,1152]{3,2,0,1:T(2,128)}), f32[10,16,2,1152]{3,2,0,1:T(2,128)S(1)}, u32[]{:S(2)}, u32[]{:S(2)}) %all-to-all-start) | async-done | bytes 1474592 | tf_op jit(solution)/shard_map/all_to_all | solution.py:99
  94.1 0.3 copy.48
  94.4 17.3 %fusion.31 = f32[10,32,1152]{2,0,1:T(8,128)S(1)} fusion(f32[10,32,1152]{2,0,1:T(8,128)S(1)} %bitcast.92), kind=kOutput, calls=%fused_computation.86 | output fusion | flops 11427840 | bytes 2949120 | tf_op jit(solution)/shard_map/jit(cumsum)/reduce_window_sum | solution.py:36
  111.7 0.2 fusion.34
  111.9 0.2 fusion.5
  112.1 0.2 maximum_bitcast_fusion.1
  112.2 0.6 fusion.14
  112.8 0.8 pad_maximum_fusion
  113.6 4.3 %copy.50 = f32[10,4,32,1152]{3,2,1,0:T(8,128)} copy(f32[10,4,32,1152]{3,0,2,1:T(8,128)S(1)} %pad_maximum_fusion) | data formatting | bytes 11796480 | tf_op jit(solution)/shard_map/stack | solution.py:37
  117.9 16.3 %copy.51 = f32[40,32,1152]{0,1,2:T(8,128)} copy(f32[40,32,1152]{2,1,0:T(8,128)} %bitcast.98) | data formatting | bytes 11796480 | tf_op jit(solution)/shard_map/reshape | solution.py:37
  134.2 16.2 %fusion.2 = f32[40,31,1152]{0,1,2:T(8,128)} fusion(f32[40,32,1152]{0,1,2:T(8,128)} %copy.51, s32[31,1152]{0,1:T(8,128)S(1)} %bitcast.105), kind=kOutput, calls=%fused_computation.4 | convolution fusion | flops 549679104 | bytes 11755008 | tf_op jit(solution)/shard_map/flc,nlc->fnc/dot_general | solution.py:38
  150.4 16.4 %copy.52 = f32[40,31,1152]{2,1,0:T(8,128)} copy(f32[40,31,1152]{0,1,2:T(8,128)} %fusion.2) | data formatting | bytes 11427840 | tf_op jit(solution)/shard_map/flc,nlc->fnc/transpose | solution.py:38
  166.7 3.2 %fusion.27 = (f32[10,1,31,1152]{3,2,1,0:T(8,128)S(1)}, f32[10,1,31,1152]{3,2,1,0:T(8,128)S(1)}, f32[10,1,31,1152]{3,2,1,0:T(8,128)S(1)}, f32[10,1,31,1152]{3,2,1,0:T(8,128)S(1)}) fusion(f32[10,4,31,1152]{3,2,1,0:T(8,128)} %bitcast.97), kind=kLoop, calls=%fused_computation.82 | loop fusion | bytes 11427840 | tf_op jit(solution)/shard_map/slice | solution.py:43
  169.9 3.3 %fusion.8 = f32[10,31,1152]{2,0,1:T(8,128)S(1)} fusion(f32[10,1,31,1152]{3,2,1,0:T(8,128)S(1)} %get-tuple-element.12, f32[10,1,31,1152]{3,2,1,0:T(8,128)S(1)} %get-tuple-element.10, f32[10,1,31,1152]{3,2,1,0:T(8,128)S(1)} %get-tuple-element.11, f32[10,1,31,1152]{3,2,1,0:T(8,128)S(1)} %get-tuple-element.9, f32[31,1152]{1,0:T(8,128)S(1)} %fusion.23, ...), kind=kLoop, calls=%fused_computation.19 | loop fusion | flops 2856960 | bytes 7428096 | tf_op jit(solution)/shard_map/add | solution.py:43
  173.3 0.2 fusion.3
  173.4 1.5 copy.57
  175.0 39.9 %all_to_all.8 = f32[10,1,32,1152]{3,1,0,2:T(1,128)S(1)} all-to-all(f32[10,1,32,1152]{3,1,0,2:T(1,128)S(1)} %copy.57), channel_id=1, replica_groups=mesh['lat'=16,'lev'=16] {'lev'}, dimensions={2} | all-to-all | bytes 2949120 | tf_op jit(solution)/shard_map/all_to_all | solution.py:101
  214.9 1.2 copy.58
  216.1 3.3 %reshape.221 = f32[10,16,2,16,72]{4,3,2,1,0:T(8,128)S(1)} reshape(f32[10,1,32,1152]{3,2,0,1:T(8,128)} %copy.58) | data formatting | bytes 2949120 | tf_op jit(solution)/shard_map/reshape | solution.py:102
  219.4 3.2 %copy.62 = f32[10,16,2,16,72]{4,3,2,1,0:T(8,128)} copy(f32[10,16,2,16,72]{4,1,2,3,0:T(8,128)S(1)} %bitcast.99) | data formatting | bytes 2949120 | tf_op jit(solution)/shard_map/reshape | solution.py:103
  222.6 4.8 %reshape.223 = f32[10,16,2,1152]{3,2,1,0:T(2,128)} reshape(f32[10,16,2,16,72]{4,3,2,1,0:T(8,128)} %copy.62) | data formatting | bytes 2949120 | tf_op jit(solution)/shard_map/reshape | solution.py:103
  (32 shorter events, 0.2 us)
Async XLA Ops:
  0.0 6.4 %copy-start.3 = (f32[16,2,1152]{2,1,0:T(2,128)S(1)}, f32[16,2,1152]{2,1,0:T(2,128)}, u32[]{:S(2)}) copy-start(f32[16,2,1152]{2,1,0:T(2,128)} %param.8) | copy-start | bytes 442372
  0.0 6.5 %copy-start = (f32[9,16,2,1152]{3,2,1,0:T(2,128)S(1)}, f32[9,16,2,1152]{3,2,1,0:T(2,128)}, u32[]{:S(2)}) copy-start(f32[9,16,2,1152]{3,2,1,0:T(2,128)} %param.7) | copy-start | bytes 3981316
  2.1 17.3 %collective-permute-start = (f32[11,2,2,1152]{3,2,1,0:T(2,128)}, f32[11,2,2,1152]{3,2,1,0:T(2,128)S(1)}, u32[]{:S(2)}, u32[]{:S(2)}) collective-permute-start(f32[11,2,2,1152]{3,2,1,0:T(2,128)} %get-tuple-element.23), channel_id=1, source_target_pairs={{16,0},{32,16},{48,32},{64,48},{80,64},{96,80},{112,96},{128,112},... | collective-permute-start | bytes 608264 | tf_op jit(solution)/shard_map/ppermute | solution.py:17
  4.0 15.4 %collective-permute-start.1 = (f32[11,2,2,1152]{3,2,1,0:T(2,128)}, f32[11,2,2,1152]{3,2,1,0:T(2,128)S(1)}, u32[]{:S(2)}, u32[]{:S(2)}) collective-permute-start(f32[11,2,2,1152]{3,2,1,0:T(2,128)} %get-tuple-element.22), channel_id=1, source_target_pairs={{0,16},{16,32},{32,48},{48,64},{64,80},{80,96},{96,112},{112,128},... | collective-permute-start | bytes 608264 | tf_op jit(solution)/shard_map/ppermute | solution.py:14
  8.6 3.0 %copy-start.11 = (f32[16,2,1152]{2,1,0:T(2,128)S(1)}, f32[16,2,1152]{2,1,0:T(2,128)}, u32[]{:S(2)}) copy-start(f32[16,2,1152]{2,1,0:T(2,128)} %param.9) | copy-start | bytes 442372
  15.8 4.6 %copy-start.1 = (f32[9,16,2,1152]{3,2,1,0:T(2,128)}, f32[9,16,2,1152]{3,2,1,0:T(2,128)S(1)}, u32[]{:S(2)}) copy-start(f32[9,16,2,1152]{3,2,1,0:T(2,128)S(1)} %fusion.22) | copy-start | bytes 3981316
  15.8 3.6 %copy-start.5 = (f32[16,2,1152]{2,1,0:T(2,128)S(1)}, f32[16,2,1152]{2,1,0:T(2,128)}, u32[]{:S(2)}) copy-start(f32[16,2,1152]{2,1,0:T(2,128)} %param.10) | copy-start | bytes 442372
  19.4 3.0 %copy-start.12 = (f32[16,2,1151]{2,1,0:T(2,128)S(1)}, f32[16,2,1151]{2,1,0:T(2,128)}, u32[]{:S(2)}) copy-start(f32[16,2,1151]{2,1,0:T(2,128)} %slice.196) | copy-start | bytes 441988
  19.5 2.9 %copy-start.6 = (f32[11,2,2,1152]{3,2,1,0:T(2,128)}, f32[11,2,2,1152]{3,2,1,0:T(2,128)S(1)}, u32[]{:S(2)}) copy-start(f32[11,2,2,1152]{3,2,1,0:T(2,128)S(1)} %collective-permute-done) | copy-start | bytes 608260
  19.5 2.9 %copy-start.7 = (f32[11,2,2,1152]{3,2,1,0:T(2,128)}, f32[11,2,2,1152]{3,2,1,0:T(2,128)S(1)}, u32[]{:S(2)}) copy-start(f32[11,2,2,1152]{3,2,1,0:T(2,128)S(1)} %collective-permute-done.1) | copy-start | bytes 608260
  26.1 1.0 copy-start.8
  26.1 1.0 copy-start.9
  26.2 1.0 copy-start.10
  26.2 1.1 copy-start.13
  27.3 1.8 copy-start.2
  27.3 1.8 slice-start
  27.3 1.8 copy-start.4
  43.2 8.8 %copy-start.14 = (s32[31,16,72]{2,1,0:T(8,128)S(1)}, s32[31,16,72]{2,1,0:T(8,128)}, u32[]{:S(2)}) copy-start(s32[31,16,72]{2,1,0:T(8,128)} %param.11) | copy-start | bytes 428548
  43.2 9.1 %copy-start.15 = (f32[31,16,72]{2,1,0:T(8,128)S(1)}, f32[31,16,72]{2,1,0:T(8,128)}, u32[]{:S(2)}) copy-start(f32[31,16,72]{2,1,0:T(8,128)} %param.13) | copy-start | bytes 428548
  43.2 9.1 %copy-start.16 = (s32[31,16,72]{2,1,0:T(8,128)S(1)}, s32[31,16,72]{2,1,0:T(8,128)}, u32[]{:S(2)}) copy-start(s32[31,16,72]{2,1,0:T(8,128)} %param.12) | copy-start | bytes 428548
  43.2 50.9 %all-to-all-start = ((f32[10,16,2,1152]{3,2,0,1:T(2,128)}), f32[10,16,2,1152]{3,2,0,1:T(2,128)S(1)}, u32[]{:S(2)}, u32[]{:S(2)}) async-start(f32[10,16,2,1152]{3,2,0,1:T(2,128)} %copy.47), calls=%async_computation | async-start | bytes 2949120 | tf_op jit(solution)/shard_map/all_to_all | solution.py:99
where the time goes:
time: 231 us; the launch traced here: 228 us
  local copies, waits for them, and re-layouts  72.3 us (31%)
  other arithmetic  43.8 us (19%)
  waiting for transfers between devices  41.6 us (18%)
  blocking collectives  39.9 us (17%)
  matrix products  16.2 us (7%)
  starting transfers between devices  13.1 us (6%)
    all_to_all x1, waiting for transfers between devices, shards(): lax.all_to_all(ordered, 'lev', split_axis=1, concat_axis=2, tiled=True)  41.6 us
    all_to_all x1, blocking collectives, shards(): lax.all_to_all(layers, 'lev', split_axis=2, concat_axis=1, tiled=True)  39.9 us
    another operation x1, other arithmetic, remap_columns(): below = jnp.cumsum(m, axis=1) - m  17.3 us
    transpose x1, local copies, waits for them, and re-layouts, remap_columns(): jnp.einsum('flc,nlc->fnc', stacked, selector, precision=lax.Precision.HIG...  16.4 us
    reshape x1, local copies, waits for them, and re-layouts, remap_columns(): jnp.stack([below, left, slope, curve], 1)  16.3 us
    dot_general x1, matrix products, remap_columns(): jnp.einsum('flc,nlc->fnc', stacked, selector, precision=lax.Precision.HIG...  16.2 us
    all_to_all x1, starting transfers between devices, shards(): lax.all_to_all(ordered, 'lev', split_axis=1, concat_axis=2, tiled=True)  8.77 us
    reshape x2, local copies, waits for them, and re-layouts, shards(): return result.reshape(width, latd, levd, nlon)  7.91 us
  transfers between devices with their start and end apart: 3, of which 1 were waited for; matrix products, arithmetic and copies ran while one was open for 6% of the time, Pallas kernels for 0%

commit v1 on v0

v1 whole, which is shorter than its diff:
```python
import functools

import jax
import jax.numpy as jnp
from jax import lax
from jax.experimental import pallas as pl
from jax.experimental.pallas import tpu as pltpu
from jax.sharding import PartitionSpec as P

F32 = jnp.float32
NTR = 9
ROWS = 16
LEVS = 2
LANES = 128
TILES = 9
CHUNK = 72
GROUPS = 16
HELD = ROWS + 4
STEP = TILES * LEVS
FIELD = HELD * STEP
VMEM_LIMIT = 40 * 1024 * 1024

PARTS = ((8, 1, True), (0, 4, False), (4, 4, False))


def fields_of(part):
    return part[1] + int(part[2])


def depth_of(part):
    return fields_of(part) * LEVS * 8 + 8


def lane_index():
    return lax.broadcasted_iota(jnp.int32, (8, LANES), 1)


def row_index():
    return lax.broadcasted_iota(jnp.int32, (8, LANES), 0)


def turn(x, shift, axis):
    shift = shift % x.shape[axis]
    return x if shift == 0 else pltpu.roll(x, shift, axis)


def west_of(tiles, lane):
    rolled = [turn(x, 1, 1) for x in tiles]
    return [jnp.where(lane == 0, rolled[c - 1], rolled[c]) for c in range(TILES)]


def east_of(tiles, lane):
    rolled = [turn(x, -1, 1) for x in tiles]
    return [jnp.where(lane == LANES - 1, rolled[(c + 1) % TILES], rolled[c]) for c in range(TILES)]


def span_of(group):
    return divmod(CHUNK * group, LANES)


def halo_kernel(tracers, thickness, courant_y, low, high, sem):
    copies = []
    for edge, (out, first) in enumerate(((low, 0), (high, ROWS - 2))):
        rows = pl.ds(first, 2)
        copies.append(pltpu.make_async_copy(tracers.at[:, rows], out.at[pl.ds(0, NTR)], sem.at[edge, 0]))
        copies.append(pltpu.make_async_copy(thickness.at[rows], out.at[NTR], sem.at[edge, 1]))
        copies.append(pltpu.make_async_copy(courant_y.at[rows], out.at[NTR + 1], sem.at[edge, 2]))
    for copy in copies:
        copy.start()
    for copy in copies:
        copy.wait()


def transport_kernel(part, lat, tracers, thickness, courant_x, courant_y, low, high, out, held, mx, ax, my, ay, fy, sem):
    first, count, with_air = part
    depth = depth_of(part)
    rest = depth - 8
    lane, row = lane_index(), row_index()
    view = held.reshape(count + 3, HELD, TILES, LEVS, LANES)
    copies = []
    for c in range(TILES):
        cut = pl.ds(LANES * c, LANES)
        own = pl.ds(2, ROWS)
        for source, target in (
            (thickness.at[:, :, cut], view.at[0, own, c]),
            (courant_y.at[:, :, cut], view.at[1, own, c]),
            (courant_x.at[:, :, cut], view.at[2, own, c]),
            (tracers.at[pl.ds(first, count), :, :, cut], view.at[pl.ds(3, count), own, c]),
            (low.at[NTR, :, :, cut], view.at[0, pl.ds(0, 2), c]),
            (low.at[pl.ds(first, count), :, :, cut], view.at[pl.ds(3, count), pl.ds(0, 2), c]),
            (high.at[pl.ds(NTR, 2), :, :, cut], view.at[pl.ds(0, 2), pl.ds(ROWS + 2, 2), c]),
            (high.at[pl.ds(first, count), :, :, cut], view.at[pl.ds(3, count), pl.ds(ROWS + 2, 2), c]),
        ):
            copies.append(pltpu.make_async_copy(source, target, sem.at[len(copies)]))
    for copy in copies:
        copy.start()
    for g in range(GROUPS):
        out[g, pl.ds(rest, 8), :] = jnp.zeros((8, LANES), F32)
    for copy in copies:
        copy.wait()

    def rows_of(array, j, c, l):
        return held[pl.ds(array * FIELD + (j + 2) * STEP + c * LEVS + l, 8, stride=STEP), :]

    def whole_row(array, j):
        return held[pl.ds(array * FIELD + (j + 2) * STEP, STEP), :]

    def place(l, c, h):
        return pl.ds((c * LEVS + l) * ROWS + 8 * h, 8)

    def factors(courant, before, after):
        mass = jnp.where(courant > 0, courant * before, courant * after)
        return mass, mass * jnp.where(courant > 0, 0.25 - 0.25 * courant, -0.25 - 0.25 * courant)

    keep = (row > 0) | (lat[0] > 0)
    for l in range(LEVS):
        for h in range(2):
            thick = [rows_of(0, 8 * h, c, l) for c in range(TILES)]
            west = west_of(thick, lane)
            for c in range(TILES):
                mass, tilt = factors(rows_of(2, 8 * h, c, l), west[c], thick[c])
                mx[place(l, c, h), :] = mass
                ax[place(l, c, h), :] = tilt
                courant = rows_of(1, 8 * h, c, l)
                if h == 0:
                    courant = jnp.where(keep, courant, 0.0)
                mass, tilt = factors(courant, rows_of(0, 8 * h - 1, c, l), thick[c])
                my[place(l, c, h), :] = mass
                ay[place(l, c, h), :] = tilt
    last_mass, last_tilt = factors(whole_row(1, ROWS), whole_row(0, ROWS - 1), whole_row(0, ROWS))

    def send(field, l, tiles):
        slot = l * 4 + field
        for g in range(GROUPS):
            t, o = span_of(g)
            a = turn(tiles[0][t], -o, 1)
            b = turn(tiles[1][t], CHUNK - o, 1)
            if o + CHUNK > LANES:
                a = jnp.where(lane < LANES - o, a, turn(tiles[0][t + 1], -o, 1))
                lon = jnp.where(lane >= CHUNK, lane - CHUNK, lane + (LANES - CHUNK))
                b = jnp.where(lon < LANES - o, b, turn(tiles[1][t + 1], CHUNK - o, 1))
            out[g, pl.ds(pl.multiple_of((field * LEVS + l) * 8, 8), 8), :] = jnp.where(lane < CHUNK, a, b)
            moved = pltpu.roll(b, slot * 16, 1)
            out[g, pl.ds(rest, 8), :] = jnp.where((lane >> 4) == slot, moved, out[g, pl.ds(rest, 8), :])

    def tracer(field, _):
        array = 3 + field
        edge_q = [whole_row(array, ROWS + k) for k in (-2, -1, 0, 1)]
        up = last_mass > 0
        value = jnp.where(up, edge_q[1], edge_q[2])
        rise = jnp.where(up, edge_q[2] - edge_q[0], edge_q[3] - edge_q[1])
        fy[pl.ds(ROWS, STEP, stride=24), :] = last_mass * value + last_tilt * rise
        for l in range(LEVS):
            tiles = []
            for h in range(2):
                q = [rows_of(array, 8 * h, c, l) for c in range(TILES)]
                qw = west_of(q, lane)
                qe = east_of(q, lane)
                d = [qe[c] - qw[c] for c in range(TILES)]
                dw = west_of(d, lane)
                flux = []
                for c in range(TILES):
                    mass = mx[place(l, c, h), :]
                    up = mass > 0
                    flux.append(mass * jnp.where(up, qw[c], q[c]) + ax[place(l, c, h), :] * jnp.where(up, dw[c], d[c]))
                flux_e = east_of(flux, lane)
                now = []
                for c in range(TILES):
                    mass = my[place(l, c, h), :]
                    up = mass > 0
                    q2, q1, q3 = (rows_of(array, 8 * h + k, c, l) for k in (-2, -1, 1))
                    value = jnp.where(up, q1, q[c])
                    rise = jnp.where(up, q[c] - q2, q3 - q1)
                    flux_y = mass * value + ay[place(l, c, h), :] * rise
                    fy[pl.ds((c * LEVS + l) * 24 + 8 * h, 8), :] = flux_y
                    thick = rows_of(0, 8 * h, c, l)
                    now.append(thick * q[c] + (flux[c] - flux_e[c]) + flux_y)
                tiles.append(now)
            for h in range(2):
                for c in range(TILES):
                    tiles[h][c] = tiles[h][c] - fy[pl.ds((c * LEVS + l) * 24 + 8 * h + 1, 8), :]
            send(field, l, tiles)
        return 0

    if count == 1:
        tracer(0, 0)
    else:
        lax.fori_loop(0, count, tracer, 0)
    if with_air:
        fy[pl.ds(ROWS, STEP, stride=24), :] = last_mass
        for l in range(LEVS):
            tiles = []
            for c in range(TILES):
                for h in range(2):
                    fy[pl.ds((c * LEVS + l) * 24 + 8 * h, 8), :] = my[place(l, c, h), :]
            for h in range(2):
                flux = [mx[place(l, c, h), :] for c in range(TILES)]
                flux_e = east_of(flux, lane)
                tiles.append(
                    [
                        rows_of(0, 8 * h, c, l)
                        + (flux[c] - flux_e[c])
                        + (my[place(l, c, h), :] - fy[pl.ds((c * LEVS + l) * 24 + 8 * h + 1, 8), :])
                        for c in range(TILES)
                    ]
                )
            send(count, l, tiles)


def target_kernel(index, offset, phase, level, frac):
    lane = lane_index()

    def spread(x0, x1, zero):
        moved = pltpu.roll(x1, CHUNK, 1)
        main = jnp.where(lane < CHUNK, x0, moved)
        tail = jnp.where(lane < 16, moved, zero)
        tail = tail + pltpu.roll(tail, 16, 1)
        tail = tail + pltpu.roll(tail, 32, 1)
        other = pltpu.roll(pltpu.roll(tail, 64, 1), 4, 0)
        return main, jnp.where(lane < 64, tail, other)

    level[pl.ds(0, 16), :] = jnp.zeros((16, LANES), jnp.int32)
    frac[pl.ds(0, 16), :] = jnp.zeros((16, LANES), F32)
    blank = jnp.zeros((8, LANES - CHUNK), F32)

    def wide(x):
        return jnp.concatenate([x, blank.astype(x.dtype)], 1)

    def one(n, _):
        halves = [wide(index[n, pl.ds(8 * h, 8), :]) for h in range(2)]
        parts = [
            wide((offset[n, pl.ds(8 * h, 8), :].astype(F32) + phase[n, pl.ds(8 * h, 8), :]) * (1.0 / 32.0))
            for h in range(2)
        ]
        for out, (x0, x1), zero in ((level, halves, 0), (frac, parts, 0.0)):
            main, tail = spread(x0, x1, zero)
            out[pl.ds(pl.multiple_of((n + 1) * 16, 16), 8), :] = main
            out[pl.ds(pl.multiple_of((n + 1) * 16 + 8, 8), 8), :] = tail
        return 0

    lax.fori_loop(0, 2 * GROUPS - 1, one, 0)


def pick(x, where):
    return jnp.take_along_axis(x, where, axis=0, mode="promise_in_bounds")


def remap_kernel(part, data, level, frac, out):
    fields, depth = fields_of(part), depth_of(part)
    rest = depth - 8
    lane, row = lane_index(), row_index()

    def targets(tile):
        found = []
        for parity in range(2):
            for half in range(2):
                start = (parity + 16 * half) * 16 + tile
                s = level[pl.ds(start, 8, stride=32), :]
                f = frac[pl.ds(start, 8, stride=32), :]
                square = f * f * 0.5
                cubic = 3.0 * square - f * f * f
                found.append(((s >> 1) & 7, s >= 16, (s & 1) == 1, f, square, cubic))
        return found

    def columns(even, odd, found):
        back = [turn(x, 1, 0) for x in odd]
        before = [jnp.where(row == 0, even[0], back[0]), jnp.where(row == 0, back[0], back[1])]
        left = [0.5 * (before[i] + even[i]) for i in range(2)]
        ahead = [turn(x, -1, 0) for x in left]
        right = [jnp.where(row == 7, ahead[1], ahead[0]), jnp.where(row == 7, odd[1], ahead[1])]
        pair = [even[i] + odd[i] for i in range(2)]
        run = list(pair)
        for shift in (1, 2, 4):
            run = [x + jnp.where(row >= shift, turn(x, shift, 0), 0.0) for x in run]
        half_sum = jnp.broadcast_to(run[0][7:8], (8, LANES))
        total = half_sum + run[1][7:8]
        below = [run[0] - pair[0], (run[1] - pair[1]) + half_sum]
        edges = []
        for where, high, is_odd, f, square, cubic in found:
            le, ri, ev, od, be = (
                jnp.where(high, pick(x[1], where), pick(x[0], where)) for x in (left, right, even, odd, below)
            )
            middle = 0.5 * (ev + od)
            lo = jnp.where(is_odd, middle, le)
            hi = jnp.where(is_odd, ri, middle)
            m = jnp.where(is_odd, od, ev)
            base = be + jnp.where(is_odd, ev, 0.0)
            edges.append(base + lo * f + (hi - lo) * square + ((m + m) - (lo + hi)) * cubic)
        ev0, ev1, od0, od1 = edges
        next0, next1 = turn(ev0, -1, 0), turn(ev1, -1, 0)
        new_even = [od0 - ev0, od1 - ev1]
        new_odd = [jnp.where(row == 7, next1, next0) - od0, jnp.where(row == 7, total, next1) - od1]
        return new_even, new_odd

    def span(start, half):
        return pl.ds(start + half * 8 * depth, 8, stride=depth)

    def main(tile, _):
        found = targets(tile)
        for field in range(fields):
            at = [(field * LEVS + l) * 8 + tile for l in range(LEVS)]
            even, odd = ([data[span(at[l], half), :] for half in range(2)] for l in range(LEVS))
            new = columns(even, odd, found)
            for l in range(LEVS):
                for half in range(2):
                    out[span(at[l], half), :] = new[l][half]
        return 0

    lax.fori_loop(0, 8, main, 0)

    def tail(tile, _):
        found = targets(8 + tile)
        at = [rest + tile, rest + tile + 4]
        a, b = ([data[span(at[i], half), :] for half in range(2)] for i in range(2))
        even = [jnp.where(lane < 64, a[half], turn(b[half], 64, 1)) for half in range(2)]
        odd = [jnp.where(lane < 64, turn(a[half], 64, 1), b[half]) for half in range(2)]
        even, odd = columns(even, odd, found)
        for half in range(2):
            out[span(at[0], half), :] = jnp.where(lane < 64, even[half], turn(odd[half], 64, 1))
            out[span(at[1], half), :] = jnp.where(lane < 64, turn(even[half], 64, 1), odd[half])
        return 0

    lax.fori_loop(0, 4, tail, 0)


def collect_kernel(part, data, *refs):
    out, flat, sem = refs[-3:]
    fields, depth = fields_of(part), depth_of(part)
    rest = depth - 8
    lane = lane_index()

    def gather(field, _):
        for l in range(LEVS):
            slot = l * 4 + field
            pieces = []
            for g in range(GROUPS):
                _, o = span_of(g)
                main = data[g, pl.ds(pl.multiple_of((field * LEVS + l) * 8, 8), 8), :]
                tail = pltpu.roll(data[g, pl.ds(rest, 8), :], LANES - slot * 16, 1)
                mixed = jnp.where(lane < 16, tail, main)
                pieces.append((turn(main, o, 1), turn(mixed, o - CHUNK, 1)))
            for h in range(2):
                for c in range(TILES):
                    value = None
                    for g in range(GROUPS):
                        start = CHUNK * g - LANES * c
                        if start >= LANES or start + CHUNK <= 0:
                            continue
                        piece = pieces[g][h]
                        value = piece if value is None else jnp.where(lane >= start, piece, value)
                    at = field * (ROWS * STEP) + 8 * h * STEP + c * LEVS + l
                    flat[pl.ds(at, 8, stride=STEP), :] = value
        return 0

    lax.fori_loop(0, fields, gather, 0)
    view = flat.reshape(fields, ROWS, TILES, LEVS, LANES)
    first, count, with_air = part
    copies = []
    for c in range(TILES):
        cut = pl.ds(LANES * c, LANES)
        target = out.at[pl.ds(first, fields), :, :, cut]
        copies.append(pltpu.make_async_copy(view.at[:, :, c], target, sem.at[c]))
    for copy in copies:
        copy.start()
    for copy in copies:
        copy.wait()


ANYWHERE = pl.BlockSpec(memory_space=pl.ANY)
IN_VMEM = pl.BlockSpec(memory_space=pltpu.VMEM)
PARAMS = pltpu.CompilerParams(vmem_limit_bytes=VMEM_LIMIT)


def transport(part, lat, tracers, thickness, courant_x, courant_y, low, high):
    shape = (GROUPS, depth_of(part), LANES)
    factor = pltpu.VMEM((LEVS * TILES * ROWS, LANES), F32)
    return pl.pallas_call(
        functools.partial(transport_kernel, part),
        out_shape=jax.ShapeDtypeStruct(shape, F32),
        in_specs=[pl.BlockSpec(memory_space=pltpu.SMEM)] + [ANYWHERE] * 6,
        out_specs=IN_VMEM,
        scratch_shapes=[
            pltpu.VMEM(((part[1] + 3) * FIELD, LANES), F32),
            factor,
            factor,
            factor,
            factor,
            pltpu.VMEM((STEP * 24, LANES), F32),
            pltpu.SemaphoreType.DMA((8 * TILES,)),
        ],
        compiler_params=PARAMS,
    )(lat, tracers, thickness, courant_x, courant_y, low, high)


def remap(part, data, level, frac):
    depth = depth_of(part)
    return pl.pallas_call(
        functools.partial(remap_kernel, part),
        out_shape=jax.ShapeDtypeStruct((GROUPS * depth, LANES), F32),
        in_specs=[IN_VMEM] * 3,
        out_specs=IN_VMEM,
        compiler_params=PARAMS,
    )(data.reshape(GROUPS * depth, LANES), level, frac).reshape(GROUPS, depth, LANES)


def collect(part, data, result):
    shape = (NTR + 1, ROWS, LEVS, LANES * TILES)
    given = (data,) if result is None else (data, result)
    return pl.pallas_call(
        functools.partial(collect_kernel, part),
        out_shape=jax.ShapeDtypeStruct(shape, F32),
        in_specs=[IN_VMEM, ANYWHERE][: len(given)],
        out_specs=ANYWHERE,
        scratch_shapes=[
            pltpu.VMEM((fields_of(part) * ROWS * STEP, LANES), F32),
            pltpu.SemaphoreType.DMA((TILES,)),
        ],
        input_output_aliases={} if result is None else {1: 0},
        compiler_params=PARAMS,
    )(*given)


def exchange(data):
    return lax.all_to_all(data, "lev", split_axis=0, concat_axis=0, tiled=True)


def shards(tracers, thickness, courant_x, courant_y, level_index, level_offset, level_phase):
    rim = jax.ShapeDtypeStruct((NTR + 2, 2, LEVS, LANES * TILES), F32)
    south, north = pl.pallas_call(
        halo_kernel,
        out_shape=(rim, rim),
        in_specs=[ANYWHERE] * 3,
        out_specs=(ANYWHERE, ANYWHERE),
        scratch_shapes=[pltpu.SemaphoreType.DMA((2, 3))],
    )(tracers, thickness, courant_y)
    count = lax.axis_size("lat")
    low = lax.ppermute(north, "lat", [(i, i + 1) for i in range(count - 1)])
    high = lax.ppermute(south, "lat", [(i + 1, i) for i in range(count - 1)])
    table = (2 * GROUPS * 16, LANES)
    level, frac = pl.pallas_call(
        target_kernel,
        out_shape=(jax.ShapeDtypeStruct(table, jnp.int32), jax.ShapeDtypeStruct(table, F32)),
        in_specs=[IN_VMEM] * 3,
        out_specs=(IN_VMEM, IN_VMEM),
        compiler_params=PARAMS,
    )(level_index, level_offset, level_phase)
    lat = lax.axis_index("lat").astype(jnp.int32).reshape(1)
    result = None
    sent = [transport(part, lat, tracers, thickness, courant_x, courant_y, low, high) for part in PARTS]
    taken = [exchange(x) for x in sent]
    mapped = [remap(part, x, level, frac) for part, x in zip(PARTS, taken)]
    back = [exchange(x) for x in mapped]
    for part, x in zip(PARTS, back):
        result = collect(part, x, result)
    return result


def solution(mesh):
    in_specs = (
        P(None, "lat", "lev", None),
        P("lat", "lev", None),
        P("lat", "lev", None),
        P("lat", "lev", None),
        P(None, "lat", "lev"),
        P(None, "lat", "lev"),
        P(None, "lat", "lev"),
    )
    out_specs = P(None, "lat", "lev", None)
    return jax.shard_map(shards, mesh=mesh, in_specs=in_specs, out_specs=out_specs, check_vma=False)
```

time: 231 us -> 156 us (0.68)
  the two profiles are of different devices: /device:TPU:2 before, /device:TPU:7 now
where the time goes in v1:
time: 156 us; the launch traced here: 155 us
  waiting for transfers between devices  65.6 us (42%)
  Pallas kernels  47.3 us (30%)
  starting transfers between devices  39.1 us (25%)
  local copies, waits for them, and re-layouts  2.82 us (2%)
    all_to_all x6, waiting for transfers between devices, exchange(): return lax.all_to_all(data, 'lev', split_axis=0, concat_axis=0, tiled=True)  54.2 us
    all_to_all x6, starting transfers between devices, exchange(): return lax.all_to_all(data, 'lev', split_axis=0, concat_axis=0, tiled=True)  27.9 us
    pallas_call x3, Pallas kernels, transport(): pl.pallas_call(functools.partial(transport_kernel, part), out_shape=jax.S...  13.7 us
    pallas_call x1, Pallas kernels, shards(): pl.pallas_call(halo_kernel, out_shape=(rim, rim), in_specs=[ANYWHERE] * 3...  13.4 us
    ppermute x1, waiting for transfers between devices, shards(): high = lax.ppermute(south, 'lat', [(i + 1, i) for i in range(count - 1)])  10.4 us
    ppermute x1, starting transfers between devices, shards(): low = lax.ppermute(north, 'lat', [(i, i + 1) for i in range(count - 1)])  9.29 us
    pallas_call x1, Pallas kernels, shards(): pl.pallas_call(target_kernel, out_shape=(jax.ShapeDtypeStruct(table, jnp....  8.68 us
    pallas_call x3, Pallas kernels, remap(): pl.pallas_call(functools.partial(remap_kernel, part), out_shape=jax.Shape...  7.02 us
  transfers between devices with their start and end apart: 8, of which 8 were waited for; matrix products, arithmetic and copies ran while one was open for 0% of the time, Pallas kernels for 18%

profile of v1, /device:TPU:7, one launch (start us, length us, event | category | flops | bytes accessed | tf_op | source)
XLA Modules:
  0.0 155.0 jit_solution(7089289086304031926)
XLA Ops:
  0.0 0.0 copy-start.2
  0.0 0.0 copy-start.1
  0.0 0.0 copy-start
  0.0 13.4 %shard_map.73 = (f32[11,2,2,1152]{3,2,1,0:T(2,128)}, f32[11,2,2,1152]{3,2,1,0:T(2,128)}) custom-call(f32[9,16,2,1152]{3,2,1,0:T(2,128)} %tracers.7, f32[16,2,1152]{2,1,0:T(2,128)} %thickness.7, f32[16,2,1152]{2,1,0:T(2,128)} %courant_y.7), custom_call_target="tpu_custom_call" | custom-call | tf_op jit(solution)/shard_map/pallas_call | solution.py:429
  13.5 9.3 %collective-permute-start = (f32[11,2,2,1152]{3,2,1,0:T(2,128)}, f32[11,2,2,1152]{3,2,1,0:T(2,128)S(1)}, u32[]{:S(2)}, u32[]{:S(2)}) collective-permute-start(f32[11,2,2,1152]{3,2,1,0:T(2,128)} %get-tuple-element.9), channel_id=1, source_target_pairs={{0,16},{16,32},{32,48},{48,64},{64,80},{80,96},{96,112},{112,128},... | collective-permute-start | bytes 608264 | tf_op jit(solution)/shard_map/ppermute | solution.py:437
  22.8 1.9 %collective-permute-start.1 = (f32[11,2,2,1152]{3,2,1,0:T(2,128)}, f32[11,2,2,1152]{3,2,1,0:T(2,128)S(1)}, u32[]{:S(2)}, u32[]{:S(2)}) collective-permute-start(f32[11,2,2,1152]{3,2,1,0:T(2,128)} %get-tuple-element.10), channel_id=1, source_target_pairs={{16,0},{32,16},{48,32},{64,48},{80,64},{96,80},{112,96},{128,112},... | collective-permute-start | bytes 608264 | tf_op jit(solution)/shard_map/ppermute | solution.py:438
  24.7 1.0 collective-permute-done.low
  25.7 10.4 %collective-permute-done.1.high = f32[11,2,2,1152]{3,2,1,0:T(2,128)S(1)} collective-permute-done((f32[11,2,2,1152]{3,2,1,0:T(2,128)}, f32[11,2,2,1152]{3,2,1,0:T(2,128)S(1)}, u32[]{:S(2)}, u32[]{:S(2)}) %collective-permute-start.1) | collective-permute-done | bytes 202784 | tf_op jit(solution)/shard_map/ppermute | solution.py:438
  36.1 0.0 copy-done.2
  36.1 0.0 copy-done.1
  36.1 0.0 copy-done
  36.2 0.0 copy-start.3
  36.2 0.9 copy-done.3
  37.1 0.0 copy-start.4
  37.1 4.1 %shard_map.79 = f32[16,40,128]{2,1,0:T(8,128)} custom-call(s32[1]{0:T(128)} %bitcast.lat, f32[9,16,2,1152]{3,2,1,0:T(2,128)S(1)} %copy-done, f32[16,2,1152]{2,1,0:T(2,128)S(1)} %copy-done.1, f32[16,2,1152]{2,1,0:T(2,128)S(1)} %copy-done.3, f32[16,2,1152]{2,1,0:T(2,128)S(1)} %copy-done.2, f32[11,2,2,1152]{3,2,1,0:T(2,128)S(1)} %collective-permute-done.low, ...), custom_call_target="tpu_custom_call" | custom-call | tf_op jit(solution)/shard_map/pallas_call | solution.py:377
  41.2 7.5 %all-to-all-start.4 = ((f32[16,40,128]{2,1,0:T(8,128)}), f32[16,40,128]{2,1,0:T(8,128)S(1)}, u32[]{:S(2)}, u32[]{:S(2)}) async-start(f32[16,40,128]{2,1,0:T(8,128)} %shard_map.79), calls=%async_computation.4 | async-start | bytes 655360 | tf_op jit(solution)/shard_map/all_to_all | solution.py:424
  48.6 0.0 copy-done.4
  48.7 4.8 %shard_map.77 = f32[16,72,128]{2,1,0:T(8,128)} custom-call(s32[1]{0:T(128)} %bitcast.lat, f32[9,16,2,1152]{3,2,1,0:T(2,128)S(1)} %copy-done, f32[16,2,1152]{2,1,0:T(2,128)S(1)} %copy-done.1, f32[16,2,1152]{2,1,0:T(2,128)S(1)} %copy-done.4, f32[16,2,1152]{2,1,0:T(2,128)S(1)} %copy-done.2, f32[11,2,2,1152]{3,2,1,0:T(2,128)S(1)} %collective-permute-done.low, ...), custom_call_target="tpu_custom_call" | custom-call | tf_op jit(solution)/shard_map/pallas_call | solution.py:377
  53.5 6.4 %all-to-all-done.4 = f32[16,40,128]{2,1,0:T(8,128)S(1)} async-done(((f32[16,40,128]{2,1,0:T(8,128)}), f32[16,40,128]{2,1,0:T(8,128)S(1)}, u32[]{:S(2)}, u32[]{:S(2)}) %all-to-all-start.4) | async-done | bytes 327712 | tf_op jit(solution)/shard_map/all_to_all | solution.py:424
  59.9 5.0 %all-to-all-start.2 = ((f32[16,72,128]{2,1,0:T(8,128)}), f32[16,72,128]{2,1,0:T(8,128)S(1)}, u32[]{:S(2)}, u32[]{:S(2)}) async-start(f32[16,72,128]{2,1,0:T(8,128)} %shard_map.77), calls=%async_computation.2 | async-start | bytes 1179648 | tf_op jit(solution)/shard_map/all_to_all | solution.py:424
  64.9 0.0 copy-start.5
  64.9 4.8 %shard_map.74 = f32[16,72,128]{2,1,0:T(8,128)} custom-call(s32[1]{0:T(128)} %bitcast.lat, f32[9,16,2,1152]{3,2,1,0:T(2,128)S(1)} %copy-done, f32[16,2,1152]{2,1,0:T(2,128)S(1)} %copy-done.1, f32[16,2,1152]{2,1,0:T(2,128)S(1)} %copy-done.4, f32[16,2,1152]{2,1,0:T(2,128)S(1)} %copy-done.2, f32[11,2,2,1152]{3,2,1,0:T(2,128)S(1)} %collective-permute-done.low, ...), custom_call_target="tpu_custom_call" | custom-call | tf_op jit(solution)/shard_map/pallas_call | solution.py:377
  69.7 11.6 %all-to-all-done.2 = f32[16,72,128]{2,1,0:T(8,128)S(1)} async-done(((f32[16,72,128]{2,1,0:T(8,128)}), f32[16,72,128]{2,1,0:T(8,128)S(1)}, u32[]{:S(2)}, u32[]{:S(2)}) %all-to-all-start.2) | async-done | bytes 589856 | tf_op jit(solution)/shard_map/all_to_all | solution.py:424
  81.2 3.6 %all-to-all-start = ((f32[16,72,128]{2,1,0:T(8,128)}), f32[16,72,128]{2,1,0:T(8,128)S(1)}, u32[]{:S(2)}, u32[]{:S(2)}) async-start(f32[16,72,128]{2,1,0:T(8,128)} %shard_map.74), calls=%async_computation | async-start | bytes 1179648 | tf_op jit(solution)/shard_map/all_to_all | solution.py:424
  84.8 0.0 copy-done.5
  84.8 0.0 copy-start.6
  84.9 0.9 copy-done.6
  85.8 0.0 copy-start.7
  85.8 0.9 copy-done.7
  86.7 8.7 %shard_map.75 = (s32[512,128]{1,0:T(8,128)S(1)}, f32[512,128]{1,0:T(8,128)S(1)}) custom-call(s32[31,16,72]{2,1,0:T(8,128)S(1)} %copy-done.5, s32[31,16,72]{2,1,0:T(8,128)S(1)} %copy-done.6, f32[31,16,72]{2,1,0:T(8,128)S(1)} %copy-done.7), custom_call_target="tpu_custom_call" | custom-call | tf_op jit(solution)/shard_map/pallas_call | solution.py:440
  95.4 2.0 %shard_map.80 = f32[640,128]{1,0:T(8,128)} custom-call(f32[640,128]{1,0:T(8,128)S(1)} %bitcast.9, s32[512,128]{1,0:T(8,128)S(1)} %get-tuple-element.11.level, f32[512,128]{1,0:T(8,128)S(1)} %get-tuple-element.12.frac), custom_call_target="tpu_custom_call" | custom-call | tf_op jit(solution)/shard_map/pallas_call | solution.py:397
  97.4 2.3 %all-to-all-done = f32[16,72,128]{2,1,0:T(8,128)S(1)} async-done(((f32[16,72,128]{2,1,0:T(8,128)}), f32[16,72,128]{2,1,0:T(8,128)S(1)}, u32[]{:S(2)}, u32[]{:S(2)}) %all-to-all-start) | async-done | bytes 589856 | tf_op jit(solution)/shard_map/all_to_all | solution.py:424
  99.8 4.6 %all-to-all-start.5 = ((f32[16,40,128]{2,1,0:T(8,128)}), f32[16,40,128]{2,1,0:T(8,128)S(1)}, u32[]{:S(2)}, u32[]{:S(2)}) async-start(f32[16,40,128]{2,1,0:T(8,128)} %bitcast.6), calls=%async_computation.5 | async-start | bytes 655360 | tf_op jit(solution)/shard_map/all_to_all | solution.py:424
  104.3 2.5 %shard_map.78 = f32[1152,128]{1,0:T(8,128)} custom-call(f32[1152,128]{1,0:T(8,128)S(1)} %bitcast.7, s32[512,128]{1,0:T(8,128)S(1)} %get-tuple-element.11.level, f32[512,128]{1,0:T(8,128)S(1)} %get-tuple-element.12.frac), custom_call_target="tpu_custom_call" | custom-call | tf_op jit(solution)/shard_map/pallas_call | solution.py:397
  106.8 10.6 %all-to-all-done.5.data = f32[16,40,128]{2,1,0:T(8,128)S(1)} async-done(((f32[16,40,128]{2,1,0:T(8,128)}), f32[16,40,128]{2,1,0:T(8,128)S(1)}, u32[]{:S(2)}, u32[]{:S(2)}) %all-to-all-start.5) | async-done | bytes 327712 | tf_op jit(solution)/shard_map/all_to_all | solution.py:424
  117.4 3.7 %all-to-all-start.3 = ((f32[16,72,128]{2,1,0:T(8,128)}), f32[16,72,128]{2,1,0:T(8,128)S(1)}, u32[]{:S(2)}, u32[]{:S(2)}) async-start(f32[16,72,128]{2,1,0:T(8,128)} %bitcast.4), calls=%async_computation.3 | async-start | bytes 1179648 | tf_op jit(solution)/shard_map/all_to_all | solution.py:424
  121.2 2.5 %shard_map.76 = f32[1152,128]{1,0:T(8,128)} custom-call(f32[1152,128]{1,0:T(8,128)S(1)} %bitcast.8, s32[512,128]{1,0:T(8,128)S(1)} %get-tuple-element.11.level, f32[512,128]{1,0:T(8,128)S(1)} %get-tuple-element.12.frac), custom_call_target="tpu_custom_call" | custom-call | tf_op jit(solution)/shard_map/pallas_call | solution.py:397
  123.7 14.3 %all-to-all-done.3.data = f32[16,72,128]{2,1,0:T(8,128)S(1)} async-done(((f32[16,72,128]{2,1,0:T(8,128)}), f32[16,72,128]{2,1,0:T(8,128)S(1)}, u32[]{:S(2)}, u32[]{:S(2)}) %all-to-all-start.3) | async-done | bytes 589856 | tf_op jit(solution)/shard_map/all_to_all | solution.py:424
  137.9 3.6 %all-to-all-start.1 = ((f32[16,72,128]{2,1,0:T(8,128)}), f32[16,72,128]{2,1,0:T(8,128)S(1)}, u32[]{:S(2)}, u32[]{:S(2)}) async-start(f32[16,72,128]{2,1,0:T(8,128)} %bitcast.2), calls=%async_computation.1 | async-start | bytes 1179648 | tf_op jit(solution)/shard_map/all_to_all | solution.py:424
  141.5 1.2 shard_map.81.refs_0_
  142.7 1.7 %shard_map.82.refs_0_ = f32[10,16,2,1152]{3,2,1,0:T(2,128)} custom-call(f32[16,72,128]{2,1,0:T(8,128)S(1)} %all-to-all-done.3.data, f32[10,16,2,1152]{3,2,1,0:T(2,128)} %shard_map.81.refs_0_), custom_call_target="tpu_custom_call", output_to_operand_aliasing={{}: (1, {})} | custom-call | tf_op jit(solution)/shard_map/pallas_call | solution.py:409
  144.4 9.0 %all-to-all-done.1.data = f32[16,72,128]{2,1,0:T(8,128)S(1)} async-done(((f32[16,72,128]{2,1,0:T(8,128)}), f32[16,72,128]{2,1,0:T(8,128)S(1)}, u32[]{:S(2)}, u32[]{:S(2)}) %all-to-all-start.1) | async-done | bytes 589856 | tf_op jit(solution)/shard_map/all_to_all | solution.py:424
  153.3 1.7 %shard_map.83 = f32[10,16,2,1152]{3,2,1,0:T(2,128)} custom-call(f32[16,72,128]{2,1,0:T(8,128)S(1)} %all-to-all-done.1.data, f32[10,16,2,1152]{3,2,1,0:T(2,128)} %shard_map.82.refs_0_), custom_call_target="tpu_custom_call", output_to_operand_aliasing={{}: (1, {})} | custom-call | tf_op jit(solution)/shard_map/pallas_call | solution.py:409
Async XLA Ops:
  0.0 36.1 %copy-start.2 = (f32[16,2,1152]{2,1,0:T(2,128)S(1)}, f32[16,2,1152]{2,1,0:T(2,128)}, u32[]{:S(2)}) copy-start(f32[16,2,1152]{2,1,0:T(2,128)} %courant_y.7) | copy-start | bytes 442372
  0.0 36.1 %copy-start.1 = (f32[16,2,1152]{2,1,0:T(2,128)S(1)}, f32[16,2,1152]{2,1,0:T(2,128)}, u32[]{:S(2)}) copy-start(f32[16,2,1152]{2,1,0:T(2,128)} %thickness.7) | copy-start | bytes 442372
  0.0 36.1 %copy-start = (f32[9,16,2,1152]{3,2,1,0:T(2,128)S(1)}, f32[9,16,2,1152]{3,2,1,0:T(2,128)}, u32[]{:S(2)}) copy-start(f32[9,16,2,1152]{3,2,1,0:T(2,128)} %tracers.7) | copy-start | bytes 3981316
  13.5 12.3 %collective-permute-start = (f32[11,2,2,1152]{3,2,1,0:T(2,128)}, f32[11,2,2,1152]{3,2,1,0:T(2,128)S(1)}, u32[]{:S(2)}, u32[]{:S(2)}) collective-permute-start(f32[11,2,2,1152]{3,2,1,0:T(2,128)} %get-tuple-element.9), channel_id=1, source_target_pairs={{0,16},{16,32},{32,48},{48,64},{64,80},{80,96},{96,112},{112,128},... | collective-permute-start | bytes 608264 | tf_op jit(solution)/shard_map/ppermute | solution.py:437
  22.8 13.4 %collective-permute-start.1 = (f32[11,2,2,1152]{3,2,1,0:T(2,128)}, f32[11,2,2,1152]{3,2,1,0:T(2,128)S(1)}, u32[]{:S(2)}, u32[]{:S(2)}) collective-permute-start(f32[11,2,2,1152]{3,2,1,0:T(2,128)} %get-tuple-element.10), channel_id=1, source_target_pairs={{16,0},{32,16},{48,32},{64,48},{80,64},{96,80},{112,96},{128,112},... | collective-permute-start | bytes 608264 | tf_op jit(solution)/shard_map/ppermute | solution.py:438
  36.2 0.9 copy-start.3
  37.1 11.6 %copy-start.4 = (f32[16,2,1152]{2,1,0:T(2,128)S(1)}, f32[16,2,1152]{2,1,0:T(2,128)}, u32[]{:S(2)}) copy-start(f32[16,2,1152]{2,1,0:T(2,128)} %courant_x.5) | copy-start | bytes 442372
  41.2 18.7 %all-to-all-start.4 = ((f32[16,40,128]{2,1,0:T(8,128)}), f32[16,40,128]{2,1,0:T(8,128)S(1)}, u32[]{:S(2)}, u32[]{:S(2)}) async-start(f32[16,40,128]{2,1,0:T(8,128)} %shard_map.79), calls=%async_computation.4 | async-start | bytes 655360 | tf_op jit(solution)/shard_map/all_to_all | solution.py:424
  59.9 21.3 %all-to-all-start.2 = ((f32[16,72,128]{2,1,0:T(8,128)}), f32[16,72,128]{2,1,0:T(8,128)S(1)}, u32[]{:S(2)}, u32[]{:S(2)}) async-start(f32[16,72,128]{2,1,0:T(8,128)} %shard_map.77), calls=%async_computation.2 | async-start | bytes 1179648 | tf_op jit(solution)/shard_map/all_to_all | solution.py:424
  64.9 20.0 %copy-start.5 = (s32[31,16,72]{2,1,0:T(8,128)S(1)}, s32[31,16,72]{2,1,0:T(8,128)}, u32[]{:S(2)}) copy-start(s32[31,16,72]{2,1,0:T(8,128)} %index.1) | copy-start | bytes 428548
  81.2 18.5 %all-to-all-start = ((f32[16,72,128]{2,1,0:T(8,128)}), f32[16,72,128]{2,1,0:T(8,128)S(1)}, u32[]{:S(2)}, u32[]{:S(2)}) async-start(f32[16,72,128]{2,1,0:T(8,128)} %shard_map.74), calls=%async_computation | async-start | bytes 1179648 | tf_op jit(solution)/shard_map/all_to_all | solution.py:424
  84.8 1.0 copy-start.6
  85.8 0.9 copy-start.7
  99.8 17.7 %all-to-all-start.5 = ((f32[16,40,128]{2,1,0:T(8,128)}), f32[16,40,128]{2,1,0:T(8,128)S(1)}, u32[]{:S(2)}, u32[]{:S(2)}) async-start(f32[16,40,128]{2,1,0:T(8,128)} %bitcast.6), calls=%async_computation.5 | async-start | bytes 655360 | tf_op jit(solution)/shard_map/all_to_all | solution.py:424
  117.4 20.5 %all-to-all-start.3 = ((f32[16,72,128]{2,1,0:T(8,128)}), f32[16,72,128]{2,1,0:T(8,128)S(1)}, u32[]{:S(2)}, u32[]{:S(2)}) async-start(f32[16,72,128]{2,1,0:T(8,128)} %bitcast.4), calls=%async_computation.3 | async-start | bytes 1179648 | tf_op jit(solution)/shard_map/all_to_all | solution.py:424
  137.9 15.4 %all-to-all-start.1 = ((f32[16,72,128]{2,1,0:T(8,128)}), f32[16,72,128]{2,1,0:T(8,128)S(1)}, u32[]{:S(2)}, u32[]{:S(2)}) async-start(f32[16,72,128]{2,1,0:T(8,128)} %bitcast.2), calls=%async_computation.1 | async-start | bytes 1179648 | tf_op jit(solution)/shard_map/all_to_all | solution.py:424

commit v2 on v1

v2 whole, which is shorter than its diff:
```python
import functools

import jax
import jax.numpy as jnp
from jax import lax
from jax.experimental import pallas as pl
from jax.experimental.pallas import tpu as pltpu
from jax.sharding import PartitionSpec as P

F32 = jnp.float32
NTR = 9
FIELDS = NTR + 1
PAIRS = FIELDS // 2
ROWS = 16
LEVS = 2
LANES = 128
TILES = 9
LONS = LANES * TILES
CHUNK = 72
GROUPS = 16
STEP = TILES * LEVS
VMEM_LIMIT = 40 * 1024 * 1024

INNER, OUTER = 1, 2

REST = PAIRS * LEVS * 8
BLOCKS = (PAIRS + 3) // 4
DEPTH = REST + BLOCKS * 8

THICK, NORTH, EAST = NTR, NTR + 1, NTR + 2


def slots_of(part):
    return 8 + 4 * part


def lane_index():
    return lax.broadcasted_iota(jnp.int32, (8, LANES), 1)


def row_index():
    return lax.broadcasted_iota(jnp.int32, (8, LANES), 0)


def turn(x, shift, axis):
    shift = shift % x.shape[axis]
    return x if shift == 0 else pltpu.roll(x, shift, axis)


def west_of(tiles, lane):
    rolled = [turn(x, 1, 1) for x in tiles]
    return [jnp.where(lane == 0, rolled[c - 1], rolled[c]) for c in range(TILES)]


def east_of(tiles, lane):
    rolled = [turn(x, -1, 1) for x in tiles]
    return [jnp.where(lane == LANES - 1, rolled[(c + 1) % TILES], rolled[c]) for c in range(TILES)]


def span_of(group):
    return divmod(CHUNK * group, LANES)


def pick(x, where):
    return jnp.take_along_axis(x, where, axis=0, mode="promise_in_bounds")


def halo_kernel(tracers, thickness, courant_y, low, high, sem):
    copies = []
    for edge, (out, first) in enumerate(((low, 0), (high, ROWS - 2))):
        rows = pl.ds(first, 2)
        copies.append(pltpu.make_async_copy(tracers.at[:, rows], out.at[pl.ds(0, NTR)], sem.at[edge, 0]))
        copies.append(pltpu.make_async_copy(thickness.at[rows], out.at[THICK], sem.at[edge, 1]))
        copies.append(pltpu.make_async_copy(courant_y.at[rows], out.at[NORTH], sem.at[edge, 2]))
    for copy in copies:
        copy.start()
    for copy in copies:
        copy.wait()


def transport_kernel(part, *refs):
    if part == OUTER:
        lat, tracers, thickness, courant_x, courant_y, low, high, out, held, mx, ax, my, ay, fy, sem = refs
    else:
        tracers, thickness, courant_x, courant_y, out, held, mx, ax, my, ay, fy, sem = refs
    slots = slots_of(part)
    lane, row = lane_index(), row_index()
    view = held.reshape(NTR + 3, slots // part, part, TILES, LEVS, LANES)
    copies = []

    def bring(source, target):
        copies.append(pltpu.make_async_copy(source, target, sem.at[len(copies)]))

    for c in range(TILES):
        cut = pl.ds(LANES * c, LANES)
        runs = ((2, 12, 0, 0),) if part == INNER else ((0, 6, 2, 0), (10, 6, 0, 1))
        for first, size, at, run in runs:
            own, into = pl.ds(first, size), pl.ds(at, size)
            bring(tracers.at[:, own, :, cut], view.at[pl.ds(0, NTR), into, run, c])
            for array, source in ((THICK, thickness), (NORTH, courant_y), (EAST, courant_x)):
                bring(source.at[own, :, cut], view.at[array, into, run, c])
        if part == OUTER:
            bring(low.at[pl.ds(0, NTR + 1), :, :, cut], view.at[pl.ds(0, NTR + 1), pl.ds(0, 2), 0, c])
            bring(high.at[:, :, :, cut], view.at[pl.ds(0, NTR + 2), pl.ds(6, 2), 1, c])
    for copy in copies:
        copy.start()
    for g in range(GROUPS):
        out[g, pl.ds(REST, 8 * BLOCKS), :] = jnp.zeros((8 * BLOCKS, LANES), F32)
    for copy in copies:
        copy.wait()

    def rows_of(array, shift, c, l):
        start = (array * slots + (2 + shift) * part) * STEP + c * LEVS + l
        return held[pl.ds(start, 8, stride=STEP), :]

    def past(array, shift):
        return held[pl.ds((array * slots + 8 + (2 + shift) * part) * STEP, part * STEP), :]

    def place(l, c):
        return pl.ds((c * LEVS + l) * 8, 8)

    def faces(l, c, shift):
        return pl.ds((c * LEVS + l) * 16 + shift, 8)

    def keep_past(values):
        for run in range(part):
            fy[pl.ds(8 + run, STEP, stride=16), :] = values[run * STEP : (run + 1) * STEP]

    def factors(courant, before, after):
        mass = jnp.where(courant > 0, courant * before, courant * after)
        return mass, mass * jnp.where(courant > 0, 0.25 - 0.25 * courant, -0.25 - 0.25 * courant)

    for l in range(LEVS):
        thick = [rows_of(THICK, 0, c, l) for c in range(TILES)]
        west = west_of(thick, lane)
        for c in range(TILES):
            mx[place(l, c), :], ax[place(l, c), :] = factors(rows_of(EAST, 0, c, l), west[c], thick[c])
            courant = rows_of(NORTH, 0, c, l)
            if part == OUTER:
                courant = jnp.where((row > 0) | (lat[0] > 0), courant, 0.0)
            my[place(l, c), :], ay[place(l, c), :] = factors(courant, rows_of(THICK, -1, c, l), thick[c])
    past_mass, past_tilt = factors(past(NORTH, 0), past(THICK, -1), past(THICK, 0))

    def air():
        keep_past(past_mass)
        for l in range(LEVS):
            for c in range(TILES):
                fy[faces(l, c, 0), :] = my[place(l, c), :]
        tiles = []
        for l in range(LEVS):
            flux = [mx[place(l, c), :] for c in range(TILES)]
            flux_e = east_of(flux, lane)
            tiles.append(
                [
                    rows_of(THICK, 0, c, l) + (flux[c] - flux_e[c]) + (my[place(l, c), :] - fy[faces(l, c, part), :])
                    for c in range(TILES)
                ]
            )
        return tiles

    def tracer(array):
        past_q = [past(array, shift) for shift in (-2, -1, 0, 1)]
        up = past_mass > 0
        value = jnp.where(up, past_q[1], past_q[2])
        rise = jnp.where(up, past_q[2] - past_q[0], past_q[3] - past_q[1])
        keep_past(past_mass * value + past_tilt * rise)
        tiles = []
        for l in range(LEVS):
            q = [rows_of(array, 0, c, l) for c in range(TILES)]
            qw = west_of(q, lane)
            qe = east_of(q, lane)
            d = [qe[c] - qw[c] for c in range(TILES)]
            dw = west_of(d, lane)
            flux = []
            for c in range(TILES):
                mass = mx[place(l, c), :]
                up = mass > 0
                flux.append(mass * jnp.where(up, qw[c], q[c]) + ax[place(l, c), :] * jnp.where(up, dw[c], d[c]))
            flux_e = east_of(flux, lane)
            now = []
            for c in range(TILES):
                mass = my[place(l, c), :]
                up = mass > 0
                q2, q1, q3 = (rows_of(array, shift, c, l) for shift in (-2, -1, 1))
                value = jnp.where(up, q1, q[c])
                rise = jnp.where(up, q[c] - q2, q3 - q1)
                flux_y = mass * value + ay[place(l, c), :] * rise
                fy[faces(l, c, 0), :] = flux_y
                now.append(rows_of(THICK, 0, c, l) * q[c] + (flux[c] - flux_e[c]) + flux_y)
            tiles.append(now)
        return [[tiles[l][c] - fy[faces(l, c, part), :] for c in range(TILES)] for l in range(LEVS)]

    def two(pair, _):
        first = tracer(2 * pair)
        send_block(pair, first, tracer(2 * pair + 1))
        return 0

    def send_block(pair, first, second):
        block = REST
        for l in range(LEVS):
            slot = l * 4 + pair
            for g in range(GROUPS):
                pack(g, l, pl.multiple_of((pair * LEVS + l) * 8, 8), block, slot, first, second)

    def pack(g, l, at, block, slot, first, second):
        t, o = span_of(g)
        a = turn(first[l][t], -o, 1)
        b = turn(second[l][t], CHUNK - o, 1)
        if o + CHUNK > LANES:
            a = jnp.where(lane < LANES - o, a, turn(first[l][t + 1], -o, 1))
            lon = jnp.where(lane >= CHUNK, lane - CHUNK, lane + (LANES - CHUNK))
            b = jnp.where(lon < LANES - o, b, turn(second[l][t + 1], CHUNK - o, 1))
        out[g, pl.ds(at, 8), :] = jnp.where(lane < CHUNK, a, b)
        moved = pltpu.roll(b, slot * 16, 1)
        out[g, pl.ds(block, 8), :] = jnp.where((lane >> 4) == slot, moved, out[g, pl.ds(block, 8), :])

    lax.fori_loop(0, PAIRS - 1, two, 0)
    first, second = tracer(NTR - 1), air()
    for l in range(LEVS):
        for g in range(GROUPS):
            pack(g, l, ((PAIRS - 1) * LEVS + l) * 8, REST + 8, l * 4, first, second)


def target_kernel(index, offset, phase, *tables):
    lane, row = lane_index(), row_index()
    blank = jnp.zeros((8, LANES - CHUNK), F32)

    def rows_of(ref, n, part):
        if part == INNER:
            found = ref[n, pl.ds(4, 8), :]
            return jnp.concatenate([found, blank.astype(found.dtype)], 1)
        low, high = (jnp.concatenate([x, blank.astype(x.dtype)], 1) for x in (ref[n, pl.ds(0, 8), :], ref[n, pl.ds(8, 8), :]))
        return jnp.where((row & 1) == 0, pick(low, row >> 1), pick(high, 4 + (row >> 1)))

    for ref in tables:
        ref[pl.ds(0, 16), :] = jnp.zeros((16, LANES), ref.dtype)
    for n in range(2 * GROUPS - 1):
        for part in (INNER, OUTER):
            level, frac = tables[2 * part - 2 : 2 * part]
            s = rows_of(index, n, part)
            f = (rows_of(offset, n, part).astype(F32) + rows_of(phase, n, part)) * (1.0 / 32.0)
            for out, x in ((level, s), (frac, f)):
                moved = turn(x, CHUNK, 1)
                tail = jnp.where(lane < 16, moved, jnp.zeros_like(moved))
                tail = tail + turn(tail, 16, 1)
                tail = tail + turn(tail, 32, 1)
                other = turn(turn(tail, 64, 1), 4, 0)
                out[pl.ds((n + 1) * 16, 8), :] = jnp.where(lane < CHUNK, x, moved)
                out[pl.ds((n + 1) * 16 + 8, 8), :] = jnp.where(lane < 64, tail, other)


def remap_kernel(data, level, frac, out):
    lane, row = lane_index(), row_index()

    def targets(tile):
        found = []
        for parity in range(2):
            for half in range(2):
                start = (parity + 16 * half) * 16 + tile
                s = level[pl.ds(start, 8, stride=32), :]
                f = frac[pl.ds(start, 8, stride=32), :]
                square = f * f * 0.5
                cubic = 3.0 * square - f * f * f
                found.append(((s >> 1) & 7, s >= 16, (s & 1) == 1, f, square, cubic))
        return found

    def columns(even, odd, found):
        back = [turn(x, 1, 0) for x in odd]
        before = [jnp.where(row == 0, even[0], back[0]), jnp.where(row == 0, back[0], back[1])]
        left = [0.5 * (before[i] + even[i]) for i in range(2)]
        ahead = [turn(x, -1, 0) for x in left]
        right = [jnp.where(row == 7, ahead[1], ahead[0]), jnp.where(row == 7, odd[1], ahead[1])]
        pair = [even[i] + odd[i] for i in range(2)]
        run = list(pair)
        for shift in (1, 2, 4):
            run = [x + jnp.where(row >= shift, turn(x, shift, 0), 0.0) for x in run]
        half_sum = jnp.broadcast_to(run[0][7:8], (8, LANES))
        total = half_sum + run[1][7:8]
        below = [run[0] - pair[0], (run[1] - pair[1]) + half_sum]
        edges = []
        for where, high, is_odd, f, square, cubic in found:
            le, ri, ev, od, be = (
                jnp.where(high, pick(x[1], where), pick(x[0], where)) for x in (left, right, even, odd, below)
            )
            middle = 0.5 * (ev + od)
            lo = jnp.where(is_odd, middle, le)
            hi = jnp.where(is_odd, ri, middle)
            m = jnp.where(is_odd, od, ev)
            base = be + jnp.where(is_odd, ev, 0.0)
            edges.append(base + lo * f + (hi - lo) * square + ((m + m) - (lo + hi)) * cubic)
        ev0, ev1, od0, od1 = edges
        next0, next1 = turn(ev0, -1, 0), turn(ev1, -1, 0)
        new_even = [od0 - ev0, od1 - ev1]
        new_odd = [jnp.where(row == 7, next1, next0) - od0, jnp.where(row == 7, total, next1) - od1]
        return new_even, new_odd

    def span(start, half):
        return pl.ds(start + half * 8 * DEPTH, 8, stride=DEPTH)

    def main(tile, _):
        found = targets(tile)
        for pair in range(PAIRS):
            at = [(pair * LEVS + l) * 8 + tile for l in range(LEVS)]
            even, odd = ([data[span(at[l], half), :] for half in range(2)] for l in range(LEVS))
            new = columns(even, odd, found)
            for l in range(LEVS):
                for half in range(2):
                    out[span(at[l], half), :] = new[l][half]
        return 0

    lax.fori_loop(0, 8, main, 0)

    def tail(tile, _):
        found = targets(8 + tile)
        for block in range(BLOCKS):
            at = [REST + 8 * block + tile, REST + 8 * block + tile + 4]
            a, b = ([data[span(at[i], half), :] for half in range(2)] for i in range(2))
            even = [jnp.where(lane < 64, a[half], turn(b[half], 64, 1)) for half in range(2)]
            odd = [jnp.where(lane < 64, turn(a[half], 64, 1), b[half]) for half in range(2)]
            even, odd = columns(even, odd, found)
            for half in range(2):
                out[span(at[0], half), :] = jnp.where(lane < 64, even[half], turn(odd[half], 64, 1))
                out[span(at[1], half), :] = jnp.where(lane < 64, turn(even[half], 64, 1), odd[half])
        return 0

    lax.fori_loop(0, 4, tail, 0)


def collect_kernel(part, data, *refs):
    out, flat, sem = refs[-3:]
    lane = lane_index()

    def unpack(pair, at, block, slot):
        for l in range(LEVS):
            pieces = []
            for g in range(GROUPS):
                _, o = span_of(g)
                main = data[g, at(l), :]
                tail = pltpu.roll(data[g, pl.ds(block, 8), :], LANES - (l * 4 + slot) * 16, 1)
                mixed = jnp.where(lane < 16, tail, main)
                pieces.append((turn(main, o, 1), turn(mixed, o - CHUNK, 1)))
            for second in range(2):
                for c in range(TILES):
                    value = None
                    for g in range(GROUPS):
                        start = CHUNK * g - LANES * c
                        if start >= LANES or start + CHUNK <= 0:
                            continue
                        piece = pieces[g][second]
                        value = piece if value is None else jnp.where(lane >= start, piece, value)
                    flat[pl.ds((2 * pair + second) * 8 * STEP + c * LEVS + l, 8, stride=STEP), :] = value

    def one(pair, _):
        unpack(pair, lambda l: pl.ds(pl.multiple_of((pair * LEVS + l) * 8, 8), 8), REST, pair)
        return 0

    lax.fori_loop(0, PAIRS - 1, one, 0)
    unpack(PAIRS - 1, lambda l: pl.ds(((PAIRS - 1) * LEVS + l) * 8, 8), REST + 8, 0)
    view = flat.reshape(FIELDS, 8 // part, part, TILES, LEVS, LANES)
    copies = []
    for c in range(TILES):
        cut = pl.ds(LANES * c, LANES)
        for run, first in enumerate((4,) if part == INNER else (0, 12)):
            target = out.at[:, pl.ds(first, 8 // part), :, cut]
            copies.append(pltpu.make_async_copy(view.at[:, :, run, c], target, sem.at[len(copies)]))
    for copy in copies:
        copy.start()
    for copy in copies:
        copy.wait()


ANYWHERE = pl.BlockSpec(memory_space=pl.ANY)
IN_VMEM = pl.BlockSpec(memory_space=pltpu.VMEM)
PARAMS = pltpu.CompilerParams(vmem_limit_bytes=VMEM_LIMIT)


def transport(part, *given):
    factor = pltpu.VMEM((STEP * 8, LANES), F32)
    scalars = [pl.BlockSpec(memory_space=pltpu.SMEM)] if part == OUTER else []
    return pl.pallas_call(
        functools.partial(transport_kernel, part),
        out_shape=jax.ShapeDtypeStruct((GROUPS, DEPTH, LANES), F32),
        in_specs=scalars + [ANYWHERE] * (len(given) - len(scalars)),
        out_specs=IN_VMEM,
        scratch_shapes=[
            pltpu.VMEM(((NTR + 3) * slots_of(part) * STEP, LANES), F32),
            factor,
            factor,
            factor,
            factor,
            pltpu.VMEM((STEP * 16, LANES), F32),
            pltpu.SemaphoreType.DMA((10 * TILES,)),
        ],
        compiler_params=PARAMS,
    )(*given)


def remap(data, level, frac):
    return pl.pallas_call(
        remap_kernel,
        out_shape=jax.ShapeDtypeStruct((GROUPS * DEPTH, LANES), F32),
        in_specs=[IN_VMEM] * 3,
        out_specs=IN_VMEM,
        compiler_params=PARAMS,
    )(data.reshape(GROUPS * DEPTH, LANES), level, frac).reshape(GROUPS, DEPTH, LANES)


def collect(part, data, result):
    given = (data,) if result is None else (data, result)
    return pl.pallas_call(
        functools.partial(collect_kernel, part),
        out_shape=jax.ShapeDtypeStruct((FIELDS, ROWS, LEVS, LONS), F32),
        in_specs=[IN_VMEM, ANYWHERE][: len(given)],
        out_specs=ANYWHERE,
        scratch_shapes=[
            pltpu.VMEM((FIELDS * 8 * STEP, LANES), F32),
            pltpu.SemaphoreType.DMA((2 * TILES,)),
        ],
        input_output_aliases={} if result is None else {1: 0},
        compiler_params=PARAMS,
    )(*given)


def exchange(data):
    return lax.all_to_all(data, "lev", split_axis=0, concat_axis=0, tiled=True)


def shards(tracers, thickness, courant_x, courant_y, level_index, level_offset, level_phase):
    rim = jax.ShapeDtypeStruct((NTR + 2, 2, LEVS, LONS), F32)
    south, north = pl.pallas_call(
        halo_kernel,
        out_shape=(rim, rim),
        in_specs=[ANYWHERE] * 3,
        out_specs=(IN_VMEM, IN_VMEM),
        scratch_shapes=[pltpu.SemaphoreType.DMA((2, 3))],
    )(tracers, thickness, courant_y)
    count = lax.axis_size("lat")
    low = lax.ppermute(north, "lat", [(i, i + 1) for i in range(count - 1)])
    high = lax.ppermute(south, "lat", [(i + 1, i) for i in range(count - 1)])
    own = (tracers, thickness, courant_x, courant_y)
    inner = exchange(transport(INNER, *own))
    lat = lax.axis_index("lat").astype(jnp.int32).reshape(1)
    outer = exchange(transport(OUTER, lat, *own, low, high))
    table = (2 * GROUPS * 16, LANES)
    tables = (jax.ShapeDtypeStruct(table, jnp.int32), jax.ShapeDtypeStruct(table, F32))
    places = pl.pallas_call(
        target_kernel,
        out_shape=tables + tables,
        in_specs=[IN_VMEM] * 3,
        out_specs=(IN_VMEM,) * 4,
        compiler_params=PARAMS,
    )(level_index, level_offset, level_phase)
    inner = exchange(remap(inner, *places[:2]))
    outer = exchange(remap(outer, *places[2:]))
    return collect(OUTER, outer, collect(INNER, inner, None))


def solution(mesh):
    in_specs = (
        P(None, "lat", "lev", None),
        P("lat", "lev", None),
        P("lat", "lev", None),
        P("lat", "lev", None),
        P(None, "lat", "lev"),
        P(None, "lat", "lev"),
        P(None, "lat", "lev"),
    )
    out_specs = P(None, "lat", "lev", None)
    return jax.shard_map(shards, mesh=mesh, in_specs=in_specs, out_specs=out_specs, check_vma=False)
```

time: 156 us -> 121 us (0.78)
  the two profiles are of different devices: /device:TPU:7 before, /device:TPU:2 now
where the time goes in v2:
time: 121 us; the launch traced here: 120 us
  waiting for transfers between devices  58.7 us (49%)
  Pallas kernels  31.7 us (26%)
  starting transfers between devices  25.2 us (21%)
  local copies, waits for them, and re-layouts  4.09 us (3%)
    all_to_all x4, waiting for transfers between devices, exchange(): return lax.all_to_all(data, 'lev', split_axis=0, concat_axis=0, tiled=True)  55.2 us
    all_to_all x4, starting transfers between devices, exchange(): return lax.all_to_all(data, 'lev', split_axis=0, concat_axis=0, tiled=True)  19.6 us
    pallas_call x2, Pallas kernels, transport(): pl.pallas_call(functools.partial(transport_kernel, part), out_shape=jax.S...  11.1 us
    pallas_call x1, Pallas kernels, shards(): pl.pallas_call(target_kernel, out_shape=tables + tables, in_specs=[IN_VME...  8.13 us
    pallas_call x2, Pallas kernels, remap(): pl.pallas_call(remap_kernel, out_shape=jax.ShapeDtypeStruct((GROUPS * DEP...  6.76 us
    unnamed x22, local copies, waits for them, and re-layouts  4.09 us
    pallas_call x2, Pallas kernels, collect(): pl.pallas_call(functools.partial(collect_kernel, part), out_shape=jax.Sha...  3.89 us
    ppermute x1, starting transfers between devices, shards(): high = lax.ppermute(south, 'lat', [(i + 1, i) for i in range(count - 1)])  3.64 us
  transfers between devices with their start and end apart: 6, of which 6 were waited for; matrix products, arithmetic and copies ran while one was open for 0% of the time, Pallas kernels for 20%

profile of v2, /device:TPU:2, one launch (start us, length us, event | category | flops | bytes accessed | tf_op | source)
XLA Modules:
  0.0 119.9 jit_solution(7013028179200332971)
XLA Ops:
  0.0 0.0 copy-start
  0.0 1.3 %copy-done = f32[9,16,2,1152]{3,2,1,0:T(2,128)S(1)} copy-done((f32[9,16,2,1152]{3,2,1,0:T(2,128)S(1)}, f32[9,16,2,1152]{3,2,1,0:T(2,128)}, u32[]{:S(2)}) %copy-start) | copy-done | bytes 1327128
  1.3 0.0 copy-start.2
  1.3 0.9 copy-done.2
  2.2 0.0 copy-start.4
  2.2 0.9 copy-done.4
  3.1 0.0 copy-start.6
  3.1 0.9 copy-done.6
  4.1 5.4 %shard_map.77 = f32[16,96,128]{2,1,0:T(8,128)} custom-call(f32[9,16,2,1152]{3,2,1,0:T(2,128)S(1)} %copy-done, f32[16,2,1152]{2,1,0:T(2,128)S(1)} %copy-done.2, f32[16,2,1152]{2,1,0:T(2,128)S(1)} %copy-done.6, f32[16,2,1152]{2,1,0:T(2,128)S(1)} %copy-done.4), custom_call_target="tpu_custom_call" | custom-call | tf_op jit(solution)/shard_map/pallas_call | solution.py:380
  9.5 0.0 copy-start.1
  9.5 0.0 copy-start.3
  9.5 0.0 copy-start.5
  9.5 0.0 copy-start.7
  9.5 8.8 %all-to-all-start.2 = ((f32[16,96,128]{2,1,0:T(8,128)}), f32[16,96,128]{2,1,0:T(8,128)S(1)}, u32[]{:S(2)}, u32[]{:S(2)}) async-start(f32[16,96,128]{2,1,0:T(8,128)} %shard_map.77), calls=%async_computation.2 | async-start | bytes 1572864 | tf_op jit(solution)/shard_map/all_to_all | solution.py:425
  18.3 1.8 %shard_map.73 = (f32[11,2,2,1152]{3,2,1,0:T(2,128)}, f32[11,2,2,1152]{3,2,1,0:T(2,128)}) custom-call(f32[9,16,2,1152]{3,2,1,0:T(2,128)} %refs_0_.1, f32[16,2,1152]{2,1,0:T(2,128)} %refs_1_.3, f32[16,2,1152]{2,1,0:T(2,128)} %refs_3_.3), custom_call_target="tpu_custom_call" | custom-call | tf_op jit(solution)/shard_map/pallas_call | solution.py:430
  20.2 1.9 %collective-permute-start = (f32[11,2,2,1152]{3,2,1,0:T(2,128)}, f32[11,2,2,1152]{3,2,1,0:T(2,128)S(1)}, u32[]{:S(2)}, u32[]{:S(2)}) collective-permute-start(f32[11,2,2,1152]{3,2,1,0:T(2,128)} %get-tuple-element.11), channel_id=1, source_target_pairs={{0,16},{16,32},{32,48},{48,64},{64,80},{80,96},{96,112},{112,128},... | collective-permute-start | bytes 608264 | tf_op jit(solution)/shard_map/ppermute | solution.py:438
  22.1 3.6 %collective-permute-start.1 = (f32[11,2,2,1152]{3,2,1,0:T(2,128)}, f32[11,2,2,1152]{3,2,1,0:T(2,128)S(1)}, u32[]{:S(2)}, u32[]{:S(2)}) collective-permute-start(f32[11,2,2,1152]{3,2,1,0:T(2,128)} %get-tuple-element.12), channel_id=1, source_target_pairs={{16,0},{32,16},{48,32},{64,48},{80,64},{96,80},{112,96},{128,112},... | collective-permute-start | bytes 608264 | tf_op jit(solution)/shard_map/ppermute | solution.py:439
  25.8 1.7 %collective-permute-done.refs_5_ = f32[11,2,2,1152]{3,2,1,0:T(2,128)S(1)} collective-permute-done((f32[11,2,2,1152]{3,2,1,0:T(2,128)}, f32[11,2,2,1152]{3,2,1,0:T(2,128)S(1)}, u32[]{:S(2)}, u32[]{:S(2)}) %collective-permute-start) | collective-permute-done | bytes 202784 | tf_op jit(solution)/shard_map/ppermute | solution.py:438
  27.4 1.9 %collective-permute-done.1.refs_6_ = f32[11,2,2,1152]{3,2,1,0:T(2,128)S(1)} collective-permute-done((f32[11,2,2,1152]{3,2,1,0:T(2,128)}, f32[11,2,2,1152]{3,2,1,0:T(2,128)S(1)}, u32[]{:S(2)}, u32[]{:S(2)}) %collective-permute-start.1) | collective-permute-done | bytes 202784 | tf_op jit(solution)/shard_map/ppermute | solution.py:439
  29.3 0.0 copy-done.1
  29.3 0.0 copy-done.3
  29.3 0.0 copy-done.5
  29.3 0.0 copy-done.7
  29.3 5.7 %shard_map.74 = f32[16,96,128]{2,1,0:T(8,128)} custom-call(s32[1]{0:T(128)} %bitcast.refs_0_, f32[9,16,2,1152]{3,2,1,0:T(2,128)S(1)} %copy-done.1, f32[16,2,1152]{2,1,0:T(2,128)S(1)} %copy-done.3, f32[16,2,1152]{2,1,0:T(2,128)S(1)} %copy-done.7, f32[16,2,1152]{2,1,0:T(2,128)S(1)} %copy-done.5, f32[11,2,2,1152]{3,2,1,0:T(2,128)S(1)} %collective-permute-done.refs_5_, ...), custom_call_target="tpu_custom_call" | custom-call | tf_op jit(solution)/shard_map/pallas_call | solution.py:380
  35.0 0.0 copy-start.8
  35.0 0.0 copy-start.9
  35.0 0.0 copy-start.10
  35.0 5.5 %all-to-all-done.2 = f32[16,96,128]{2,1,0:T(8,128)S(1)} async-done(((f32[16,96,128]{2,1,0:T(8,128)}), f32[16,96,128]{2,1,0:T(8,128)S(1)}, u32[]{:S(2)}, u32[]{:S(2)}) %all-to-all-start.2) | async-done | bytes 786464 | tf_op jit(solution)/shard_map/all_to_all | solution.py:425
  40.5 3.6 %all-to-all-start = ((f32[16,96,128]{2,1,0:T(8,128)}), f32[16,96,128]{2,1,0:T(8,128)S(1)}, u32[]{:S(2)}, u32[]{:S(2)}) async-start(f32[16,96,128]{2,1,0:T(8,128)} %shard_map.74), calls=%async_computation | async-start | bytes 1572864 | tf_op jit(solution)/shard_map/all_to_all | solution.py:425
  44.1 0.0 copy-done.8
  44.1 0.0 copy-done.9
  44.1 0.0 copy-done.10
  44.1 8.1 %shard_map.75 = (s32[512,128]{1,0:T(8,128)S(1)}, f32[512,128]{1,0:T(8,128)S(1)}, s32[512,128]{1,0:T(8,128)S(1)}, f32[512,128]{1,0:T(8,128)S(1)}) custom-call(s32[31,16,72]{2,1,0:T(8,128)S(1)} %copy-done.8, s32[31,16,72]{2,1,0:T(8,128)S(1)} %copy-done.9, f32[31,16,72]{2,1,0:T(8,128)S(1)} %copy-done.10), custom_call_target="tpu_custom_call" | custom-call | tf_op jit(solution)/shard_map/pallas_call | solution.py:446
  52.3 3.4 %shard_map.78 = f32[1536,128]{1,0:T(8,128)} custom-call(f32[1536,128]{1,0:T(8,128)S(1)} %bitcast.5, s32[512,128]{1,0:T(8,128)S(1)} %get-tuple-element.15.level, f32[512,128]{1,0:T(8,128)S(1)} %get-tuple-element.16.frac), custom_call_target="tpu_custom_call" | custom-call | tf_op jit(solution)/shard_map/pallas_call | solution.py:399
  55.7 11.3 %all-to-all-done = f32[16,96,128]{2,1,0:T(8,128)S(1)} async-done(((f32[16,96,128]{2,1,0:T(8,128)}), f32[16,96,128]{2,1,0:T(8,128)S(1)}, u32[]{:S(2)}, u32[]{:S(2)}) %all-to-all-start) | async-done | bytes 786464 | tf_op jit(solution)/shard_map/all_to_all | solution.py:425
  67.0 3.6 %all-to-all-start.3 = ((f32[16,96,128]{2,1,0:T(8,128)}), f32[16,96,128]{2,1,0:T(8,128)S(1)}, u32[]{:S(2)}, u32[]{:S(2)}) async-start(f32[16,96,128]{2,1,0:T(8,128)} %bitcast.4), calls=%async_computation.3 | async-start | bytes 1572864 | tf_op jit(solution)/shard_map/all_to_all | solution.py:425
  70.6 3.4 %shard_map.76 = f32[1536,128]{1,0:T(8,128)} custom-call(f32[1536,128]{1,0:T(8,128)S(1)} %bitcast.6, s32[512,128]{1,0:T(8,128)S(1)} %get-tuple-element.13.level, f32[512,128]{1,0:T(8,128)S(1)} %get-tuple-element.14.frac), custom_call_target="tpu_custom_call" | custom-call | tf_op jit(solution)/shard_map/pallas_call | solution.py:399
  74.0 18.5 %all-to-all-done.3.data = f32[16,96,128]{2,1,0:T(8,128)S(1)} async-done(((f32[16,96,128]{2,1,0:T(8,128)}), f32[16,96,128]{2,1,0:T(8,128)S(1)}, u32[]{:S(2)}, u32[]{:S(2)}) %all-to-all-start.3) | async-done | bytes 786464 | tf_op jit(solution)/shard_map/all_to_all | solution.py:425
  92.5 3.6 %all-to-all-start.1 = ((f32[16,96,128]{2,1,0:T(8,128)}), f32[16,96,128]{2,1,0:T(8,128)S(1)}, u32[]{:S(2)}, u32[]{:S(2)}) async-start(f32[16,96,128]{2,1,0:T(8,128)} %bitcast.2), calls=%async_computation.1 | async-start | bytes 1572864 | tf_op jit(solution)/shard_map/all_to_all | solution.py:425
  96.1 2.0 %shard_map.79.refs_0_ = f32[10,16,2,1152]{3,2,1,0:T(2,128)} custom-call(f32[16,96,128]{2,1,0:T(8,128)S(1)} %all-to-all-done.3.data), custom_call_target="tpu_custom_call" | custom-call | tf_op jit(solution)/shard_map/pallas_call | solution.py:410
  98.1 19.9 %all-to-all-done.1.data = f32[16,96,128]{2,1,0:T(8,128)S(1)} async-done(((f32[16,96,128]{2,1,0:T(8,128)}), f32[16,96,128]{2,1,0:T(8,128)S(1)}, u32[]{:S(2)}, u32[]{:S(2)}) %all-to-all-start.1) | async-done | bytes 786464 | tf_op jit(solution)/shard_map/all_to_all | solution.py:425
  118.0 1.9 %shard_map.80 = f32[10,16,2,1152]{3,2,1,0:T(2,128)} custom-call(f32[16,96,128]{2,1,0:T(8,128)S(1)} %all-to-all-done.1.data, f32[10,16,2,1152]{3,2,1,0:T(2,128)} %shard_map.79.refs_0_), custom_call_target="tpu_custom_call", output_to_operand_aliasing={{}: (1, {})} | custom-call | tf_op jit(solution)/shard_map/pallas_call | solution.py:410
Async XLA Ops:
  0.0 1.3 %copy-start = (f32[9,16,2,1152]{3,2,1,0:T(2,128)S(1)}, f32[9,16,2,1152]{3,2,1,0:T(2,128)}, u32[]{:S(2)}) copy-start(f32[9,16,2,1152]{3,2,1,0:T(2,128)} %refs_0_.1) | copy-start | bytes 3981316
  1.3 0.9 copy-start.2
  2.2 0.9 copy-start.4
  3.1 0.9 copy-start.6
  9.5 19.8 %copy-start.1 = (f32[9,16,2,1152]{3,2,1,0:T(2,128)S(1)}, f32[9,16,2,1152]{3,2,1,0:T(2,128)}, u32[]{:S(2)}) copy-start(f32[9,16,2,1152]{3,2,1,0:T(2,128)} %refs_0_.1) | copy-start | bytes 3981316
  9.5 19.8 %copy-start.3 = (f32[16,2,1152]{2,1,0:T(2,128)S(1)}, f32[16,2,1152]{2,1,0:T(2,128)}, u32[]{:S(2)}) copy-start(f32[16,2,1152]{2,1,0:T(2,128)} %refs_1_.3) | copy-start | bytes 442372
  9.5 19.8 %copy-start.5 = (f32[16,2,1152]{2,1,0:T(2,128)S(1)}, f32[16,2,1152]{2,1,0:T(2,128)}, u32[]{:S(2)}) copy-start(f32[16,2,1152]{2,1,0:T(2,128)} %refs_3_.3) | copy-start | bytes 442372
  9.5 19.8 %copy-start.7 = (f32[16,2,1152]{2,1,0:T(2,128)S(1)}, f32[16,2,1152]{2,1,0:T(2,128)}, u32[]{:S(2)}) copy-start(f32[16,2,1152]{2,1,0:T(2,128)} %refs_2_.3) | copy-start | bytes 442372
  9.5 30.9 %all-to-all-start.2 = ((f32[16,96,128]{2,1,0:T(8,128)}), f32[16,96,128]{2,1,0:T(8,128)S(1)}, u32[]{:S(2)}, u32[]{:S(2)}) async-start(f32[16,96,128]{2,1,0:T(8,128)} %shard_map.77), calls=%async_computation.2 | async-start | bytes 1572864 | tf_op jit(solution)/shard_map/all_to_all | solution.py:425
  20.2 7.3 %collective-permute-start = (f32[11,2,2,1152]{3,2,1,0:T(2,128)}, f32[11,2,2,1152]{3,2,1,0:T(2,128)S(1)}, u32[]{:S(2)}, u32[]{:S(2)}) collective-permute-start(f32[11,2,2,1152]{3,2,1,0:T(2,128)} %get-tuple-element.11), channel_id=1, source_target_pairs={{0,16},{16,32},{32,48},{48,64},{64,80},{80,96},{96,112},{112,128},... | collective-permute-start | bytes 608264 | tf_op jit(solution)/shard_map/ppermute | solution.py:438
  22.1 7.2 %collective-permute-start.1 = (f32[11,2,2,1152]{3,2,1,0:T(2,128)}, f32[11,2,2,1152]{3,2,1,0:T(2,128)S(1)}, u32[]{:S(2)}, u32[]{:S(2)}) collective-permute-start(f32[11,2,2,1152]{3,2,1,0:T(2,128)} %get-tuple-element.12), channel_id=1, source_target_pairs={{16,0},{32,16},{48,32},{64,48},{80,64},{96,80},{112,96},{128,112},... | collective-permute-start | bytes 608264 | tf_op jit(solution)/shard_map/ppermute | solution.py:439
  35.0 9.1 %copy-start.8 = (s32[31,16,72]{2,1,0:T(8,128)S(1)}, s32[31,16,72]{2,1,0:T(8,128)}, u32[]{:S(2)}) copy-start(s32[31,16,72]{2,1,0:T(8,128)} %index.1) | copy-start | bytes 428548
  35.0 9.1 %copy-start.9 = (s32[31,16,72]{2,1,0:T(8,128)S(1)}, s32[31,16,72]{2,1,0:T(8,128)}, u32[]{:S(2)}) copy-start(s32[31,16,72]{2,1,0:T(8,128)} %offset.1) | copy-start | bytes 428548
  35.0 9.1 %copy-start.10 = (f32[31,16,72]{2,1,0:T(8,128)S(1)}, f32[31,16,72]{2,1,0:T(8,128)}, u32[]{:S(2)}) copy-start(f32[31,16,72]{2,1,0:T(8,128)} %phase.1) | copy-start | bytes 428548
  40.5 26.5 %all-to-all-start = ((f32[16,96,128]{2,1,0:T(8,128)}), f32[16,96,128]{2,1,0:T(8,128)S(1)}, u32[]{:S(2)}, u32[]{:S(2)}) async-start(f32[16,96,128]{2,1,0:T(8,128)} %shard_map.74), calls=%async_computation | async-start | bytes 1572864 | tf_op jit(solution)/shard_map/all_to_all | solution.py:425
  67.0 25.5 %all-to-all-start.3 = ((f32[16,96,128]{2,1,0:T(8,128)}), f32[16,96,128]{2,1,0:T(8,128)S(1)}, u32[]{:S(2)}, u32[]{:S(2)}) async-start(f32[16,96,128]{2,1,0:T(8,128)} %bitcast.4), calls=%async_computation.3 | async-start | bytes 1572864 | tf_op jit(solution)/shard_map/all_to_all | solution.py:425
  92.5 25.5 %all-to-all-start.1 = ((f32[16,96,128]{2,1,0:T(8,128)}), f32[16,96,128]{2,1,0:T(8,128)S(1)}, u32[]{:S(2)}, u32[]{:S(2)}) async-start(f32[16,96,128]{2,1,0:T(8,128)} %bitcast.2), calls=%async_computation.1 | async-start | bytes 1572864 | tf_op jit(solution)/shard_map/all_to_all | solution.py:425

commit v3 on v2

--- a/solution.py
+++ b/solution.py
@@ -82,7 +82,7 @@
     if part == OUTER:
         lat, tracers, thickness, courant_x, courant_y, low, high, out, held, mx, ax, my, ay, fy, sem = refs
     else:
-        tracers, thickness, courant_x, courant_y, out, held, mx, ax, my, ay, fy, sem = refs
+        tracers, thickness, courant_x, courant_y, _, out, held, mx, ax, my, ay, fy, sem = refs
     slots = slots_of(part)
     lane, row = lane_index(), row_index()
     view = held.reshape(NTR + 3, slots // part, part, TILES, LEVS, LANES)
@@ -370,6 +370,7 @@
 
 
 ANYWHERE = pl.BlockSpec(memory_space=pl.ANY)
+IN_HBM = pl.BlockSpec(memory_space=pltpu.HBM)
 IN_VMEM = pl.BlockSpec(memory_space=pltpu.VMEM)
 PARAMS = pltpu.CompilerParams(vmem_limit_bytes=VMEM_LIMIT)
 
@@ -377,10 +378,11 @@
 def transport(part, *given):
     factor = pltpu.VMEM((STEP * 8, LANES), F32)
     scalars = [pl.BlockSpec(memory_space=pltpu.SMEM)] if part == OUTER else []
+    others = [ANYWHERE] * (len(given) - len(scalars) - 4)
     return pl.pallas_call(
         functools.partial(transport_kernel, part),
         out_shape=jax.ShapeDtypeStruct((GROUPS, DEPTH, LANES), F32),
-        in_specs=scalars + [ANYWHERE] * (len(given) - len(scalars)),
+        in_specs=scalars + [IN_HBM] * 4 + others,
         out_specs=IN_VMEM,
         scratch_shapes=[
             pltpu.VMEM(((NTR + 3) * slots_of(part) * STEP, LANES), F32),
@@ -426,19 +428,19 @@
 
 
 def shards(tracers, thickness, courant_x, courant_y, level_index, level_offset, level_phase):
+    own = [pltpu.with_memory_space_constraint(x, pltpu.HBM) for x in (tracers, thickness, courant_x, courant_y)]
     rim = jax.ShapeDtypeStruct((NTR + 2, 2, LEVS, LONS), F32)
     south, north = pl.pallas_call(
         halo_kernel,
         out_shape=(rim, rim),
-        in_specs=[ANYWHERE] * 3,
+        in_specs=[IN_HBM] * 3,
         out_specs=(IN_VMEM, IN_VMEM),
         scratch_shapes=[pltpu.SemaphoreType.DMA((2, 3))],
-    )(tracers, thickness, courant_y)
+    )(own[0], own[1], own[3])
     count = lax.axis_size("lat")
     low = lax.ppermute(north, "lat", [(i, i + 1) for i in range(count - 1)])
     high = lax.ppermute(south, "lat", [(i + 1, i) for i in range(count - 1)])
-    own = (tracers, thickness, courant_x, courant_y)
-    inner = exchange(transport(INNER, *own))
+    inner = exchange(transport(INNER, *own, south))
     lat = lax.axis_index("lat").astype(jnp.int32).reshape(1)
     outer = exchange(transport(OUTER, lat, *own, low, high))
     table = (2 * GROUPS * 16, LANES)

time: 121 us -> 123 us (1.017)
  the two profiles are of different devices: /device:TPU:2 before, /device:TPU:7 now
where the time goes in v3:
time: 123 us; the launch traced here: 121 us
  waiting for transfers between devices  53.7 us (44%)
  Pallas kernels  33.5 us (27%)
  starting transfers between devices  33 us (27%)
    all_to_all x4, waiting for transfers between devices, exchange(): return lax.all_to_all(data, 'lev', split_axis=0, concat_axis=0, tiled=True)  42.4 us
    all_to_all x4, starting transfers between devices, exchange(): return lax.all_to_all(data, 'lev', split_axis=0, concat_axis=0, tiled=True)  24.2 us
    pallas_call x2, Pallas kernels, transport(): pl.pallas_call(functools.partial(transport_kernel, part), out_shape=jax.S...  12.9 us
    pallas_call x1, Pallas kernels, shards(): pl.pallas_call(target_kernel, out_shape=tables + tables, in_specs=[IN_VME...  8.13 us
    ppermute x1, starting transfers between devices, shards(): low = lax.ppermute(north, 'lat', [(i, i + 1) for i in range(count - 1)])  6.88 us
    pallas_call x2, Pallas kernels, remap(): pl.pallas_call(remap_kernel, out_shape=jax.ShapeDtypeStruct((GROUPS * DEP...  6.77 us
    ppermute x1, waiting for transfers between devices, shards(): low = lax.ppermute(north, 'lat', [(i, i + 1) for i in range(count - 1)])  6.67 us
    ppermute x1, waiting for transfers between devices, shards(): high = lax.ppermute(south, 'lat', [(i + 1, i) for i in range(count - 1)])  4.67 us
  transfers between devices with their start and end apart: 6, of which 5 were waited for; matrix products, arithmetic and copies ran while one was open for 0% of the time, Pallas kernels for 19%

profile of v3, /device:TPU:7, one launch (start us, length us, event | category | flops | bytes accessed | tf_op | source)
XLA Modules:
  0.0 121.4 jit_solution(4725358253217534929)
XLA Ops:
  0.0 1.9 %shard_map.73 = (f32[11,2,2,1152]{3,2,1,0:T(2,128)}, f32[11,2,2,1152]{3,2,1,0:T(2,128)}) custom-call(f32[9,16,2,1152]{3,2,1,0:T(2,128)} %refs_0_.1, f32[16,2,1152]{2,1,0:T(2,128)} %refs_1_.3, f32[16,2,1152]{2,1,0:T(2,128)} %refs_3_.3), custom_call_target="tpu_custom_call" | custom-call | tf_op jit(solution)/shard_map/pallas_call | solution.py:433
  1.9 0.0 copy-start.3
  1.9 0.9 copy-done.3
  2.8 6.4 %shard_map.77 = f32[16,96,128]{2,1,0:T(8,128)} custom-call(f32[9,16,2,1152]{3,2,1,0:T(2,128)} %refs_0_.1, f32[16,2,1152]{2,1,0:T(2,128)} %refs_1_.3, f32[16,2,1152]{2,1,0:T(2,128)} %refs_2_.3, f32[16,2,1152]{2,1,0:T(2,128)} %refs_3_.3, f32[11,2,2,1152]{3,2,1,0:T(2,128)S(1)} %copy-done.3), custom_call_target="tpu_custom_call" | custom-call | tf_op jit(solution)/shard_map/pallas_call | solution.py:382
  9.2 0.0 copy-start.5
  9.2 0.0 copy-start.4
  9.2 8.5 %all-to-all-start.2 = ((f32[16,96,128]{2,1,0:T(8,128)}), f32[16,96,128]{2,1,0:T(8,128)S(1)}, u32[]{:S(2)}, u32[]{:S(2)}) async-start(f32[16,96,128]{2,1,0:T(8,128)} %shard_map.77), calls=%async_computation.2 | async-start | bytes 1572864 | tf_op jit(solution)/shard_map/all_to_all | solution.py:427
  17.7 0.0 copy-done.5
  17.8 6.9 %collective-permute-start = (f32[11,2,2,1152]{3,2,1,0:T(2,128)S(1)}, f32[11,2,2,1152]{3,2,1,0:T(2,128)S(1)}, u32[]{:S(2)}, u32[]{:S(2)}) collective-permute-start(f32[11,2,2,1152]{3,2,1,0:T(2,128)S(1)} %copy-done.5), channel_id=1, source_target_pairs={{0,16},{16,32},{32,48},{48,64},{64,80},{80,96},{96,112},{112,128},... | collective-permute-start | bytes 608264 | tf_op jit(solution)/shard_map/ppermute | solution.py:441
  24.6 0.0 copy-done.4
  24.6 1.9 %collective-permute-start.1 = (f32[11,2,2,1152]{3,2,1,0:T(2,128)S(1)}, f32[11,2,2,1152]{3,2,1,0:T(2,128)S(1)}, u32[]{:S(2)}, u32[]{:S(2)}) collective-permute-start(f32[11,2,2,1152]{3,2,1,0:T(2,128)S(1)} %copy-done.4), channel_id=1, source_target_pairs={{16,0},{32,16},{48,32},{64,48},{80,64},{96,80},{112,96},{128,112},... | collective-permute-start | bytes 608264 | tf_op jit(solution)/shard_map/ppermute | solution.py:442
  26.6 6.7 %collective-permute-done.refs_5_ = f32[11,2,2,1152]{3,2,1,0:T(2,128)S(1)} collective-permute-done((f32[11,2,2,1152]{3,2,1,0:T(2,128)S(1)}, f32[11,2,2,1152]{3,2,1,0:T(2,128)S(1)}, u32[]{:S(2)}, u32[]{:S(2)}) %collective-permute-start) | collective-permute-done | bytes 202784 | tf_op jit(solution)/shard_map/ppermute | solution.py:441
  33.3 4.7 %collective-permute-done.1.refs_6_ = f32[11,2,2,1152]{3,2,1,0:T(2,128)S(1)} collective-permute-done((f32[11,2,2,1152]{3,2,1,0:T(2,128)S(1)}, f32[11,2,2,1152]{3,2,1,0:T(2,128)S(1)}, u32[]{:S(2)}, u32[]{:S(2)}) %collective-permute-start.1) | collective-permute-done | bytes 202784 | tf_op jit(solution)/shard_map/ppermute | solution.py:442
  37.9 6.4 %shard_map.74 = f32[16,96,128]{2,1,0:T(8,128)} custom-call(s32[1]{0:T(128)} %bitcast.refs_0_, f32[9,16,2,1152]{3,2,1,0:T(2,128)} %refs_0_.1, f32[16,2,1152]{2,1,0:T(2,128)} %refs_1_.3, f32[16,2,1152]{2,1,0:T(2,128)} %refs_2_.3, f32[16,2,1152]{2,1,0:T(2,128)} %refs_3_.3, f32[11,2,2,1152]{3,2,1,0:T(2,128)S(1)} %collective-permute-done.refs_5_, ...), custom_call_target="tpu_custom_call" | custom-call | tf_op jit(solution)/shard_map/pallas_call | solution.py:382
  44.4 0.0 copy-start
  44.4 0.0 copy-start.1
  44.4 0.0 copy-start.2
  44.4 0.0 all-to-all-done.2
  44.4 8.4 %all-to-all-start = ((f32[16,96,128]{2,1,0:T(8,128)}), f32[16,96,128]{2,1,0:T(8,128)S(1)}, u32[]{:S(2)}, u32[]{:S(2)}) async-start(f32[16,96,128]{2,1,0:T(8,128)} %shard_map.74), calls=%async_computation | async-start | bytes 1572864 | tf_op jit(solution)/shard_map/all_to_all | solution.py:427
  52.9 0.0 copy-done
  52.9 0.0 copy-done.1
  52.9 0.0 copy-done.2
  52.9 8.1 %shard_map.75 = (s32[512,128]{1,0:T(8,128)S(1)}, f32[512,128]{1,0:T(8,128)S(1)}, s32[512,128]{1,0:T(8,128)S(1)}, f32[512,128]{1,0:T(8,128)S(1)}) custom-call(s32[31,16,72]{2,1,0:T(8,128)S(1)} %copy-done, s32[31,16,72]{2,1,0:T(8,128)S(1)} %copy-done.1, f32[31,16,72]{2,1,0:T(8,128)S(1)} %copy-done.2), custom_call_target="tpu_custom_call" | custom-call | tf_op jit(solution)/shard_map/pallas_call | solution.py:448
  61.0 3.4 %shard_map.78 = f32[1536,128]{1,0:T(8,128)} custom-call(f32[1536,128]{1,0:T(8,128)S(1)} %bitcast.5, s32[512,128]{1,0:T(8,128)S(1)} %get-tuple-element.15.level, f32[512,128]{1,0:T(8,128)S(1)} %get-tuple-element.16.frac), custom_call_target="tpu_custom_call" | custom-call | tf_op jit(solution)/shard_map/pallas_call | solution.py:401
  64.4 5.0 %all-to-all-done = f32[16,96,128]{2,1,0:T(8,128)S(1)} async-done(((f32[16,96,128]{2,1,0:T(8,128)}), f32[16,96,128]{2,1,0:T(8,128)S(1)}, u32[]{:S(2)}, u32[]{:S(2)}) %all-to-all-start) | async-done | bytes 786464 | tf_op jit(solution)/shard_map/all_to_all | solution.py:427
  69.5 3.6 %all-to-all-start.3 = ((f32[16,96,128]{2,1,0:T(8,128)}), f32[16,96,128]{2,1,0:T(8,128)S(1)}, u32[]{:S(2)}, u32[]{:S(2)}) async-start(f32[16,96,128]{2,1,0:T(8,128)} %bitcast.4), calls=%async_computation.3 | async-start | bytes 1572864 | tf_op jit(solution)/shard_map/all_to_all | solution.py:427
  73.1 3.4 %shard_map.76 = f32[1536,128]{1,0:T(8,128)} custom-call(f32[1536,128]{1,0:T(8,128)S(1)} %bitcast.6, s32[512,128]{1,0:T(8,128)S(1)} %get-tuple-element.13.level, f32[512,128]{1,0:T(8,128)S(1)} %get-tuple-element.14.frac), custom_call_target="tpu_custom_call" | custom-call | tf_op jit(solution)/shard_map/pallas_call | solution.py:401
  76.5 17.5 %all-to-all-done.3.data = f32[16,96,128]{2,1,0:T(8,128)S(1)} async-done(((f32[16,96,128]{2,1,0:T(8,128)}), f32[16,96,128]{2,1,0:T(8,128)S(1)}, u32[]{:S(2)}, u32[]{:S(2)}) %all-to-all-start.3) | async-done | bytes 786464 | tf_op jit(solution)/shard_map/all_to_all | solution.py:427
  94.0 3.6 %all-to-all-start.1 = ((f32[16,96,128]{2,1,0:T(8,128)}), f32[16,96,128]{2,1,0:T(8,128)S(1)}, u32[]{:S(2)}, u32[]{:S(2)}) async-start(f32[16,96,128]{2,1,0:T(8,128)} %bitcast.2), calls=%async_computation.1 | async-start | bytes 1572864 | tf_op jit(solution)/shard_map/all_to_all | solution.py:427
  97.6 2.0 %shard_map.79.refs_0_ = f32[10,16,2,1152]{3,2,1,0:T(2,128)} custom-call(f32[16,96,128]{2,1,0:T(8,128)S(1)} %all-to-all-done.3.data), custom_call_target="tpu_custom_call" | custom-call | tf_op jit(solution)/shard_map/pallas_call | solution.py:412
  99.5 19.9 %all-to-all-done.1.data = f32[16,96,128]{2,1,0:T(8,128)S(1)} async-done(((f32[16,96,128]{2,1,0:T(8,128)}), f32[16,96,128]{2,1,0:T(8,128)S(1)}, u32[]{:S(2)}, u32[]{:S(2)}) %all-to-all-start.1) | async-done | bytes 786464 | tf_op jit(solution)/shard_map/all_to_all | solution.py:427
  119.4 1.9 %shard_map.80 = f32[10,16,2,1152]{3,2,1,0:T(2,128)} custom-call(f32[16,96,128]{2,1,0:T(8,128)S(1)} %all-to-all-done.1.data, f32[10,16,2,1152]{3,2,1,0:T(2,128)} %shard_map.79.refs_0_), custom_call_target="tpu_custom_call", output_to_operand_aliasing={{}: (1, {})} | custom-call | tf_op jit(solution)/shard_map/pallas_call | solution.py:412
Async XLA Ops:
  1.9 0.9 copy-start.3
  9.2 8.5 %copy-start.5 = (f32[11,2,2,1152]{3,2,1,0:T(2,128)S(1)}, f32[11,2,2,1152]{3,2,1,0:T(2,128)}, u32[]{:S(2)}) copy-start(f32[11,2,2,1152]{3,2,1,0:T(2,128)} %get-tuple-element.11) | copy-start | bytes 608260
  9.2 15.4 %copy-start.4 = (f32[11,2,2,1152]{3,2,1,0:T(2,128)S(1)}, f32[11,2,2,1152]{3,2,1,0:T(2,128)}, u32[]{:S(2)}) copy-start(f32[11,2,2,1152]{3,2,1,0:T(2,128)} %get-tuple-element.12.refs_4_) | copy-start | bytes 608260
  9.2 35.2 %all-to-all-start.2 = ((f32[16,96,128]{2,1,0:T(8,128)}), f32[16,96,128]{2,1,0:T(8,128)S(1)}, u32[]{:S(2)}, u32[]{:S(2)}) async-start(f32[16,96,128]{2,1,0:T(8,128)} %shard_map.77), calls=%async_computation.2 | async-start | bytes 1572864 | tf_op jit(solution)/shard_map/all_to_all | solution.py:427
  17.8 15.5 %collective-permute-start = (f32[11,2,2,1152]{3,2,1,0:T(2,128)S(1)}, f32[11,2,2,1152]{3,2,1,0:T(2,128)S(1)}, u32[]{:S(2)}, u32[]{:S(2)}) collective-permute-start(f32[11,2,2,1152]{3,2,1,0:T(2,128)S(1)} %copy-done.5), channel_id=1, source_target_pairs={{0,16},{16,32},{32,48},{48,64},{64,80},{80,96},{96,112},{112,128},... | collective-permute-start | bytes 608264 | tf_op jit(solution)/shard_map/ppermute | solution.py:441
  24.6 13.3 %collective-permute-start.1 = (f32[11,2,2,1152]{3,2,1,0:T(2,128)S(1)}, f32[11,2,2,1152]{3,2,1,0:T(2,128)S(1)}, u32[]{:S(2)}, u32[]{:S(2)}) collective-permute-start(f32[11,2,2,1152]{3,2,1,0:T(2,128)S(1)} %copy-done.4), channel_id=1, source_target_pairs={{16,0},{32,16},{48,32},{64,48},{80,64},{96,80},{112,96},{128,112},... | collective-permute-start | bytes 608264 | tf_op jit(solution)/shard_map/ppermute | solution.py:442
  44.4 8.5 %copy-start = (s32[31,16,72]{2,1,0:T(8,128)S(1)}, s32[31,16,72]{2,1,0:T(8,128)}, u32[]{:S(2)}) copy-start(s32[31,16,72]{2,1,0:T(8,128)} %index.1) | copy-start | bytes 428548
  44.4 8.5 %copy-start.1 = (s32[31,16,72]{2,1,0:T(8,128)S(1)}, s32[31,16,72]{2,1,0:T(8,128)}, u32[]{:S(2)}) copy-start(s32[31,16,72]{2,1,0:T(8,128)} %offset.1) | copy-start | bytes 428548
  44.4 8.5 %copy-start.2 = (f32[31,16,72]{2,1,0:T(8,128)S(1)}, f32[31,16,72]{2,1,0:T(8,128)}, u32[]{:S(2)}) copy-start(f32[31,16,72]{2,1,0:T(8,128)} %phase.1) | copy-start | bytes 428548
  44.4 25.1 %all-to-all-start = ((f32[16,96,128]{2,1,0:T(8,128)}), f32[16,96,128]{2,1,0:T(8,128)S(1)}, u32[]{:S(2)}, u32[]{:S(2)}) async-start(f32[16,96,128]{2,1,0:T(8,128)} %shard_map.74), calls=%async_computation | async-start | bytes 1572864 | tf_op jit(solution)/shard_map/all_to_all | solution.py:427
  69.5 24.5 %all-to-all-start.3 = ((f32[16,96,128]{2,1,0:T(8,128)}), f32[16,96,128]{2,1,0:T(8,128)S(1)}, u32[]{:S(2)}, u32[]{:S(2)}) async-start(f32[16,96,128]{2,1,0:T(8,128)} %bitcast.4), calls=%async_computation.3 | async-start | bytes 1572864 | tf_op jit(solution)/shard_map/all_to_all | solution.py:427
  94.0 25.4 %all-to-all-start.1 = ((f32[16,96,128]{2,1,0:T(8,128)}), f32[16,96,128]{2,1,0:T(8,128)S(1)}, u32[]{:S(2)}, u32[]{:S(2)}) async-start(f32[16,96,128]{2,1,0:T(8,128)} %bitcast.2), calls=%async_computation.1 | async-start | bytes 1572864 | tf_op jit(solution)/shard_map/all_to_all | solution.py:427

commit v4 on v3

--- a/solution.py
+++ b/solution.py
@@ -80,9 +80,13 @@
 
 def transport_kernel(part, *refs):
     if part == OUTER:
-        lat, tracers, thickness, courant_x, courant_y, low, high, out, held, mx, ax, my, ay, fy, sem = refs
+        where, tracers, thickness, courant_x, courant_y, low, high, _, out, held, mx, ax, my, ay, fy, sem = refs
     else:
         tracers, thickness, courant_x, courant_y, _, out, held, mx, ax, my, ay, fy, sem = refs
+    chunk = list(range(GROUPS))
+    if part == OUTER:
+        y, z = where[1] >> 2, where[1] & 3
+        chunk = [4 * ((g & 3) ^ z) + (((g >> 2) - y) & 3) for g in range(GROUPS)]
     slots = slots_of(part)
     lane, row = lane_index(), row_index()
     view = held.reshape(NTR + 3, slots // part, part, TILES, LEVS, LANES)
@@ -137,7 +141,7 @@
             mx[place(l, c), :], ax[place(l, c), :] = factors(rows_of(EAST, 0, c, l), west[c], thick[c])
             courant = rows_of(NORTH, 0, c, l)
             if part == OUTER:
-                courant = jnp.where((row > 0) | (lat[0] > 0), courant, 0.0)
+                courant = jnp.where((row > 0) | (where[0] > 0), courant, 0.0)
             my[place(l, c), :], ay[place(l, c), :] = factors(courant, rows_of(THICK, -1, c, l), thick[c])
     past_mass, past_tilt = factors(past(NORTH, 0), past(THICK, -1), past(THICK, 0))
 
@@ -210,9 +214,10 @@
             a = jnp.where(lane < LANES - o, a, turn(first[l][t + 1], -o, 1))
             lon = jnp.where(lane >= CHUNK, lane - CHUNK, lane + (LANES - CHUNK))
             b = jnp.where(lon < LANES - o, b, turn(second[l][t + 1], CHUNK - o, 1))
-        out[g, pl.ds(at, 8), :] = jnp.where(lane < CHUNK, a, b)
+        out[chunk[g], pl.ds(at, 8), :] = jnp.where(lane < CHUNK, a, b)
         moved = pltpu.roll(b, slot * 16, 1)
-        out[g, pl.ds(block, 8), :] = jnp.where((lane >> 4) == slot, moved, out[g, pl.ds(block, 8), :])
+        last = pl.ds(block, 8)
+        out[chunk[g], last, :] = jnp.where((lane >> 4) == slot, moved, out[chunk[g], last, :])
 
     lax.fori_loop(0, PAIRS - 1, two, 0)
     first, second = tracer(NTR - 1), air()
@@ -221,35 +226,34 @@
             pack(g, l, ((PAIRS - 1) * LEVS + l) * 8, REST + 8, l * 4, first, second)
 
 
-def target_kernel(index, offset, phase, *tables):
-    lane, row = lane_index(), row_index()
+def target_kernel(index, offset, phase, inner, outer):
+    lane = lane_index()
     blank = jnp.zeros((8, LANES - CHUNK), F32)
-
-    def rows_of(ref, n, part):
-        if part == INNER:
-            found = ref[n, pl.ds(4, 8), :]
-            return jnp.concatenate([found, blank.astype(found.dtype)], 1)
-        low, high = (jnp.concatenate([x, blank.astype(x.dtype)], 1) for x in (ref[n, pl.ds(0, 8), :], ref[n, pl.ds(8, 8), :]))
-        return jnp.where((row & 1) == 0, pick(low, row >> 1), pick(high, 4 + (row >> 1)))
-
-    for ref in tables:
-        ref[pl.ds(0, 16), :] = jnp.zeros((16, LANES), ref.dtype)
+    for ref in (inner, outer):
+        ref[pl.ds(0, 16), :] = jnp.zeros((16, LANES), F32)
     for n in range(2 * GROUPS - 1):
-        for part in (INNER, OUTER):
-            level, frac = tables[2 * part - 2 : 2 * part]
-            s = rows_of(index, n, part)
-            f = (rows_of(offset, n, part).astype(F32) + rows_of(phase, n, part)) * (1.0 / 32.0)
-            for out, x in ((level, s), (frac, f)):
-                moved = turn(x, CHUNK, 1)
-                tail = jnp.where(lane < 16, moved, jnp.zeros_like(moved))
-                tail = tail + turn(tail, 16, 1)
-                tail = tail + turn(tail, 32, 1)
-                other = turn(turn(tail, 64, 1), 4, 0)
-                out[pl.ds((n + 1) * 16, 8), :] = jnp.where(lane < CHUNK, x, moved)
-                out[pl.ds((n + 1) * 16 + 8, 8), :] = jnp.where(lane < 64, tail, other)
-
-
-def remap_kernel(data, level, frac, out):
+        at = (n + 1) * 16
+        main, tail = [], []
+        for h in range(2):
+            rows = pl.ds(8 * h, 8)
+            part = (offset[n, rows, :].astype(F32) + phase[n, rows, :]) * (1.0 / 32.0)
+            x = jnp.concatenate([index[n, rows, :].astype(F32) + part, blank], 1)
+            moved = turn(x, CHUNK, 1)
+            main.append(jnp.where(lane < CHUNK, x, moved))
+            last = jnp.where(lane < 16, moved, 0.0)
+            last = last + turn(last, 16, 1)
+            tail.append(last + turn(last, 32, 1))
+        other = [turn(x, 64, 1) for x in tail]
+        inner[pl.ds(at, 4), :] = main[0][4:]
+        inner[pl.ds(at + 4, 4), :] = main[1][:4]
+        inner[pl.ds(at + 8, 8), :] = turn(tail[0], 4, 0) + other[1]
+        outer[pl.ds(at, 4, stride=2), :] = main[0][:4]
+        outer[pl.ds(at + 1, 4, stride=2), :] = main[1][4:]
+        outer[pl.ds(at + 8, 2, stride=2), :] = (tail[0] + turn(other[0], -2, 0))[:2]
+        outer[pl.ds(at + 9, 2, stride=2), :] = (tail[1] + turn(other[1], -2, 0))[4:6]
+
+
+def remap_rows(data, table, out):
     lane, row = lane_index(), row_index()
 
     def targets(tile):
@@ -257,8 +261,9 @@
         for parity in range(2):
             for half in range(2):
                 start = (parity + 16 * half) * 16 + tile
-                s = level[pl.ds(start, 8, stride=32), :]
-                f = frac[pl.ds(start, 8, stride=32), :]
+                position = table[pl.ds(start, 8, stride=32), :]
+                s = jnp.minimum(position.astype(jnp.int32), 2 * GROUPS - 1)
+                f = position - s.astype(F32)
                 square = f * f * 0.5
                 cubic = 3.0 * square - f * f * f
                 found.append(((s >> 1) & 7, s >= 16, (s & 1) == 1, f, square, cubic))
@@ -326,8 +331,48 @@
     lax.fori_loop(0, 4, tail, 0)
 
 
-def collect_kernel(part, data, *refs):
-    out, flat, sem = refs[-3:]
+def places_of(where):
+    y, z = where[1] >> 2, where[1] & 3
+    return [[((y - j) & 3) * 4 + (z ^ k) for k in range(4)] for j in range(4)]
+
+
+def gather_chunks(where, sources, target, sem):
+    copies = []
+    for j, found in enumerate(places_of(where)):
+        for k, place in enumerate(found):
+            copies.append(pltpu.make_async_copy(sources[j][k], target(place), sem.at[4 * j + k]))
+    for copy in copies:
+        copy.start()
+    for copy in copies:
+        copy.wait()
+
+
+def remap_outer_kernel(where, *refs):
+    given, (table, out, data, new, sem) = refs[:4], refs[4:]
+
+    def rows(place):
+        return pl.ds(pl.multiple_of(place * DEPTH, 8), DEPTH)
+
+    gather_chunks(where, [[given[j].at[k] for k in range(4)] for j in range(4)], lambda p: data.at[rows(p)], sem)
+    remap_rows(data, table, new)
+    y, z = where[1] >> 2, where[1] & 3
+    copies = []
+    for j in range(4):
+        for k in range(4):
+            place = ((y + j) & 3) * 4 + (z ^ k)
+            copies.append(pltpu.make_async_copy(new.at[rows(place)], out.at[4 * j + k], sem.at[4 * j + k]))
+    for copy in copies:
+        copy.start()
+    for copy in copies:
+        copy.wait()
+
+
+def collect_kernel(part, *refs):
+    if part == INNER:
+        data, out, flat, sem = refs
+    else:
+        where, given, (_, out, data, flat, sem) = refs[0], refs[1:5], refs[5:]
+        gather_chunks(where, [[given[k].at[j] for k in range(4)] for j in range(4)], lambda p: data.at[p], sem)
     lane = lane_index()
 
     def unpack(pair, at, block, slot):
@@ -370,6 +415,7 @@
 
 
 ANYWHERE = pl.BlockSpec(memory_space=pl.ANY)
+IN_SMEM = pl.BlockSpec(memory_space=pltpu.SMEM)
 IN_HBM = pl.BlockSpec(memory_space=pltpu.HBM)
 IN_VMEM = pl.BlockSpec(memory_space=pltpu.VMEM)
 PARAMS = pltpu.CompilerParams(vmem_limit_bytes=VMEM_LIMIT)
@@ -377,7 +423,7 @@
 
 def transport(part, *given):
     factor = pltpu.VMEM((STEP * 8, LANES), F32)
-    scalars = [pl.BlockSpec(memory_space=pltpu.SMEM)] if part == OUTER else []
+    scalars = [IN_SMEM] if part == OUTER else []
     others = [ANYWHERE] * (len(given) - len(scalars) - 4)
     return pl.pallas_call(
         functools.partial(transport_kernel, part),
@@ -397,28 +443,39 @@
     )(*given)
 
 
-def remap(data, level, frac):
+def remap_inner(data, table):
     return pl.pallas_call(
-        remap_kernel,
+        remap_rows,
         out_shape=jax.ShapeDtypeStruct((GROUPS * DEPTH, LANES), F32),
-        in_specs=[IN_VMEM] * 3,
+        in_specs=[IN_VMEM] * 2,
         out_specs=IN_VMEM,
         compiler_params=PARAMS,
-    )(data.reshape(GROUPS * DEPTH, LANES), level, frac).reshape(GROUPS, DEPTH, LANES)
-
-
-def collect(part, data, result):
-    given = (data,) if result is None else (data, result)
+    )(data.reshape(GROUPS * DEPTH, LANES), table).reshape(GROUPS, DEPTH, LANES)
+
+
+def remap_outer(where, given, table):
+    held = pltpu.VMEM((GROUPS * DEPTH, LANES), F32)
+    return pl.pallas_call(
+        remap_outer_kernel,
+        out_shape=jax.ShapeDtypeStruct((GROUPS, DEPTH, LANES), F32),
+        in_specs=[IN_SMEM] + [ANYWHERE] * 4 + [IN_VMEM],
+        out_specs=ANYWHERE,
+        scratch_shapes=[held, held, pltpu.SemaphoreType.DMA((GROUPS,))],
+        compiler_params=PARAMS,
+    )(where, *given, table)
+
+
+def collect(part, *given):
+    scratch = [pltpu.VMEM((FIELDS * 8 * STEP, LANES), F32), pltpu.SemaphoreType.DMA((2 * TILES,))]
+    if part == OUTER:
+        scratch = [pltpu.VMEM((GROUPS, DEPTH, LANES), F32)] + scratch
     return pl.pallas_call(
         functools.partial(collect_kernel, part),
         out_shape=jax.ShapeDtypeStruct((FIELDS, ROWS, LEVS, LONS), F32),
-        in_specs=[IN_VMEM, ANYWHERE][: len(given)],
+        in_specs=[IN_VMEM] if part == INNER else [IN_SMEM] + [ANYWHERE] * 5,
         out_specs=ANYWHERE,
-        scratch_shapes=[
-            pltpu.VMEM((FIELDS * 8 * STEP, LANES), F32),
-            pltpu.SemaphoreType.DMA((2 * TILES,)),
-        ],
-        input_output_aliases={} if result is None else {1: 0},
+        scratch_shapes=scratch,
+        input_output_aliases={} if part == INNER else {5: 0},
         compiler_params=PARAMS,
     )(*given)
 
@@ -427,8 +484,35 @@
     return lax.all_to_all(data, "lev", split_axis=0, concat_axis=0, tiled=True)
 
 
+def over_z(data, k):
+    return lax.ppermute(data, "lev", [(i, i ^ k) for i in range(GROUPS)])
+
+
+def over_y(data, j):
+    return lax.ppermute(data, "lev", [(i, (i + 4 * j) % GROUPS) for i in range(GROUPS)])
+
+
+def exchange_out(data):
+    part = [data[4 * k : 4 * k + 4] for k in range(4)]
+    for k in (2, 3, 1):
+        part[k] = over_z(part[k], k)
+    turned = [jnp.stack([part[k][j] for k in range(4)]) for j in range(4)]
+    return [turned[0]] + [over_y(turned[j], j) for j in range(1, 4)]
+
+
+def exchange_back(data):
+    part = [data[4 * j : 4 * j + 4] for j in range(4)]
+    for j in range(1, 4):
+        part[j] = over_y(part[j], j)
+    turned = [jnp.stack([part[j][k] for j in range(4)]) for k in range(4)]
+    for k in (2, 3, 1):
+        turned[k] = over_z(turned[k], k)
+    return turned
+
+
 def shards(tracers, thickness, courant_x, courant_y, level_index, level_offset, level_phase):
     own = [pltpu.with_memory_space_constraint(x, pltpu.HBM) for x in (tracers, thickness, courant_x, courant_y)]
+    where = jnp.stack([lax.axis_index("lat"), lax.axis_index("lev")]).astype(jnp.int32)
     rim = jax.ShapeDtypeStruct((NTR + 2, 2, LEVS, LONS), F32)
     south, north = pl.pallas_call(
         halo_kernel,
@@ -441,20 +525,18 @@
     low = lax.ppermute(north, "lat", [(i, i + 1) for i in range(count - 1)])
     high = lax.ppermute(south, "lat", [(i + 1, i) for i in range(count - 1)])
     inner = exchange(transport(INNER, *own, south))
-    lat = lax.axis_index("lat").astype(jnp.int32).reshape(1)
-    outer = exchange(transport(OUTER, lat, *own, low, high))
-    table = (2 * GROUPS * 16, LANES)
-    tables = (jax.ShapeDtypeStruct(table, jnp.int32), jax.ShapeDtypeStruct(table, F32))
-    places = pl.pallas_call(
+    table = jax.ShapeDtypeStruct((2 * GROUPS * 16, LANES), F32)
+    inner_table, outer_table = pl.pallas_call(
         target_kernel,
-        out_shape=tables + tables,
+        out_shape=(table, table),
         in_specs=[IN_VMEM] * 3,
-        out_specs=(IN_VMEM,) * 4,
+        out_specs=(IN_VMEM, IN_VMEM),
         compiler_params=PARAMS,
     )(level_index, level_offset, level_phase)
-    inner = exchange(remap(inner, *places[:2]))
-    outer = exchange(remap(outer, *places[2:]))
-    return collect(OUTER, outer, collect(INNER, inner, None))
+    outer = exchange_out(transport(OUTER, where, *own, low, high, outer_table))
+    inner = exchange(remap_inner(inner, inner_table))
+    outer = exchange_back(remap_outer(where, outer, outer_table))
+    return collect(OUTER, where, *outer, collect(INNER, inner))
 
 
 def solution(mesh):

time: 123 us -> 133 us (1.081)
  the two profiles are of different devices: /device:TPU:7 before, /device:TPU:38 now
where the time goes in v4:
time: 133 us; the launch traced here: 132 us
  waiting for transfers between devices  59 us (44%)
  starting transfers between devices  42.6 us (32%)
  Pallas kernels  29.3 us (22%)
    ppermute x6, waiting for transfers between devices, over_z(): return lax.ppermute(data, 'lev', [(i, i ^ k) for i in range(GROUPS)])  36.8 us
    ppermute x6, waiting for transfers between devices, over_y(): lax.ppermute(data, 'lev', [(i, (i + 4 * j) % GROUPS) for i in range(GROUP...  22.2 us
    all_to_all x2, starting transfers between devices, exchange(): return lax.all_to_all(data, 'lev', split_axis=0, concat_axis=0, tiled=True)  17 us
    pallas_call x2, Pallas kernels, transport(): pl.pallas_call(functools.partial(transport_kernel, part), out_shape=jax.S...  12.6 us
    ppermute x6, starting transfers between devices, over_y(): lax.ppermute(data, 'lev', [(i, (i + 4 * j) % GROUPS) for i in range(GROUP...  11.9 us
    ppermute x6, starting transfers between devices, over_z(): return lax.ppermute(data, 'lev', [(i, i ^ k) for i in range(GROUPS)])  8.21 us
    pallas_call x1, Pallas kernels, remap_outer(): pl.pallas_call(remap_outer_kernel, out_shape=jax.ShapeDtypeStruct((GROUPS...  5.57 us
    pallas_call x2, Pallas kernels, collect(): pl.pallas_call(functools.partial(collect_kernel, part), out_shape=jax.Sha...  5.5 us
  transfers between devices with their start and end apart: 16, of which 10 were waited for; matrix products, arithmetic and copies ran while one was open for 0% of the time, Pallas kernels for 16%

profile of v4, /device:TPU:38, one launch (start us, length us, event | category | flops | bytes accessed | tf_op | source)
XLA Modules:
  0.0 132.5 jit_solution(4493687878514171414)
XLA Ops:
  0.0 1.8 %shard_map.73 = (f32[11,2,2,1152]{3,2,1,0:T(2,128)}, f32[11,2,2,1152]{3,2,1,0:T(2,128)}) custom-call(f32[9,16,2,1152]{3,2,1,0:T(2,128)} %refs_0_.1, f32[16,2,1152]{2,1,0:T(2,128)} %refs_1_.3, f32[16,2,1152]{2,1,0:T(2,128)} %refs_3_.3), custom_call_target="tpu_custom_call" | custom-call | tf_op jit(solution)/shard_map/pallas_call | solution.py:517
  1.8 1.9 %collective-permute-start = (f32[11,2,2,1152]{3,2,1,0:T(2,128)}, f32[11,2,2,1152]{3,2,1,0:T(2,128)S(1)}, u32[]{:S(2)}, u32[]{:S(2)}) collective-permute-start(f32[11,2,2,1152]{3,2,1,0:T(2,128)} %get-tuple-element.9), channel_id=1, source_target_pairs={{0,16},{16,32},{32,48},{48,64},{64,80},{80,96},{96,112},{112,128},... | collective-permute-start | bytes 608264 | tf_op jit(solution)/shard_map/ppermute | solution.py:525
  3.8 3.6 %collective-permute-start.1 = (f32[11,2,2,1152]{3,2,1,0:T(2,128)}, f32[11,2,2,1152]{3,2,1,0:T(2,128)S(1)}, u32[]{:S(2)}, u32[]{:S(2)}) collective-permute-start(f32[11,2,2,1152]{3,2,1,0:T(2,128)} %get-tuple-element.10.refs_4_), channel_id=1, source_target_pairs={{16,0},{32,16},{48,32},{64,48},{80,64},{96,80},{112,96},{128,112},... | collective-permute-start | bytes 608264 | tf_op jit(solution)/shard_map/ppermute | solution.py:526
  7.4 0.0 copy-start.3
  7.4 0.9 copy-done.3
  8.4 6.4 %shard_map.77 = f32[16,96,128]{2,1,0:T(8,128)} custom-call(f32[9,16,2,1152]{3,2,1,0:T(2,128)} %refs_0_.1, f32[16,2,1152]{2,1,0:T(2,128)} %refs_1_.3, f32[16,2,1152]{2,1,0:T(2,128)} %refs_2_.3, f32[16,2,1152]{2,1,0:T(2,128)} %refs_3_.3, f32[11,2,2,1152]{3,2,1,0:T(2,128)S(1)} %copy-done.3), custom_call_target="tpu_custom_call" | custom-call | tf_op jit(solution)/shard_map/pallas_call | solution.py:428
  14.8 0.0 copy-start
  14.8 0.0 copy-start.1
  14.8 0.0 copy-start.2
  14.8 8.8 %all-to-all-start = ((f32[16,96,128]{2,1,0:T(8,128)}), f32[16,96,128]{2,1,0:T(8,128)S(1)}, u32[]{:S(2)}, u32[]{:S(2)}) async-start(f32[16,96,128]{2,1,0:T(8,128)} %shard_map.77), calls=%async_computation | async-start | bytes 1572864 | tf_op jit(solution)/shard_map/all_to_all | solution.py:484
  23.6 0.0 copy-done
  23.6 0.0 copy-done.1
  23.6 0.0 copy-done.2
  23.6 0.5 shard_map.74
  24.1 0.1 pad_add_fusion.refs_0_.where
  24.2 0.0 collective-permute-done.refs_5_
  24.2 0.0 collective-permute-done.1.refs_6_
  24.2 6.2 %shard_map.75 = f32[16,96,128]{2,1,0:T(8,128)S(1)} custom-call(s32[2]{0:T(128)S(1)} %pad_add_fusion.refs_0_.where, f32[9,16,2,1152]{3,2,1,0:T(2,128)} %refs_0_.1, f32[16,2,1152]{2,1,0:T(2,128)} %refs_1_.3, f32[16,2,1152]{2,1,0:T(2,128)} %refs_2_.3, f32[16,2,1152]{2,1,0:T(2,128)} %refs_3_.3, f32[11,2,2,1152]{3,2,1,0:T(2,128)S(1)} %collective-permute-done.refs_5_, ...), custom_call_target="tpu_custom_call" | custom-call | tf_op jit(solution)/shard_map/pallas_call | solution.py:428
  30.4 0.2 collective-permute-start.2
  30.6 2.8 %collective-permute-start.4 = (f32[4,96,128]{2,1,0:T(8,128)S(1)}, f32[4,96,128]{2,1,0:T(8,128)S(1)}, u32[]{:S(2)}, u32[]{:S(2)}) collective-permute-start(f32[4,96,128]{2,1,0:T(8,128)S(1)} %get-tuple-element.25), channel_id=1, source_target_pairs={{0,3},{1,2},{2,1},{3,0},{4,7},{5,6},{6,5},{7,4},{8,11},{9,10},{10,... | collective-permute-start | bytes 589832 | tf_op jit(solution)/shard_map/ppermute | solution.py:488
  33.4 1.5 %collective-permute-start.3 = (f32[4,96,128]{2,1,0:T(8,128)S(1)}, f32[4,96,128]{2,1,0:T(8,128)S(1)}, u32[]{:S(2)}, u32[]{:S(2)}) collective-permute-start(f32[4,96,128]{2,1,0:T(8,128)S(1)} %get-tuple-element.26), channel_id=1, source_target_pairs={{0,2},{1,3},{2,0},{3,1},{4,6},{5,7},{6,4},{7,5},{8,10},{9,11},{10,... | collective-permute-start | bytes 589832 | tf_op jit(solution)/shard_map/ppermute | solution.py:488
  34.9 5.7 %collective-permute-done.2 = f32[4,96,128]{2,1,0:T(8,128)S(1)} collective-permute-done((f32[4,96,128]{2,1,0:T(8,128)S(1)}, f32[4,96,128]{2,1,0:T(8,128)S(1)}, u32[]{:S(2)}, u32[]{:S(2)}) %collective-permute-start.2) | collective-permute-done | bytes 196640 | tf_op jit(solution)/shard_map/ppermute | solution.py:488
  40.6 14.7 %collective-permute-done.4 = f32[4,96,128]{2,1,0:T(8,128)S(1)} collective-permute-done((f32[4,96,128]{2,1,0:T(8,128)S(1)}, f32[4,96,128]{2,1,0:T(8,128)S(1)}, u32[]{:S(2)}, u32[]{:S(2)}) %collective-permute-start.4) | collective-permute-done | bytes 196640 | tf_op jit(solution)/shard_map/ppermute | solution.py:488
  55.3 2.3 %collective-permute-done.3 = f32[4,96,128]{2,1,0:T(8,128)S(1)} collective-permute-done((f32[4,96,128]{2,1,0:T(8,128)S(1)}, f32[4,96,128]{2,1,0:T(8,128)S(1)}, u32[]{:S(2)}, u32[]{:S(2)}) %collective-permute-start.3) | collective-permute-done | bytes 196640 | tf_op jit(solution)/shard_map/ppermute | solution.py:488
  57.6 2.5 %collective-permute-start.5 = (f32[4,96,128]{2,1,0:T(8,128)S(1)}, f32[4,96,128]{2,1,0:T(8,128)S(1)}, u32[]{:S(2)}, u32[]{:S(2)}) collective-permute-start(f32[4,96,128]{2,1,0:T(8,128)S(1)} %pad_maximum_fusion.1), channel_id=1, source_target_pairs={{0,4},{1,5},{2,6},{3,7},{4,8},{5,9},{6,10},{7,11},{8,12},{9,13},{1... | collective-permute-start | bytes 589832 | tf_op jit(solution)/shard_map/ppermute | solution.py:492
  60.1 2.8 %collective-permute-start.6 = (f32[4,96,128]{2,1,0:T(8,128)S(1)}, f32[4,96,128]{2,1,0:T(8,128)S(1)}, u32[]{:S(2)}, u32[]{:S(2)}) collective-permute-start(f32[4,96,128]{2,1,0:T(8,128)S(1)} %pad_maximum_fusion.2), channel_id=1, source_target_pairs={{0,8},{1,9},{2,10},{3,11},{4,12},{5,13},{6,14},{7,15},{8,0},{9,1},... | collective-permute-start | bytes 589832 | tf_op jit(solution)/shard_map/ppermute | solution.py:492
  62.9 1.5 %collective-permute-start.7 = (f32[4,96,128]{2,1,0:T(8,128)S(1)}, f32[4,96,128]{2,1,0:T(8,128)S(1)}, u32[]{:S(2)}, u32[]{:S(2)}) collective-permute-start(f32[4,96,128]{2,1,0:T(8,128)S(1)} %pad_maximum_fusion.3), channel_id=1, source_target_pairs={{0,12},{1,13},{2,14},{3,15},{4,0},{5,1},{6,2},{7,3},{8,4},{9,5},{1... | collective-permute-start | bytes 589832 | tf_op jit(solution)/shard_map/ppermute | solution.py:492
  64.5 2.2 %collective-permute-done.5.refs_1_ = f32[4,96,128]{2,1,0:T(8,128)S(1)} collective-permute-done((f32[4,96,128]{2,1,0:T(8,128)S(1)}, f32[4,96,128]{2,1,0:T(8,128)S(1)}, u32[]{:S(2)}, u32[]{:S(2)}) %collective-permute-start.5) | collective-permute-done | bytes 196640 | tf_op jit(solution)/shard_map/ppermute | solution.py:492
  66.7 5.4 %collective-permute-done.6.refs_2_ = f32[4,96,128]{2,1,0:T(8,128)S(1)} collective-permute-done((f32[4,96,128]{2,1,0:T(8,128)S(1)}, f32[4,96,128]{2,1,0:T(8,128)S(1)}, u32[]{:S(2)}, u32[]{:S(2)}) %collective-permute-start.6) | collective-permute-done | bytes 196640 | tf_op jit(solution)/shard_map/ppermute | solution.py:492
  72.1 0.0 collective-permute-done.7.refs_3_
  72.1 5.6 %shard_map.76 = f32[16,96,128]{2,1,0:T(8,128)S(1)} custom-call(s32[2]{0:T(128)S(1)} %pad_add_fusion.refs_0_.where, f32[4,96,128]{2,1,0:T(8,128)S(1)} %pad_maximum_fusion.refs_0_, f32[4,96,128]{2,1,0:T(8,128)S(1)} %collective-permute-done.5.refs_1_, f32[4,96,128]{2,1,0:T(8,128)S(1)} %collective-permute-done.6.refs_2_, ...), custom_call_target="tpu_custom_call" | custom-call | tf_op jit(solution)/shard_map/pallas_call | solution.py:458
  77.7 0.0 all-to-all-done
  77.7 3.3 %shard_map.78 = f32[1536,128]{1,0:T(8,128)} custom-call(f32[1536,128]{1,0:T(8,128)S(1)} %bitcast.4, f32[512,128]{1,0:T(8,128)S(1)} %get-tuple-element.12.table), custom_call_target="tpu_custom_call" | custom-call | tf_op jit(solution)/shard_map/pallas_call | solution.py:447
  81.0 8.2 %all-to-all-start.1 = ((f32[16,96,128]{2,1,0:T(8,128)}), f32[16,96,128]{2,1,0:T(8,128)S(1)}, u32[]{:S(2)}, u32[]{:S(2)}) async-start(f32[16,96,128]{2,1,0:T(8,128)} %bitcast.3), calls=%async_computation.1 | async-start | bytes 1572864 | tf_op jit(solution)/shard_map/all_to_all | solution.py:484
  89.2 1.5 %collective-permute-start.8 = (f32[4,96,128]{2,1,0:T(8,128)S(1)}, f32[4,96,128]{2,1,0:T(8,128)S(1)}, u32[]{:S(2)}, u32[]{:S(2)}) collective-permute-start(f32[4,96,128]{2,1,0:T(8,128)S(1)} %get-tuple-element.17), channel_id=1, source_target_pairs={{0,4},{1,5},{2,6},{3,7},{4,8},{5,9},{6,10},{7,11},{8,12},{9,13},{1... | collective-permute-start | bytes 589832 | tf_op jit(solution)/shard_map/ppermute | solution.py:492
  90.7 1.8 %collective-permute-start.10 = (f32[4,96,128]{2,1,0:T(8,128)S(1)}, f32[4,96,128]{2,1,0:T(8,128)S(1)}, u32[]{:S(2)}, u32[]{:S(2)}) collective-permute-start(f32[4,96,128]{2,1,0:T(8,128)S(1)} %get-tuple-element.18), channel_id=1, source_target_pairs={{0,12},{1,13},{2,14},{3,15},{4,0},{5,1},{6,2},{7,3},{8,4},{9,5},{1... | collective-permute-start | bytes 589832 | tf_op jit(solution)/shard_map/ppermute | solution.py:492
  92.5 1.8 %collective-permute-start.9 = (f32[4,96,128]{2,1,0:T(8,128)S(1)}, f32[4,96,128]{2,1,0:T(8,128)S(1)}, u32[]{:S(2)}, u32[]{:S(2)}) collective-permute-start(f32[4,96,128]{2,1,0:T(8,128)S(1)} %get-tuple-element.19), channel_id=1, source_target_pairs={{0,8},{1,9},{2,10},{3,11},{4,12},{5,13},{6,14},{7,15},{8,0},{9,1},... | collective-permute-start | bytes 589832 | tf_op jit(solution)/shard_map/ppermute | solution.py:492
  94.3 10.4 %collective-permute-done.8 = f32[4,96,128]{2,1,0:T(8,128)S(1)} collective-permute-done((f32[4,96,128]{2,1,0:T(8,128)S(1)}, f32[4,96,128]{2,1,0:T(8,128)S(1)}, u32[]{:S(2)}, u32[]{:S(2)}) %collective-permute-start.8) | collective-permute-done | bytes 196640 | tf_op jit(solution)/shard_map/ppermute | solution.py:492
  104.7 0.0 collective-permute-done.10
  104.8 4.1 %collective-permute-done.9 = f32[4,96,128]{2,1,0:T(8,128)S(1)} collective-permute-done((f32[4,96,128]{2,1,0:T(8,128)S(1)}, f32[4,96,128]{2,1,0:T(8,128)S(1)}, u32[]{:S(2)}, u32[]{:S(2)}) %collective-permute-start.9) | collective-permute-done | bytes 196640 | tf_op jit(solution)/shard_map/ppermute | solution.py:492
  108.9 0.1 collective-permute-start.11
  109.1 3.0 %collective-permute-start.12 = (f32[4,96,128]{2,1,0:T(8,128)S(1)}, f32[4,96,128]{2,1,0:T(8,128)S(1)}, u32[]{:S(2)}, u32[]{:S(2)}) collective-permute-start(f32[4,96,128]{2,1,0:T(8,128)S(1)} %pad_maximum_fusion.6), channel_id=1, source_target_pairs={{0,2},{1,3},{2,0},{3,1},{4,6},{5,7},{6,4},{7,5},{8,10},{9,11},{10,... | collective-permute-start | bytes 589832 | tf_op jit(solution)/shard_map/ppermute | solution.py:488
  112.1 0.7 collective-permute-start.13
  112.7 0.0 all-to-all-done.1.refs_0_
  112.7 2.0 %shard_map.79.refs_5_ = f32[10,16,2,1152]{3,2,1,0:T(2,128)} custom-call(f32[16,96,128]{2,1,0:T(8,128)S(1)} %all-to-all-done.1.refs_0_), custom_call_target="tpu_custom_call" | custom-call | tf_op jit(solution)/shard_map/pallas_call | solution.py:472
  114.7 1.5 %collective-permute-done.11.refs_2_ = f32[4,96,128]{2,1,0:T(8,128)S(1)} collective-permute-done((f32[4,96,128]{2,1,0:T(8,128)S(1)}, f32[4,96,128]{2,1,0:T(8,128)S(1)}, u32[]{:S(2)}, u32[]{:S(2)}) %collective-permute-start.11) | collective-permute-done | bytes 196640 | tf_op jit(solution)/shard_map/ppermute | solution.py:488
  116.2 9.1 %collective-permute-done.12.refs_3_ = f32[4,96,128]{2,1,0:T(8,128)S(1)} collective-permute-done((f32[4,96,128]{2,1,0:T(8,128)S(1)}, f32[4,96,128]{2,1,0:T(8,128)S(1)}, u32[]{:S(2)}, u32[]{:S(2)}) %collective-permute-start.12) | collective-permute-done | bytes 196640 | tf_op jit(solution)/shard_map/ppermute | solution.py:488
  125.3 3.6 %collective-permute-done.13.refs_4_ = f32[4,96,128]{2,1,0:T(8,128)S(1)} collective-permute-done((f32[4,96,128]{2,1,0:T(8,128)S(1)}, f32[4,96,128]{2,1,0:T(8,128)S(1)}, u32[]{:S(2)}, u32[]{:S(2)}) %collective-permute-start.13) | collective-permute-done | bytes 196640 | tf_op jit(solution)/shard_map/ppermute | solution.py:488
  128.9 3.5 %shard_map.80 = f32[10,16,2,1152]{3,2,1,0:T(2,128)} custom-call(s32[2]{0:T(128)S(1)} %pad_add_fusion.refs_0_.where, f32[4,96,128]{2,1,0:T(8,128)S(1)} %pad_maximum_fusion.4.refs_1_, f32[4,96,128]{2,1,0:T(8,128)S(1)} %collective-permute-done.11.refs_2_, f32[4,96,128]{2,1,0:T(8,128)S(1)} %collective-permute-done.12.refs_3_, ...), custom_call_target="tpu_custom_call", output_to_operand_aliasing={{}: (5, {})} | custom-call | tf_op jit(solution)/shard_map/pallas_call | solution.py:472
  (18 shorter events, 0.3 us)
Async XLA Ops:
  1.8 22.3 %collective-permute-start = (f32[11,2,2,1152]{3,2,1,0:T(2,128)}, f32[11,2,2,1152]{3,2,1,0:T(2,128)S(1)}, u32[]{:S(2)}, u32[]{:S(2)}) collective-permute-start(f32[11,2,2,1152]{3,2,1,0:T(2,128)} %get-tuple-element.9), channel_id=1, source_target_pairs={{0,16},{16,32},{32,48},{48,64},{64,80},{80,96},{96,112},{112,128},... | collective-permute-start | bytes 608264 | tf_op jit(solution)/shard_map/ppermute | solution.py:525
  3.8 20.4 %collective-permute-start.1 = (f32[11,2,2,1152]{3,2,1,0:T(2,128)}, f32[11,2,2,1152]{3,2,1,0:T(2,128)S(1)}, u32[]{:S(2)}, u32[]{:S(2)}) collective-permute-start(f32[11,2,2,1152]{3,2,1,0:T(2,128)} %get-tuple-element.10.refs_4_), channel_id=1, source_target_pairs={{16,0},{32,16},{48,32},{64,48},{80,64},{96,80},{112,96},{128,112},... | collective-permute-start | bytes 608264 | tf_op jit(solution)/shard_map/ppermute | solution.py:526
  7.4 0.9 copy-start.3
  14.8 8.8 %copy-start = (s32[31,16,72]{2,1,0:T(8,128)S(1)}, s32[31,16,72]{2,1,0:T(8,128)}, u32[]{:S(2)}) copy-start(s32[31,16,72]{2,1,0:T(8,128)} %index.1) | copy-start | bytes 428548
  14.8 8.8 %copy-start.1 = (s32[31,16,72]{2,1,0:T(8,128)S(1)}, s32[31,16,72]{2,1,0:T(8,128)}, u32[]{:S(2)}) copy-start(s32[31,16,72]{2,1,0:T(8,128)} %offset.1) | copy-start | bytes 428548
  14.8 8.8 %copy-start.2 = (f32[31,16,72]{2,1,0:T(8,128)S(1)}, f32[31,16,72]{2,1,0:T(8,128)}, u32[]{:S(2)}) copy-start(f32[31,16,72]{2,1,0:T(8,128)} %phase.1) | copy-start | bytes 428548
  14.8 62.9 %all-to-all-start = ((f32[16,96,128]{2,1,0:T(8,128)}), f32[16,96,128]{2,1,0:T(8,128)S(1)}, u32[]{:S(2)}, u32[]{:S(2)}) async-start(f32[16,96,128]{2,1,0:T(8,128)} %shard_map.77), calls=%async_computation | async-start | bytes 1572864 | tf_op jit(solution)/shard_map/all_to_all | solution.py:484
  30.4 10.1 %collective-permute-start.2 = (f32[4,96,128]{2,1,0:T(8,128)S(1)}, f32[4,96,128]{2,1,0:T(8,128)S(1)}, u32[]{:S(2)}, u32[]{:S(2)}) collective-permute-start(f32[4,96,128]{2,1,0:T(8,128)S(1)} %get-tuple-element.24), channel_id=1, source_target_pairs={{0,1},{1,0},{2,3},{3,2},{4,5},{5,4},{6,7},{7,6},{8,9},{9,8},{10,11... | collective-permute-start | bytes 589832 | tf_op jit(solution)/shard_map/ppermute | solution.py:488
  30.6 24.6 %collective-permute-start.4 = (f32[4,96,128]{2,1,0:T(8,128)S(1)}, f32[4,96,128]{2,1,0:T(8,128)S(1)}, u32[]{:S(2)}, u32[]{:S(2)}) collective-permute-start(f32[4,96,128]{2,1,0:T(8,128)S(1)} %get-tuple-element.25), channel_id=1, source_target_pairs={{0,3},{1,2},{2,1},{3,0},{4,7},{5,6},{6,5},{7,4},{8,11},{9,10},{10,... | collective-permute-start | bytes 589832 | tf_op jit(solution)/shard_map/ppermute | solution.py:488
  33.4 24.1 %collective-permute-start.3 = (f32[4,96,128]{2,1,0:T(8,128)S(1)}, f32[4,96,128]{2,1,0:T(8,128)S(1)}, u32[]{:S(2)}, u32[]{:S(2)}) collective-permute-start(f32[4,96,128]{2,1,0:T(8,128)S(1)} %get-tuple-element.26), channel_id=1, source_target_pairs={{0,2},{1,3},{2,0},{3,1},{4,6},{5,7},{6,4},{7,5},{8,10},{9,11},{10,... | collective-permute-start | bytes 589832 | tf_op jit(solution)/shard_map/ppermute | solution.py:488
  57.6 9.1 %collective-permute-start.5 = (f32[4,96,128]{2,1,0:T(8,128)S(1)}, f32[4,96,128]{2,1,0:T(8,128)S(1)}, u32[]{:S(2)}, u32[]{:S(2)}) collective-permute-start(f32[4,96,128]{2,1,0:T(8,128)S(1)} %pad_maximum_fusion.1), channel_id=1, source_target_pairs={{0,4},{1,5},{2,6},{3,7},{4,8},{5,9},{6,10},{7,11},{8,12},{9,13},{1... | collective-permute-start | bytes 589832 | tf_op jit(solution)/shard_map/ppermute | solution.py:492
  60.1 12.0 %collective-permute-start.6 = (f32[4,96,128]{2,1,0:T(8,128)S(1)}, f32[4,96,128]{2,1,0:T(8,128)S(1)}, u32[]{:S(2)}, u32[]{:S(2)}) collective-permute-start(f32[4,96,128]{2,1,0:T(8,128)S(1)} %pad_maximum_fusion.2), channel_id=1, source_target_pairs={{0,8},{1,9},{2,10},{3,11},{4,12},{5,13},{6,14},{7,15},{8,0},{9,1},... | collective-permute-start | bytes 589832 | tf_op jit(solution)/shard_map/ppermute | solution.py:492
  62.9 9.2 %collective-permute-start.7 = (f32[4,96,128]{2,1,0:T(8,128)S(1)}, f32[4,96,128]{2,1,0:T(8,128)S(1)}, u32[]{:S(2)}, u32[]{:S(2)}) collective-permute-start(f32[4,96,128]{2,1,0:T(8,128)S(1)} %pad_maximum_fusion.3), channel_id=1, source_target_pairs={{0,12},{1,13},{2,14},{3,15},{4,0},{5,1},{6,2},{7,3},{8,4},{9,5},{1... | collective-permute-start | bytes 589832 | tf_op jit(solution)/shard_map/ppermute | solution.py:492
  81.0 31.7 %all-to-all-start.1 = ((f32[16,96,128]{2,1,0:T(8,128)}), f32[16,96,128]{2,1,0:T(8,128)S(1)}, u32[]{:S(2)}, u32[]{:S(2)}) async-start(f32[16,96,128]{2,1,0:T(8,128)} %bitcast.3), calls=%async_computation.1 | async-start | bytes 1572864 | tf_op jit(solution)/shard_map/all_to_all | solution.py:484
  89.2 15.5 %collective-permute-start.8 = (f32[4,96,128]{2,1,0:T(8,128)S(1)}, f32[4,96,128]{2,1,0:T(8,128)S(1)}, u32[]{:S(2)}, u32[]{:S(2)}) collective-permute-start(f32[4,96,128]{2,1,0:T(8,128)S(1)} %get-tuple-element.17), channel_id=1, source_target_pairs={{0,4},{1,5},{2,6},{3,7},{4,8},{5,9},{6,10},{7,11},{8,12},{9,13},{1... | collective-permute-start | bytes 589832 | tf_op jit(solution)/shard_map/ppermute | solution.py:492
  90.7 14.0 %collective-permute-start.10 = (f32[4,96,128]{2,1,0:T(8,128)S(1)}, f32[4,96,128]{2,1,0:T(8,128)S(1)}, u32[]{:S(2)}, u32[]{:S(2)}) collective-permute-start(f32[4,96,128]{2,1,0:T(8,128)S(1)} %get-tuple-element.18), channel_id=1, source_target_pairs={{0,12},{1,13},{2,14},{3,15},{4,0},{5,1},{6,2},{7,3},{8,4},{9,5},{1... | collective-permute-start | bytes 589832 | tf_op jit(solution)/shard_map/ppermute | solution.py:492
  92.5 16.4 %collective-permute-start.9 = (f32[4,96,128]{2,1,0:T(8,128)S(1)}, f32[4,96,128]{2,1,0:T(8,128)S(1)}, u32[]{:S(2)}, u32[]{:S(2)}) collective-permute-start(f32[4,96,128]{2,1,0:T(8,128)S(1)} %get-tuple-element.19), channel_id=1, source_target_pairs={{0,8},{1,9},{2,10},{3,11},{4,12},{5,13},{6,14},{7,15},{8,0},{9,1},... | collective-permute-start | bytes 589832 | tf_op jit(solution)/shard_map/ppermute | solution.py:492
  108.9 7.3 %collective-permute-start.11 = (f32[4,96,128]{2,1,0:T(8,128)S(1)}, f32[4,96,128]{2,1,0:T(8,128)S(1)}, u32[]{:S(2)}, u32[]{:S(2)}) collective-permute-start(f32[4,96,128]{2,1,0:T(8,128)S(1)} %pad_maximum_fusion.5), channel_id=1, source_target_pairs={{0,1},{1,0},{2,3},{3,2},{4,5},{5,4},{6,7},{7,6},{8,9},{9,8},{10,11... | collective-permute-start | bytes 589832 | tf_op jit(solution)/shard_map/ppermute | solution.py:488
  109.1 16.3 %collective-permute-start.12 = (f32[4,96,128]{2,1,0:T(8,128)S(1)}, f32[4,96,128]{2,1,0:T(8,128)S(1)}, u32[]{:S(2)}, u32[]{:S(2)}) collective-permute-start(f32[4,96,128]{2,1,0:T(8,128)S(1)} %pad_maximum_fusion.6), channel_id=1, source_target_pairs={{0,2},{1,3},{2,0},{3,1},{4,6},{5,7},{6,4},{7,5},{8,10},{9,11},{10,... | collective-permute-start | bytes 589832 | tf_op jit(solution)/shard_map/ppermute | solution.py:488
  112.1 16.9 %collective-permute-start.13 = (f32[4,96,128]{2,1,0:T(8,128)S(1)}, f32[4,96,128]{2,1,0:T(8,128)S(1)}, u32[]{:S(2)}, u32[]{:S(2)}) collective-permute-start(f32[4,96,128]{2,1,0:T(8,128)S(1)} %pad_maximum_fusion.7), channel_id=1, source_target_pairs={{0,3},{1,2},{2,1},{3,0},{4,7},{5,6},{6,5},{7,4},{8,11},{9,10},{10,... | collective-permute-start | bytes 589832 | tf_op jit(solution)/shard_map/ppermute | solution.py:488

commit v5 on v4

--- a/solution.py
+++ b/solution.py
@@ -80,13 +80,10 @@
 
 def transport_kernel(part, *refs):
     if part == OUTER:
-        where, tracers, thickness, courant_x, courant_y, low, high, _, out, held, mx, ax, my, ay, fy, sem = refs
+        tracers, thickness, courant_x, courant_y, low, high, _, out, held, mx, ax, my, ay, fy, sem = refs
     else:
         tracers, thickness, courant_x, courant_y, _, out, held, mx, ax, my, ay, fy, sem = refs
-    chunk = list(range(GROUPS))
-    if part == OUTER:
-        y, z = where[1] >> 2, where[1] & 3
-        chunk = [4 * ((g & 3) ^ z) + (((g >> 2) - y) & 3) for g in range(GROUPS)]
+    chunk = slots_to()
     slots = slots_of(part)
     lane, row = lane_index(), row_index()
     view = held.reshape(NTR + 3, slots // part, part, TILES, LEVS, LANES)
@@ -141,7 +138,7 @@
             mx[place(l, c), :], ax[place(l, c), :] = factors(rows_of(EAST, 0, c, l), west[c], thick[c])
             courant = rows_of(NORTH, 0, c, l)
             if part == OUTER:
-                courant = jnp.where((row > 0) | (where[0] > 0), courant, 0.0)
+                courant = jnp.where((row > 0) | (lax.axis_index("lat") > 0), courant, 0.0)
             my[place(l, c), :], ay[place(l, c), :] = factors(courant, rows_of(THICK, -1, c, l), thick[c])
     past_mass, past_tilt = factors(past(NORTH, 0), past(THICK, -1), past(THICK, 0))
 
@@ -331,36 +328,45 @@
     lax.fori_loop(0, 4, tail, 0)
 
 
-def places_of(where):
-    y, z = where[1] >> 2, where[1] & 3
-    return [[((y - j) & 3) * 4 + (z ^ k) for k in range(4)] for j in range(4)]
-
-
-def gather_chunks(where, sources, target, sem):
+def place_of():
+    lev = lax.axis_index("lev")
+    return lev >> 2, lev & 3, (lax.axis_index("lat") & 1) == 1
+
+
+def slots_to():
+    y, z, odd = place_of()
+    slots = []
+    for g in range(GROUPS):
+        j, k = ((g >> 2) - y) & 3, (g & 3) ^ z
+        slots.append(jnp.where(odd, 4 * j + k, 4 * k + j))
+    return slots
+
+
+def gather_chunks(given, target, sem):
+    y, z, odd = place_of()
     copies = []
-    for j, found in enumerate(places_of(where)):
-        for k, place in enumerate(found):
-            copies.append(pltpu.make_async_copy(sources[j][k], target(place), sem.at[4 * j + k]))
+    for a in range(4):
+        for b in range(4):
+            j, k = jnp.where(odd, a, b), jnp.where(odd, b, a)
+            place = ((y - j) & 3) * 4 + (z ^ k)
+            copies.append(pltpu.make_async_copy(given[b].at[a], target(place), sem.at[4 * a + b]))
     for copy in copies:
         copy.start()
     for copy in copies:
         copy.wait()
 
 
-def remap_outer_kernel(where, *refs):
+def remap_kernel(*refs):
     given, (table, out, data, new, sem) = refs[:4], refs[4:]
 
     def rows(place):
         return pl.ds(pl.multiple_of(place * DEPTH, 8), DEPTH)
 
-    gather_chunks(where, [[given[j].at[k] for k in range(4)] for j in range(4)], lambda p: data.at[rows(p)], sem)
+    gather_chunks(given, lambda place: data.at[rows(place)], sem)
     remap_rows(data, table, new)
-    y, z = where[1] >> 2, where[1] & 3
     copies = []
-    for j in range(4):
-        for k in range(4):
-            place = ((y + j) & 3) * 4 + (z ^ k)
-            copies.append(pltpu.make_async_copy(new.at[rows(place)], out.at[4 * j + k], sem.at[4 * j + k]))
+    for g, slot in enumerate(slots_to()):
+        copies.append(pltpu.make_async_copy(new.at[rows(g)], out.at[slot], sem.at[g]))
     for copy in copies:
         copy.start()
     for copy in copies:
@@ -368,11 +374,8 @@
 
 
 def collect_kernel(part, *refs):
-    if part == INNER:
-        data, out, flat, sem = refs
-    else:
-        where, given, (_, out, data, flat, sem) = refs[0], refs[1:5], refs[5:]
-        gather_chunks(where, [[given[k].at[j] for k in range(4)] for j in range(4)], lambda p: data.at[p], sem)
+    given, (out, data, flat, sem) = refs[:4], refs[-4:]
+    gather_chunks(given, lambda place: data.at[place], sem)
     lane = lane_index()
 
     def unpack(pair, at, block, slot):
@@ -415,7 +418,6 @@
 
 
 ANYWHERE = pl.BlockSpec(memory_space=pl.ANY)
-IN_SMEM = pl.BlockSpec(memory_space=pltpu.SMEM)
 IN_HBM = pl.BlockSpec(memory_space=pltpu.HBM)
 IN_VMEM = pl.BlockSpec(memory_space=pltpu.VMEM)
 PARAMS = pltpu.CompilerParams(vmem_limit_bytes=VMEM_LIMIT)
@@ -423,12 +425,10 @@
 
 def transport(part, *given):
     factor = pltpu.VMEM((STEP * 8, LANES), F32)
-    scalars = [IN_SMEM] if part == OUTER else []
-    others = [ANYWHERE] * (len(given) - len(scalars) - 4)
     return pl.pallas_call(
         functools.partial(transport_kernel, part),
         out_shape=jax.ShapeDtypeStruct((GROUPS, DEPTH, LANES), F32),
-        in_specs=scalars + [IN_HBM] * 4 + others,
+        in_specs=[IN_HBM] * 4 + [ANYWHERE] * (len(given) - 4),
         out_specs=IN_VMEM,
         scratch_shapes=[
             pltpu.VMEM(((NTR + 3) * slots_of(part) * STEP, LANES), F32),
@@ -443,76 +443,62 @@
     )(*given)
 
 
-def remap_inner(data, table):
-    return pl.pallas_call(
-        remap_rows,
-        out_shape=jax.ShapeDtypeStruct((GROUPS * DEPTH, LANES), F32),
-        in_specs=[IN_VMEM] * 2,
-        out_specs=IN_VMEM,
-        compiler_params=PARAMS,
-    )(data.reshape(GROUPS * DEPTH, LANES), table).reshape(GROUPS, DEPTH, LANES)
-
-
-def remap_outer(where, given, table):
+def remap(given, table):
     held = pltpu.VMEM((GROUPS * DEPTH, LANES), F32)
     return pl.pallas_call(
-        remap_outer_kernel,
+        remap_kernel,
         out_shape=jax.ShapeDtypeStruct((GROUPS, DEPTH, LANES), F32),
-        in_specs=[IN_SMEM] + [ANYWHERE] * 4 + [IN_VMEM],
+        in_specs=[ANYWHERE] * 4 + [IN_VMEM],
         out_specs=ANYWHERE,
         scratch_shapes=[held, held, pltpu.SemaphoreType.DMA((GROUPS,))],
         compiler_params=PARAMS,
-    )(where, *given, table)
-
-
-def collect(part, *given):
-    scratch = [pltpu.VMEM((FIELDS * 8 * STEP, LANES), F32), pltpu.SemaphoreType.DMA((2 * TILES,))]
-    if part == OUTER:
-        scratch = [pltpu.VMEM((GROUPS, DEPTH, LANES), F32)] + scratch
+    )(*given, table)
+
+
+def collect(part, given, *result):
     return pl.pallas_call(
         functools.partial(collect_kernel, part),
         out_shape=jax.ShapeDtypeStruct((FIELDS, ROWS, LEVS, LONS), F32),
-        in_specs=[IN_VMEM] if part == INNER else [IN_SMEM] + [ANYWHERE] * 5,
+        in_specs=[ANYWHERE] * (4 + len(result)),
         out_specs=ANYWHERE,
-        scratch_shapes=scratch,
-        input_output_aliases={} if part == INNER else {5: 0},
+        scratch_shapes=[
+            pltpu.VMEM((GROUPS, DEPTH, LANES), F32),
+            pltpu.VMEM((FIELDS * 8 * STEP, LANES), F32),
+            pltpu.SemaphoreType.DMA((2 * TILES,)),
+        ],
+        input_output_aliases={4: 0} if result else {},
         compiler_params=PARAMS,
-    )(*given)
-
-
-def exchange(data):
-    return lax.all_to_all(data, "lev", split_axis=0, concat_axis=0, tiled=True)
-
-
-def over_z(data, k):
-    return lax.ppermute(data, "lev", [(i, i ^ k) for i in range(GROUPS)])
-
-
-def over_y(data, j):
-    return lax.ppermute(data, "lev", [(i, (i + 4 * j) % GROUPS) for i in range(GROUPS)])
-
-
-def exchange_out(data):
-    part = [data[4 * k : 4 * k + 4] for k in range(4)]
-    for k in (2, 3, 1):
-        part[k] = over_z(part[k], k)
-    turned = [jnp.stack([part[k][j] for k in range(4)]) for j in range(4)]
-    return [turned[0]] + [over_y(turned[j], j) for j in range(1, 4)]
-
-
-def exchange_back(data):
-    part = [data[4 * j : 4 * j + 4] for j in range(4)]
-    for j in range(1, 4):
-        part[j] = over_y(part[j], j)
-    turned = [jnp.stack([part[j][k] for j in range(4)]) for k in range(4)]
-    for k in (2, 3, 1):
-        turned[k] = over_z(turned[k], k)
-    return turned
+    )(*given, *result)
+
+
+def hop(blocks, first):
+    lats = lax.axis_size("lat")
+    moved = {}
+    for a in (2, 3, 1):
+        pairs = []
+        for lat in range(lats):
+            along_z = (lat % 2 == 0) == first
+            for lev in range(GROUPS):
+                target = lev ^ a if along_z else (lev + 4 * a) % GROUPS
+                pairs.append((lat * GROUPS + lev, lat * GROUPS + target))
+        moved[a] = lax.ppermute(blocks[a], ("lat", "lev"), pairs)
+    return [blocks[0]] + [moved[a] for a in range(1, 4)]
+
+
+def first_hop(data):
+    return hop([data[4 * a : 4 * a + 4] for a in range(4)], True)
+
+
+def second_hop(rows):
+    return hop([jnp.stack([rows[a][b] for a in range(4)]) for b in range(4)], False)
+
+
+def after(values, *others):
+    return lax.optimization_barrier((values, others))[0]
 
 
 def shards(tracers, thickness, courant_x, courant_y, level_index, level_offset, level_phase):
     own = [pltpu.with_memory_space_constraint(x, pltpu.HBM) for x in (tracers, thickness, courant_x, courant_y)]
-    where = jnp.stack([lax.axis_index("lat"), lax.axis_index("lev")]).astype(jnp.int32)
     rim = jax.ShapeDtypeStruct((NTR + 2, 2, LEVS, LONS), F32)
     south, north = pl.pallas_call(
         halo_kernel,
@@ -524,7 +510,7 @@
     count = lax.axis_size("lat")
     low = lax.ppermute(north, "lat", [(i, i + 1) for i in range(count - 1)])
     high = lax.ppermute(south, "lat", [(i + 1, i) for i in range(count - 1)])
-    inner = exchange(transport(INNER, *own, south))
+    inner = transport(INNER, *own, south)
     table = jax.ShapeDtypeStruct((2 * GROUPS * 16, LANES), F32)
     inner_table, outer_table = pl.pallas_call(
         target_kernel,
@@ -533,10 +519,16 @@
         out_specs=(IN_VMEM, IN_VMEM),
         compiler_params=PARAMS,
     )(level_index, level_offset, level_phase)
-    outer = exchange_out(transport(OUTER, where, *own, low, high, outer_table))
-    inner = exchange(remap_inner(inner, inner_table))
-    outer = exchange_back(remap_outer(where, outer, outer_table))
-    return collect(OUTER, where, *outer, collect(INNER, inner))
+    outer = transport(OUTER, *own, low, high, outer_table)
+    inner = first_hop(inner)
+    inner, outer = second_hop(after(inner, outer)), first_hop(outer)
+    outer = second_hop(outer)
+    inner = remap(inner, inner_table)
+    outer = remap(after(outer, inner), outer_table)
+    inner = first_hop(inner)
+    inner, outer = second_hop(after(inner, outer)), first_hop(outer)
+    outer = second_hop(outer)
+    return collect(OUTER, outer, collect(INNER, inner))
 
 
 def solution(mesh):

time: 133 us -> 118 us (0.89)
  the two profiles are of different devices: /device:TPU:38 before, /device:TPU:14 now
where the time goes in v5:
time: 118 us; the launch traced here: 117 us
  starting transfers between devices  43.9 us (37%)
  waiting for transfers between devices  41.9 us (36%)
  Pallas kernels  29.2 us (25%)
  local copies, waits for them, and re-layouts  1.37 us (1%)
    ppermute x24, waiting for transfers between devices, hop(): moved[a] = lax.ppermute(blocks[a], ('lat', 'lev'), pairs)  41.9 us
    ppermute x24, starting transfers between devices, hop(): moved[a] = lax.ppermute(blocks[a], ('lat', 'lev'), pairs)  38.4 us
    pallas_call x2, Pallas kernels, transport(): pl.pallas_call(functools.partial(transport_kernel, part), out_shape=jax.S...  11.3 us
    pallas_call x2, Pallas kernels, remap(): pl.pallas_call(remap_kernel, out_shape=jax.ShapeDtypeStruct((GROUPS, DEPT...  9.5 us
    pallas_call x2, Pallas kernels, collect(): pl.pallas_call(functools.partial(collect_kernel, part), out_shape=jax.Sha...  6.16 us
    ppermute x1, starting transfers between devices, shards(): high = lax.ppermute(south, 'lat', [(i + 1, i) for i in range(count - 1)])  3.64 us
  transfers between devices with their start and end apart: 26, of which 9 were waited for; matrix products, arithmetic and copies ran while one was open for 1% of the time, Pallas kernels for 21%

profile of v5, /device:TPU:14, one launch (start us, length us, event | category | flops | bytes accessed | tf_op | source)
XLA Modules:
  0.0 117.3 jit_solution(17367045059454933655)
XLA Ops:
  0.0 1.8 %shard_map.73 = (f32[11,2,2,1152]{3,2,1,0:T(2,128)}, f32[11,2,2,1152]{3,2,1,0:T(2,128)}) custom-call(f32[9,16,2,1152]{3,2,1,0:T(2,128)} %refs_0_.3, f32[16,2,1152]{2,1,0:T(2,128)} %refs_1_.3, f32[16,2,1152]{2,1,0:T(2,128)} %refs_3_.3), custom_call_target="tpu_custom_call" | custom-call | tf_op jit(solution)/shard_map/pallas_call | solution.py:503
  1.8 1.9 %collective-permute-start = (f32[11,2,2,1152]{3,2,1,0:T(2,128)}, f32[11,2,2,1152]{3,2,1,0:T(2,128)S(1)}, u32[]{:S(2)}, u32[]{:S(2)}) collective-permute-start(f32[11,2,2,1152]{3,2,1,0:T(2,128)} %get-tuple-element.21), channel_id=1, source_target_pairs={{0,16},{16,32},{32,48},{48,64},{64,80},{80,96},{96,112},{112,128},... | collective-permute-start | bytes 608264 | tf_op jit(solution)/shard_map/ppermute | solution.py:511
  3.8 3.6 %collective-permute-start.1 = (f32[11,2,2,1152]{3,2,1,0:T(2,128)}, f32[11,2,2,1152]{3,2,1,0:T(2,128)S(1)}, u32[]{:S(2)}, u32[]{:S(2)}) collective-permute-start(f32[11,2,2,1152]{3,2,1,0:T(2,128)} %get-tuple-element.22.refs_4_), channel_id=1, source_target_pairs={{16,0},{32,16},{48,32},{64,48},{80,64},{96,80},{112,96},{128,112},... | collective-permute-start | bytes 608264 | tf_op jit(solution)/shard_map/ppermute | solution.py:512
  7.4 0.0 copy-start.3
  7.4 0.9 copy-done.3
  8.4 5.6 %shard_map.76 = f32[16,96,128]{2,1,0:T(8,128)S(1)} custom-call(f32[9,16,2,1152]{3,2,1,0:T(2,128)} %refs_0_.3, f32[16,2,1152]{2,1,0:T(2,128)} %refs_1_.3, f32[16,2,1152]{2,1,0:T(2,128)} %refs_2_.3, f32[16,2,1152]{2,1,0:T(2,128)} %refs_3_.3, f32[11,2,2,1152]{3,2,1,0:T(2,128)S(1)} %copy-done.3), custom_call_target="tpu_custom_call" | custom-call | tf_op jit(solution)/shard_map/pallas_call | solution.py:428
  14.0 0.0 copy-start
  14.0 0.0 copy-start.1
  14.0 0.0 copy-start.2
  14.0 0.1 fusion.3
  14.1 4.7 %collective-permute-start.10 = (f32[4,96,128]{2,1,0:T(8,128)S(1)}, f32[4,96,128]{2,1,0:T(8,128)S(1)}, u32[]{:S(2)}, u32[]{:S(2)}) collective-permute-start(f32[4,96,128]{2,1,0:T(8,128)S(1)} %get-tuple-element.48), channel_id=1, source_target_pairs={{0,3},{1,2},{2,1},{3,0},{4,7},{5,6},{6,5},{7,4},{8,11},{9,10},{10,... | collective-permute-start | bytes 589832 | tf_op jit(solution)/shard_map/ppermute | solution.py:484
  18.8 0.0 collective-permute-start.9
  18.8 0.7 collective-permute-start.8
  19.4 0.5 shard_map.74
  19.9 0.0 collective-permute-done.refs_4_
  19.9 0.0 collective-permute-done.1.refs_5_
  19.9 5.7 %shard_map.75 = f32[16,96,128]{2,1,0:T(8,128)S(1)} custom-call(f32[9,16,2,1152]{3,2,1,0:T(2,128)} %refs_0_.3, f32[16,2,1152]{2,1,0:T(2,128)} %refs_1_.3, f32[16,2,1152]{2,1,0:T(2,128)} %refs_2_.3, f32[16,2,1152]{2,1,0:T(2,128)} %refs_3_.3, f32[11,2,2,1152]{3,2,1,0:T(2,128)S(1)} %collective-permute-done.refs_4_, ...), custom_call_target="tpu_custom_call" | custom-call | tf_op jit(solution)/shard_map/pallas_call | solution.py:428
  25.7 0.0 collective-permute-done.10
  25.7 1.8 %collective-permute-done.9 = f32[4,96,128]{2,1,0:T(8,128)S(1)} collective-permute-done((f32[4,96,128]{2,1,0:T(8,128)S(1)}, f32[4,96,128]{2,1,0:T(8,128)S(1)}, u32[]{:S(2)}, u32[]{:S(2)}) %collective-permute-start.9) | collective-permute-done | bytes 196640 | tf_op jit(solution)/shard_map/ppermute | solution.py:484
  27.5 0.0 collective-permute-done.8
  27.6 1.7 %collective-permute-start.11 = (f32[4,96,128]{2,1,0:T(8,128)S(1)}, f32[4,96,128]{2,1,0:T(8,128)S(1)}, u32[]{:S(2)}, u32[]{:S(2)}) collective-permute-start(f32[4,96,128]{2,1,0:T(8,128)S(1)} %pad_maximum_fusion.5), channel_id=1, source_target_pairs={{0,4},{1,5},{2,6},{3,7},{4,8},{5,9},{6,10},{7,11},{8,12},{9,13},{1... | collective-permute-start | bytes 589832 | tf_op jit(solution)/shard_map/ppermute | solution.py:484
  29.3 1.0 collective-permute-start.12
  30.3 2.5 %collective-permute-start.13 = (f32[4,96,128]{2,1,0:T(8,128)S(1)}, f32[4,96,128]{2,1,0:T(8,128)S(1)}, u32[]{:S(2)}, u32[]{:S(2)}) collective-permute-start(f32[4,96,128]{2,1,0:T(8,128)S(1)} %pad_maximum_fusion.7), channel_id=1, source_target_pairs={{0,12},{1,13},{2,14},{3,15},{4,0},{5,1},{6,2},{7,3},{8,4},{9,5},{1... | collective-permute-start | bytes 589832 | tf_op jit(solution)/shard_map/ppermute | solution.py:484
  32.8 1.2 %collective-permute-start.2 = (f32[4,96,128]{2,1,0:T(8,128)S(1)}, f32[4,96,128]{2,1,0:T(8,128)S(1)}, u32[]{:S(2)}, u32[]{:S(2)}) collective-permute-start(f32[4,96,128]{2,1,0:T(8,128)S(1)} %get-tuple-element.56), channel_id=1, source_target_pairs={{0,1},{1,0},{2,3},{3,2},{4,5},{5,4},{6,7},{7,6},{8,9},{9,8},{10,11... | collective-permute-start | bytes 589832 | tf_op jit(solution)/shard_map/ppermute | solution.py:484
  34.0 1.6 %collective-permute-start.4 = (f32[4,96,128]{2,1,0:T(8,128)S(1)}, f32[4,96,128]{2,1,0:T(8,128)S(1)}, u32[]{:S(2)}, u32[]{:S(2)}) collective-permute-start(f32[4,96,128]{2,1,0:T(8,128)S(1)} %get-tuple-element.57), channel_id=1, source_target_pairs={{0,3},{1,2},{2,1},{3,0},{4,7},{5,6},{6,5},{7,4},{8,11},{9,10},{10,... | collective-permute-start | bytes 589832 | tf_op jit(solution)/shard_map/ppermute | solution.py:484
  35.7 4.9 %collective-permute-done.2 = f32[4,96,128]{2,1,0:T(8,128)S(1)} collective-permute-done((f32[4,96,128]{2,1,0:T(8,128)S(1)}, f32[4,96,128]{2,1,0:T(8,128)S(1)}, u32[]{:S(2)}, u32[]{:S(2)}) %collective-permute-start.2) | collective-permute-done | bytes 196640 | tf_op jit(solution)/shard_map/ppermute | solution.py:484
  40.5 1.4 %collective-permute-start.3 = (f32[4,96,128]{2,1,0:T(8,128)S(1)}, f32[4,96,128]{2,1,0:T(8,128)S(1)}, u32[]{:S(2)}, u32[]{:S(2)}) collective-permute-start(f32[4,96,128]{2,1,0:T(8,128)S(1)} %get-tuple-element.58), channel_id=1, source_target_pairs={{0,2},{1,3},{2,0},{3,1},{4,6},{5,7},{6,4},{7,5},{8,10},{9,11},{10,... | collective-permute-start | bytes 589832 | tf_op jit(solution)/shard_map/ppermute | solution.py:484
  42.0 3.7 %collective-permute-done.4 = f32[4,96,128]{2,1,0:T(8,128)S(1)} collective-permute-done((f32[4,96,128]{2,1,0:T(8,128)S(1)}, f32[4,96,128]{2,1,0:T(8,128)S(1)}, u32[]{:S(2)}, u32[]{:S(2)}) %collective-permute-start.4) | collective-permute-done | bytes 196640 | tf_op jit(solution)/shard_map/ppermute | solution.py:484
  45.7 13.2 %collective-permute-done.3 = f32[4,96,128]{2,1,0:T(8,128)S(1)} collective-permute-done((f32[4,96,128]{2,1,0:T(8,128)S(1)}, f32[4,96,128]{2,1,0:T(8,128)S(1)}, u32[]{:S(2)}, u32[]{:S(2)}) %collective-permute-start.3) | collective-permute-done | bytes 196640 | tf_op jit(solution)/shard_map/ppermute | solution.py:484
  58.9 0.1 collective-permute-start.5
  59.1 3.2 %collective-permute-start.6 = (f32[4,96,128]{2,1,0:T(8,128)S(1)}, f32[4,96,128]{2,1,0:T(8,128)S(1)}, u32[]{:S(2)}, u32[]{:S(2)}) collective-permute-start(f32[4,96,128]{2,1,0:T(8,128)S(1)} %pad_maximum_fusion.2), channel_id=1, source_target_pairs={{0,8},{1,9},{2,10},{3,11},{4,12},{5,13},{6,14},{7,15},{8,0},{9,1},... | collective-permute-start | bytes 589832 | tf_op jit(solution)/shard_map/ppermute | solution.py:484
  62.3 0.0 collective-permute-done.11.refs_1_
  62.3 0.3 collective-permute-start.7
  62.6 0.0 collective-permute-done.12.refs_2_
  62.6 0.0 collective-permute-done.13.refs_3_
  62.6 4.8 %shard_map.77 = f32[16,96,128]{2,1,0:T(8,128)S(1)} custom-call(f32[4,96,128]{2,1,0:T(8,128)S(1)} %pad_maximum_fusion.4.refs_0_, f32[4,96,128]{2,1,0:T(8,128)S(1)} %collective-permute-done.11.refs_1_, f32[4,96,128]{2,1,0:T(8,128)S(1)} %collective-permute-done.12.refs_2_, f32[4,96,128]{2,1,0:T(8,128)S(1)} %collective-permute-done.13.refs_3_, ...), custom_call_target="tpu_custom_call" | custom-call | tf_op jit(solution)/shard_map/pallas_call | solution.py:448
  67.4 0.1 fusion
  67.4 2.5 %collective-permute-start.22 = (f32[4,96,128]{2,1,0:T(8,128)S(1)}, f32[4,96,128]{2,1,0:T(8,128)S(1)}, u32[]{:S(2)}, u32[]{:S(2)}) collective-permute-start(f32[4,96,128]{2,1,0:T(8,128)S(1)} %get-tuple-element.37), channel_id=1, source_target_pairs={{0,3},{1,2},{2,1},{3,0},{4,7},{5,6},{6,5},{7,4},{8,11},{9,10},{10,... | collective-permute-start | bytes 589832 | tf_op jit(solution)/shard_map/ppermute | solution.py:484
  69.9 0.0 collective-permute-start.21
  70.0 2.1 %collective-permute-start.20 = (f32[4,96,128]{2,1,0:T(8,128)S(1)}, f32[4,96,128]{2,1,0:T(8,128)S(1)}, u32[]{:S(2)}, u32[]{:S(2)}) collective-permute-start(f32[4,96,128]{2,1,0:T(8,128)S(1)} %get-tuple-element.39), channel_id=1, source_target_pairs={{0,1},{1,0},{2,3},{3,2},{4,5},{5,4},{6,7},{7,6},{8,9},{9,8},{10,11... | collective-permute-start | bytes 589832 | tf_op jit(solution)/shard_map/ppermute | solution.py:484
  72.0 0.0 collective-permute-done.6.refs_2_
  72.0 0.0 collective-permute-done.7.refs_3_
  72.0 4.7 %shard_map.78 = f32[16,96,128]{2,1,0:T(8,128)S(1)} custom-call(f32[4,96,128]{2,1,0:T(8,128)S(1)} %pad_maximum_fusion.refs_0_, f32[4,96,128]{2,1,0:T(8,128)S(1)} %collective-permute-done.5.refs_1_, f32[4,96,128]{2,1,0:T(8,128)S(1)} %collective-permute-done.6.refs_2_, f32[4,96,128]{2,1,0:T(8,128)S(1)} %collective-permute-done.7.refs_3_, ...), custom_call_target="tpu_custom_call" | custom-call | tf_op jit(solution)/shard_map/pallas_call | solution.py:448
  76.8 0.2 collective-permute-start.14
  77.0 2.4 %collective-permute-start.16 = (f32[4,96,128]{2,1,0:T(8,128)S(1)}, f32[4,96,128]{2,1,0:T(8,128)S(1)}, u32[]{:S(2)}, u32[]{:S(2)}) collective-permute-start(f32[4,96,128]{2,1,0:T(8,128)S(1)} %get-tuple-element.46), channel_id=1, source_target_pairs={{0,3},{1,2},{2,1},{3,0},{4,7},{5,6},{6,5},{7,4},{8,11},{9,10},{10,... | collective-permute-start | bytes 589832 | tf_op jit(solution)/shard_map/ppermute | solution.py:484
  79.4 0.0 collective-permute-done.22
  79.4 1.0 collective-permute-start.15
  80.4 0.0 collective-permute-done.21
  80.4 1.9 %collective-permute-done.20 = f32[4,96,128]{2,1,0:T(8,128)S(1)} collective-permute-done((f32[4,96,128]{2,1,0:T(8,128)S(1)}, f32[4,96,128]{2,1,0:T(8,128)S(1)}, u32[]{:S(2)}, u32[]{:S(2)}) %collective-permute-start.20) | collective-permute-done | bytes 196640 | tf_op jit(solution)/shard_map/ppermute | solution.py:484
  82.4 3.0 %collective-permute-start.23 = (f32[4,96,128]{2,1,0:T(8,128)S(1)}, f32[4,96,128]{2,1,0:T(8,128)S(1)}, u32[]{:S(2)}, u32[]{:S(2)}) collective-permute-start(f32[4,96,128]{2,1,0:T(8,128)S(1)} %pad_maximum_fusion.13), channel_id=1, source_target_pairs={{0,4},{1,5},{2,6},{3,7},{4,8},{5,9},{6,10},{7,11},{8,12},{9,13},{1... | collective-permute-start | bytes 589832 | tf_op jit(solution)/shard_map/ppermute | solution.py:484
  85.5 1.7 %collective-permute-start.24 = (f32[4,96,128]{2,1,0:T(8,128)S(1)}, f32[4,96,128]{2,1,0:T(8,128)S(1)}, u32[]{:S(2)}, u32[]{:S(2)}) collective-permute-start(f32[4,96,128]{2,1,0:T(8,128)S(1)} %pad_maximum_fusion.14), channel_id=1, source_target_pairs={{0,8},{1,9},{2,10},{3,11},{4,12},{5,13},{6,14},{7,15},{8,0},{9,1},... | collective-permute-start | bytes 589832 | tf_op jit(solution)/shard_map/ppermute | solution.py:484
  87.3 3.5 %collective-permute-done.14 = f32[4,96,128]{2,1,0:T(8,128)S(1)} collective-permute-done((f32[4,96,128]{2,1,0:T(8,128)S(1)}, f32[4,96,128]{2,1,0:T(8,128)S(1)}, u32[]{:S(2)}, u32[]{:S(2)}) %collective-permute-start.14) | collective-permute-done | bytes 196640 | tf_op jit(solution)/shard_map/ppermute | solution.py:484
  90.7 2.5 %collective-permute-start.25 = (f32[4,96,128]{2,1,0:T(8,128)S(1)}, f32[4,96,128]{2,1,0:T(8,128)S(1)}, u32[]{:S(2)}, u32[]{:S(2)}) collective-permute-start(f32[4,96,128]{2,1,0:T(8,128)S(1)} %pad_maximum_fusion.15), channel_id=1, source_target_pairs={{0,12},{1,13},{2,14},{3,15},{4,0},{5,1},{6,2},{7,3},{8,4},{9,5},{1... | collective-permute-start | bytes 589832 | tf_op jit(solution)/shard_map/ppermute | solution.py:484
  93.3 9.5 %collective-permute-done.15 = f32[4,96,128]{2,1,0:T(8,128)S(1)} collective-permute-done((f32[4,96,128]{2,1,0:T(8,128)S(1)}, f32[4,96,128]{2,1,0:T(8,128)S(1)}, u32[]{:S(2)}, u32[]{:S(2)}) %collective-permute-start.15) | collective-permute-done | bytes 196640 | tf_op jit(solution)/shard_map/ppermute | solution.py:484
  102.8 1.9 %collective-permute-start.17 = (f32[4,96,128]{2,1,0:T(8,128)S(1)}, f32[4,96,128]{2,1,0:T(8,128)S(1)}, u32[]{:S(2)}, u32[]{:S(2)}) collective-permute-start(f32[4,96,128]{2,1,0:T(8,128)S(1)} %pad_maximum_fusion.9), channel_id=1, source_target_pairs={{0,4},{1,5},{2,6},{3,7},{4,8},{5,9},{6,10},{7,11},{8,12},{9,13},{1... | collective-permute-start | bytes 589832 | tf_op jit(solution)/shard_map/ppermute | solution.py:484
  104.7 1.7 %collective-permute-start.18 = (f32[4,96,128]{2,1,0:T(8,128)S(1)}, f32[4,96,128]{2,1,0:T(8,128)S(1)}, u32[]{:S(2)}, u32[]{:S(2)}) collective-permute-start(f32[4,96,128]{2,1,0:T(8,128)S(1)} %pad_maximum_fusion.10), channel_id=1, source_target_pairs={{0,8},{1,9},{2,10},{3,11},{4,12},{5,13},{6,14},{7,15},{8,0},{9,1},... | collective-permute-start | bytes 589832 | tf_op jit(solution)/shard_map/ppermute | solution.py:484
  106.5 0.0 collective-permute-done.23.refs_1_
  106.5 1.0 collective-permute-start.19
  107.5 0.0 collective-permute-done.25.refs_3_
  107.5 3.1 %shard_map.79.refs_4_ = f32[10,16,2,1152]{3,2,1,0:T(2,128)} custom-call(f32[4,96,128]{2,1,0:T(8,128)S(1)} %pad_maximum_fusion.12.refs_0_, f32[4,96,128]{2,1,0:T(8,128)S(1)} %collective-permute-done.23.refs_1_, f32[4,96,128]{2,1,0:T(8,128)S(1)} %collective-permute-done.24.refs_2_, f32[4,96,128]{2,1,0:T(8,128)S(1)} %collective-permute-done.25.refs_3_), custom_call_target="tpu_custom_call" | custom-call | tf_op jit(solution)/shard_map/pallas_call | solution.py:459
  110.7 0.0 collective-permute-done.17.refs_1_
  110.7 1.4 %collective-permute-done.18.refs_2_ = f32[4,96,128]{2,1,0:T(8,128)S(1)} collective-permute-done((f32[4,96,128]{2,1,0:T(8,128)S(1)}, f32[4,96,128]{2,1,0:T(8,128)S(1)}, u32[]{:S(2)}, u32[]{:S(2)}) %collective-permute-start.18) | collective-permute-done | bytes 196640 | tf_op jit(solution)/shard_map/ppermute | solution.py:484
  112.1 2.0 %collective-permute-done.19.refs_3_ = f32[4,96,128]{2,1,0:T(8,128)S(1)} collective-permute-done((f32[4,96,128]{2,1,0:T(8,128)S(1)}, f32[4,96,128]{2,1,0:T(8,128)S(1)}, u32[]{:S(2)}, u32[]{:S(2)}) %collective-permute-start.19) | collective-permute-done | bytes 196640 | tf_op jit(solution)/shard_map/ppermute | solution.py:484
  114.1 3.0 %shard_map.80 = f32[10,16,2,1152]{3,2,1,0:T(2,128)} custom-call(f32[4,96,128]{2,1,0:T(8,128)S(1)} %pad_maximum_fusion.8.refs_0_, f32[4,96,128]{2,1,0:T(8,128)S(1)} %collective-permute-done.17.refs_1_, f32[4,96,128]{2,1,0:T(8,128)S(1)} %collective-permute-done.18.refs_2_, ...), custom_call_target="tpu_custom_call", output_to_operand_aliasing={{}: (4, {})} | custom-call | tf_op jit(solution)/shard_map/pallas_call | solution.py:459
  (38 shorter events, 0.6 us)
Async XLA Ops:
  1.8 18.1 %collective-permute-start = (f32[11,2,2,1152]{3,2,1,0:T(2,128)}, f32[11,2,2,1152]{3,2,1,0:T(2,128)S(1)}, u32[]{:S(2)}, u32[]{:S(2)}) collective-permute-start(f32[11,2,2,1152]{3,2,1,0:T(2,128)} %get-tuple-element.21), channel_id=1, source_target_pairs={{0,16},{16,32},{32,48},{48,64},{64,80},{80,96},{96,112},{112,128},... | collective-permute-start | bytes 608264 | tf_op jit(solution)/shard_map/ppermute | solution.py:511
  3.8 16.2 %collective-permute-start.1 = (f32[11,2,2,1152]{3,2,1,0:T(2,128)}, f32[11,2,2,1152]{3,2,1,0:T(2,128)S(1)}, u32[]{:S(2)}, u32[]{:S(2)}) collective-permute-start(f32[11,2,2,1152]{3,2,1,0:T(2,128)} %get-tuple-element.22.refs_4_), channel_id=1, source_target_pairs={{16,0},{32,16},{48,32},{64,48},{80,64},{96,80},{112,96},{128,112},... | collective-permute-start | bytes 608264 | tf_op jit(solution)/shard_map/ppermute | solution.py:512
  7.4 0.9 copy-start.3
  14.0 5.5 %copy-start = (s32[31,16,72]{2,1,0:T(8,128)S(1)}, s32[31,16,72]{2,1,0:T(8,128)}, u32[]{:S(2)}) copy-start(s32[31,16,72]{2,1,0:T(8,128)} %index.1) | copy-start | bytes 428548
  14.0 5.5 %copy-start.1 = (s32[31,16,72]{2,1,0:T(8,128)S(1)}, s32[31,16,72]{2,1,0:T(8,128)}, u32[]{:S(2)}) copy-start(s32[31,16,72]{2,1,0:T(8,128)} %offset.1) | copy-start | bytes 428548
  14.0 5.4 %copy-start.2 = (f32[31,16,72]{2,1,0:T(8,128)S(1)}, f32[31,16,72]{2,1,0:T(8,128)}, u32[]{:S(2)}) copy-start(f32[31,16,72]{2,1,0:T(8,128)} %phase.1) | copy-start | bytes 428548
  14.1 11.6 %collective-permute-start.10 = (f32[4,96,128]{2,1,0:T(8,128)S(1)}, f32[4,96,128]{2,1,0:T(8,128)S(1)}, u32[]{:S(2)}, u32[]{:S(2)}) collective-permute-start(f32[4,96,128]{2,1,0:T(8,128)S(1)} %get-tuple-element.48), channel_id=1, source_target_pairs={{0,3},{1,2},{2,1},{3,0},{4,7},{5,6},{6,5},{7,4},{8,11},{9,10},{10,... | collective-permute-start | bytes 589832 | tf_op jit(solution)/shard_map/ppermute | solution.py:484
  18.8 8.7 %collective-permute-start.9 = (f32[4,96,128]{2,1,0:T(8,128)S(1)}, f32[4,96,128]{2,1,0:T(8,128)S(1)}, u32[]{:S(2)}, u32[]{:S(2)}) collective-permute-start(f32[4,96,128]{2,1,0:T(8,128)S(1)} %get-tuple-element.49), channel_id=1, source_target_pairs={{0,2},{1,3},{2,0},{3,1},{4,6},{5,7},{6,4},{7,5},{8,10},{9,11},{10,... | collective-permute-start | bytes 589832 | tf_op jit(solution)/shard_map/ppermute | solution.py:484
  18.8 8.7 %collective-permute-start.8 = (f32[4,96,128]{2,1,0:T(8,128)S(1)}, f32[4,96,128]{2,1,0:T(8,128)S(1)}, u32[]{:S(2)}, u32[]{:S(2)}) collective-permute-start(f32[4,96,128]{2,1,0:T(8,128)S(1)} %get-tuple-element.50), channel_id=1, source_target_pairs={{0,1},{1,0},{2,3},{3,2},{4,5},{5,4},{6,7},{7,6},{8,9},{9,8},{10,11... | collective-permute-start | bytes 589832 | tf_op jit(solution)/shard_map/ppermute | solution.py:484
  27.6 34.7 %collective-permute-start.11 = (f32[4,96,128]{2,1,0:T(8,128)S(1)}, f32[4,96,128]{2,1,0:T(8,128)S(1)}, u32[]{:S(2)}, u32[]{:S(2)}) collective-permute-start(f32[4,96,128]{2,1,0:T(8,128)S(1)} %pad_maximum_fusion.5), channel_id=1, source_target_pairs={{0,4},{1,5},{2,6},{3,7},{4,8},{5,9},{6,10},{7,11},{8,12},{9,13},{1... | collective-permute-start | bytes 589832 | tf_op jit(solution)/shard_map/ppermute | solution.py:484
  29.3 33.3 %collective-permute-start.12 = (f32[4,96,128]{2,1,0:T(8,128)S(1)}, f32[4,96,128]{2,1,0:T(8,128)S(1)}, u32[]{:S(2)}, u32[]{:S(2)}) collective-permute-start(f32[4,96,128]{2,1,0:T(8,128)S(1)} %pad_maximum_fusion.6), channel_id=1, source_target_pairs={{0,8},{1,9},{2,10},{3,11},{4,12},{5,13},{6,14},{7,15},{8,0},{9,1},... | collective-permute-start | bytes 589832 | tf_op jit(solution)/shard_map/ppermute | solution.py:484
  30.3 32.3 %collective-permute-start.13 = (f32[4,96,128]{2,1,0:T(8,128)S(1)}, f32[4,96,128]{2,1,0:T(8,128)S(1)}, u32[]{:S(2)}, u32[]{:S(2)}) collective-permute-start(f32[4,96,128]{2,1,0:T(8,128)S(1)} %pad_maximum_fusion.7), channel_id=1, source_target_pairs={{0,12},{1,13},{2,14},{3,15},{4,0},{5,1},{6,2},{7,3},{8,4},{9,5},{1... | collective-permute-start | bytes 589832 | tf_op jit(solution)/shard_map/ppermute | solution.py:484
  32.8 7.7 %collective-permute-start.2 = (f32[4,96,128]{2,1,0:T(8,128)S(1)}, f32[4,96,128]{2,1,0:T(8,128)S(1)}, u32[]{:S(2)}, u32[]{:S(2)}) collective-permute-start(f32[4,96,128]{2,1,0:T(8,128)S(1)} %get-tuple-element.56), channel_id=1, source_target_pairs={{0,1},{1,0},{2,3},{3,2},{4,5},{5,4},{6,7},{7,6},{8,9},{9,8},{10,11... | collective-permute-start | bytes 589832 | tf_op jit(solution)/shard_map/ppermute | solution.py:484
  34.0 11.7 %collective-permute-start.4 = (f32[4,96,128]{2,1,0:T(8,128)S(1)}, f32[4,96,128]{2,1,0:T(8,128)S(1)}, u32[]{:S(2)}, u32[]{:S(2)}) collective-permute-start(f32[4,96,128]{2,1,0:T(8,128)S(1)} %get-tuple-element.57), channel_id=1, source_target_pairs={{0,3},{1,2},{2,1},{3,0},{4,7},{5,6},{6,5},{7,4},{8,11},{9,10},{10,... | collective-permute-start | bytes 589832 | tf_op jit(solution)/shard_map/ppermute | solution.py:484
  40.5 18.4 %collective-permute-start.3 = (f32[4,96,128]{2,1,0:T(8,128)S(1)}, f32[4,96,128]{2,1,0:T(8,128)S(1)}, u32[]{:S(2)}, u32[]{:S(2)}) collective-permute-start(f32[4,96,128]{2,1,0:T(8,128)S(1)} %get-tuple-element.58), channel_id=1, source_target_pairs={{0,2},{1,3},{2,0},{3,1},{4,6},{5,7},{6,4},{7,5},{8,10},{9,11},{10,... | collective-permute-start | bytes 589832 | tf_op jit(solution)/shard_map/ppermute | solution.py:484
  58.9 11.0 %collective-permute-start.5 = (f32[4,96,128]{2,1,0:T(8,128)S(1)}, f32[4,96,128]{2,1,0:T(8,128)S(1)}, u32[]{:S(2)}, u32[]{:S(2)}) collective-permute-start(f32[4,96,128]{2,1,0:T(8,128)S(1)} %pad_maximum_fusion.1), channel_id=1, source_target_pairs={{0,4},{1,5},{2,6},{3,7},{4,8},{5,9},{6,10},{7,11},{8,12},{9,13},{1... | collective-permute-start | bytes 589832 | tf_op jit(solution)/shard_map/ppermute | solution.py:484
  59.1 13.0 %collective-permute-start.6 = (f32[4,96,128]{2,1,0:T(8,128)S(1)}, f32[4,96,128]{2,1,0:T(8,128)S(1)}, u32[]{:S(2)}, u32[]{:S(2)}) collective-permute-start(f32[4,96,128]{2,1,0:T(8,128)S(1)} %pad_maximum_fusion.2), channel_id=1, source_target_pairs={{0,8},{1,9},{2,10},{3,11},{4,12},{5,13},{6,14},{7,15},{8,0},{9,1},... | collective-permute-start | bytes 589832 | tf_op jit(solution)/shard_map/ppermute | solution.py:484
  62.3 9.7 %collective-permute-start.7 = (f32[4,96,128]{2,1,0:T(8,128)S(1)}, f32[4,96,128]{2,1,0:T(8,128)S(1)}, u32[]{:S(2)}, u32[]{:S(2)}) collective-permute-start(f32[4,96,128]{2,1,0:T(8,128)S(1)} %pad_maximum_fusion.3), channel_id=1, source_target_pairs={{0,12},{1,13},{2,14},{3,15},{4,0},{5,1},{6,2},{7,3},{8,4},{9,5},{1... | collective-permute-start | bytes 589832 | tf_op jit(solution)/shard_map/ppermute | solution.py:484
  67.4 11.9 %collective-permute-start.22 = (f32[4,96,128]{2,1,0:T(8,128)S(1)}, f32[4,96,128]{2,1,0:T(8,128)S(1)}, u32[]{:S(2)}, u32[]{:S(2)}) collective-permute-start(f32[4,96,128]{2,1,0:T(8,128)S(1)} %get-tuple-element.37), channel_id=1, source_target_pairs={{0,3},{1,2},{2,1},{3,0},{4,7},{5,6},{6,5},{7,4},{8,11},{9,10},{10,... | collective-permute-start | bytes 589832 | tf_op jit(solution)/shard_map/ppermute | solution.py:484
  69.9 10.4 %collective-permute-start.21 = (f32[4,96,128]{2,1,0:T(8,128)S(1)}, f32[4,96,128]{2,1,0:T(8,128)S(1)}, u32[]{:S(2)}, u32[]{:S(2)}) collective-permute-start(f32[4,96,128]{2,1,0:T(8,128)S(1)} %get-tuple-element.38), channel_id=1, source_target_pairs={{0,2},{1,3},{2,0},{3,1},{4,6},{5,7},{6,4},{7,5},{8,10},{9,11},{10,... | collective-permute-start | bytes 589832 | tf_op jit(solution)/shard_map/ppermute | solution.py:484
  70.0 12.4 %collective-permute-start.20 = (f32[4,96,128]{2,1,0:T(8,128)S(1)}, f32[4,96,128]{2,1,0:T(8,128)S(1)}, u32[]{:S(2)}, u32[]{:S(2)}) collective-permute-start(f32[4,96,128]{2,1,0:T(8,128)S(1)} %get-tuple-element.39), channel_id=1, source_target_pairs={{0,1},{1,0},{2,3},{3,2},{4,5},{5,4},{6,7},{7,6},{8,9},{9,8},{10,11... | collective-permute-start | bytes 589832 | tf_op jit(solution)/shard_map/ppermute | solution.py:484
  76.8 13.9 %collective-permute-start.14 = (f32[4,96,128]{2,1,0:T(8,128)S(1)}, f32[4,96,128]{2,1,0:T(8,128)S(1)}, u32[]{:S(2)}, u32[]{:S(2)}) collective-permute-start(f32[4,96,128]{2,1,0:T(8,128)S(1)} %get-tuple-element.45), channel_id=1, source_target_pairs={{0,1},{1,0},{2,3},{3,2},{4,5},{5,4},{6,7},{7,6},{8,9},{9,8},{10,11... | collective-permute-start | bytes 589832 | tf_op jit(solution)/shard_map/ppermute | solution.py:484
  77.0 16.4 %collective-permute-start.16 = (f32[4,96,128]{2,1,0:T(8,128)S(1)}, f32[4,96,128]{2,1,0:T(8,128)S(1)}, u32[]{:S(2)}, u32[]{:S(2)}) collective-permute-start(f32[4,96,128]{2,1,0:T(8,128)S(1)} %get-tuple-element.46), channel_id=1, source_target_pairs={{0,3},{1,2},{2,1},{3,0},{4,7},{5,6},{6,5},{7,4},{8,11},{9,10},{10,... | collective-permute-start | bytes 589832 | tf_op jit(solution)/shard_map/ppermute | solution.py:484
  79.4 23.4 %collective-permute-start.15 = (f32[4,96,128]{2,1,0:T(8,128)S(1)}, f32[4,96,128]{2,1,0:T(8,128)S(1)}, u32[]{:S(2)}, u32[]{:S(2)}) collective-permute-start(f32[4,96,128]{2,1,0:T(8,128)S(1)} %get-tuple-element.47), channel_id=1, source_target_pairs={{0,2},{1,3},{2,0},{3,1},{4,6},{5,7},{6,4},{7,5},{8,10},{9,11},{10,... | collective-permute-start | bytes 589832 | tf_op jit(solution)/shard_map/ppermute | solution.py:484
  82.4 24.0 %collective-permute-start.23 = (f32[4,96,128]{2,1,0:T(8,128)S(1)}, f32[4,96,128]{2,1,0:T(8,128)S(1)}, u32[]{:S(2)}, u32[]{:S(2)}) collective-permute-start(f32[4,96,128]{2,1,0:T(8,128)S(1)} %pad_maximum_fusion.13), channel_id=1, source_target_pairs={{0,4},{1,5},{2,6},{3,7},{4,8},{5,9},{6,10},{7,11},{8,12},{9,13},{1... | collective-permute-start | bytes 589832 | tf_op jit(solution)/shard_map/ppermute | solution.py:484
  85.5 22.0 %collective-permute-start.24 = (f32[4,96,128]{2,1,0:T(8,128)S(1)}, f32[4,96,128]{2,1,0:T(8,128)S(1)}, u32[]{:S(2)}, u32[]{:S(2)}) collective-permute-start(f32[4,96,128]{2,1,0:T(8,128)S(1)} %pad_maximum_fusion.14), channel_id=1, source_target_pairs={{0,8},{1,9},{2,10},{3,11},{4,12},{5,13},{6,14},{7,15},{8,0},{9,1},... | collective-permute-start | bytes 589832 | tf_op jit(solution)/shard_map/ppermute | solution.py:484
  90.7 16.8 %collective-permute-start.25 = (f32[4,96,128]{2,1,0:T(8,128)S(1)}, f32[4,96,128]{2,1,0:T(8,128)S(1)}, u32[]{:S(2)}, u32[]{:S(2)}) collective-permute-start(f32[4,96,128]{2,1,0:T(8,128)S(1)} %pad_maximum_fusion.15), channel_id=1, source_target_pairs={{0,12},{1,13},{2,14},{3,15},{4,0},{5,1},{6,2},{7,3},{8,4},{9,5},{1... | collective-permute-start | bytes 589832 | tf_op jit(solution)/shard_map/ppermute | solution.py:484
  102.8 7.8 %collective-permute-start.17 = (f32[4,96,128]{2,1,0:T(8,128)S(1)}, f32[4,96,128]{2,1,0:T(8,128)S(1)}, u32[]{:S(2)}, u32[]{:S(2)}) collective-permute-start(f32[4,96,128]{2,1,0:T(8,128)S(1)} %pad_maximum_fusion.9), channel_id=1, source_target_pairs={{0,4},{1,5},{2,6},{3,7},{4,8},{5,9},{6,10},{7,11},{8,12},{9,13},{1... | collective-permute-start | bytes 589832 | tf_op jit(solution)/shard_map/ppermute | solution.py:484
  104.7 7.4 %collective-permute-start.18 = (f32[4,96,128]{2,1,0:T(8,128)S(1)}, f32[4,96,128]{2,1,0:T(8,128)S(1)}, u32[]{:S(2)}, u32[]{:S(2)}) collective-permute-start(f32[4,96,128]{2,1,0:T(8,128)S(1)} %pad_maximum_fusion.10), channel_id=1, source_target_pairs={{0,8},{1,9},{2,10},{3,11},{4,12},{5,13},{6,14},{7,15},{8,0},{9,1},... | collective-permute-start | bytes 589832 | tf_op jit(solution)/shard_map/ppermute | solution.py:484
  106.5 7.6 %collective-permute-start.19 = (f32[4,96,128]{2,1,0:T(8,128)S(1)}, f32[4,96,128]{2,1,0:T(8,128)S(1)}, u32[]{:S(2)}, u32[]{:S(2)}) collective-permute-start(f32[4,96,128]{2,1,0:T(8,128)S(1)} %pad_maximum_fusion.11), channel_id=1, source_target_pairs={{0,12},{1,13},{2,14},{3,15},{4,0},{5,1},{6,2},{7,3},{8,4},{9,5},{1... | collective-permute-start | bytes 589832 | tf_op jit(solution)/shard_map/ppermute | solution.py:484

commit v6 on v5

--- a/solution.py
+++ b/solution.py
@@ -65,9 +65,14 @@
     return jnp.take_along_axis(x, where, axis=0, mode="promise_in_bounds")
 
 
-def halo_kernel(tracers, thickness, courant_y, low, high, sem):
+def on_odd_row():
+    return (lax.axis_index("lat") & 1) == 1
+
+
+def halo_kernel(tracers, thickness, courant_y, inside, across, sem):
+    odd = on_odd_row()
     copies = []
-    for edge, (out, first) in enumerate(((low, 0), (high, ROWS - 2))):
+    for edge, (out, first) in enumerate(((inside, jnp.where(odd, 0, ROWS - 2)), (across, jnp.where(odd, ROWS - 2, 0)))):
         rows = pl.ds(first, 2)
         copies.append(pltpu.make_async_copy(tracers.at[:, rows], out.at[pl.ds(0, NTR)], sem.at[edge, 0]))
         copies.append(pltpu.make_async_copy(thickness.at[rows], out.at[THICK], sem.at[edge, 1]))
@@ -80,7 +85,7 @@
 
 def transport_kernel(part, *refs):
     if part == OUTER:
-        tracers, thickness, courant_x, courant_y, low, high, _, out, held, mx, ax, my, ay, fy, sem = refs
+        tracers, thickness, courant_x, courant_y, inside, across, _, out, held, mx, ax, my, ay, fy, sem = refs
     else:
         tracers, thickness, courant_x, courant_y, _, out, held, mx, ax, my, ay, fy, sem = refs
     chunk = slots_to()
@@ -100,11 +105,32 @@
             bring(tracers.at[:, own, :, cut], view.at[pl.ds(0, NTR), into, run, c])
             for array, source in ((THICK, thickness), (NORTH, courant_y), (EAST, courant_x)):
                 bring(source.at[own, :, cut], view.at[array, into, run, c])
-        if part == OUTER:
-            bring(low.at[pl.ds(0, NTR + 1), :, :, cut], view.at[pl.ds(0, NTR + 1), pl.ds(0, 2), 0, c])
-            bring(high.at[:, :, :, cut], view.at[pl.ds(0, NTR + 2), pl.ds(6, 2), 1, c])
     for copy in copies:
         copy.start()
+    if part == OUTER:
+
+        def bring_halos(low, high):
+            for c in range(TILES):
+                cut = pl.ds(LANES * c, LANES)
+                bring(low.at[pl.ds(0, NTR + 1), :, :, cut], view.at[pl.ds(0, NTR + 1), pl.ds(0, 2), 0, c])
+                bring(high.at[:, :, :, cut], view.at[pl.ds(0, NTR + 2), pl.ds(6, 2), 1, c])
+            return copies[-2 * TILES :]
+
+        odd = on_odd_row()
+
+        @pl.when(odd)
+        def _():
+            for copy in bring_halos(inside, across):
+                copy.start()
+
+        del copies[-2 * TILES :]
+        halos = bring_halos(across, inside)
+
+        @pl.when(jnp.logical_not(odd))
+        def _():
+            for copy in halos:
+                copy.start()
+
     for g in range(GROUPS):
         out[g, pl.ds(REST, 8 * BLOCKS), :] = jnp.zeros((8 * BLOCKS, LANES), F32)
     for copy in copies:
@@ -330,7 +356,7 @@
 
 def place_of():
     lev = lax.axis_index("lev")
-    return lev >> 2, lev & 3, (lax.axis_index("lat") & 1) == 1
+    return lev >> 2, lev & 3, on_odd_row()
 
 
 def slots_to():
@@ -428,7 +454,7 @@
     return pl.pallas_call(
         functools.partial(transport_kernel, part),
         out_shape=jax.ShapeDtypeStruct((GROUPS, DEPTH, LANES), F32),
-        in_specs=[IN_HBM] * 4 + [ANYWHERE] * (len(given) - 4),
+        in_specs=[IN_HBM] * 4 + [IN_HBM if part == INNER else ANYWHERE] * (len(given) - 4),
         out_specs=IN_VMEM,
         scratch_shapes=[
             pltpu.VMEM(((NTR + 3) * slots_of(part) * STEP, LANES), F32),
@@ -499,18 +525,20 @@
 
 def shards(tracers, thickness, courant_x, courant_y, level_index, level_offset, level_phase):
     own = [pltpu.with_memory_space_constraint(x, pltpu.HBM) for x in (tracers, thickness, courant_x, courant_y)]
-    rim = jax.ShapeDtypeStruct((NTR + 2, 2, LEVS, LONS), F32)
-    south, north = pl.pallas_call(
+    rim = pltpu.HBM((NTR + 2, 2, LEVS, LONS), F32)
+    inside, across = pl.pallas_call(
         halo_kernel,
         out_shape=(rim, rim),
         in_specs=[IN_HBM] * 3,
         out_specs=(IN_VMEM, IN_VMEM),
         scratch_shapes=[pltpu.SemaphoreType.DMA((2, 3))],
     )(own[0], own[1], own[3])
-    count = lax.axis_size("lat")
-    low = lax.ppermute(north, "lat", [(i, i + 1) for i in range(count - 1)])
-    high = lax.ppermute(south, "lat", [(i + 1, i) for i in range(count - 1)])
-    inner = transport(INNER, *own, south)
+    lats = lax.axis_size("lat")
+    to_core = [(i, i ^ 1) for i in range(lats)]
+    to_chip = [(i, i + 1) for i in range(1, lats - 1, 2)] + [(i + 1, i) for i in range(1, lats - 1, 2)]
+    first = pltpu.with_memory_space_constraint(inside, pltpu.HBM)
+    inside, across = lax.ppermute(inside, "lat", to_core), lax.ppermute(across, "lat", to_chip)
+    inner = transport(INNER, *own, first)
     table = jax.ShapeDtypeStruct((2 * GROUPS * 16, LANES), F32)
     inner_table, outer_table = pl.pallas_call(
         target_kernel,
@@ -519,13 +547,13 @@
         out_specs=(IN_VMEM, IN_VMEM),
         compiler_params=PARAMS,
     )(level_index, level_offset, level_phase)
-    outer = transport(OUTER, *own, low, high, outer_table)
+    outer = transport(OUTER, *own, inside, across, outer_table)
     inner = first_hop(inner)
     inner, outer = second_hop(after(inner, outer)), first_hop(outer)
-    outer = second_hop(outer)
     inner = remap(inner, inner_table)
-    outer = remap(after(outer, inner), outer_table)
+    outer = second_hop(after(outer, inner))
     inner = first_hop(inner)
+    outer = remap(outer, outer_table)
     inner, outer = second_hop(after(inner, outer)), first_hop(outer)
     outer = second_hop(outer)
     return collect(OUTER, outer, collect(INNER, inner))

time: 118 us -> 110 us (0.932)
  starting transfers between devices: 43.9 us -> 40.8 us
  waiting for transfers between devices: 41.9 us -> 39 us
    ppermute x24, starting transfers between devices: 38.4 us -> 31.6 us  [hop(): moved[a] = lax.ppermute(blocks[a], ('lat', 'lev'), pairs)]
    ppermute x2, starting transfers between devices: 5.56 us -> 9.21 us  [the longest x1 7.04 us: shards(): lax.ppermute(inside, 'lat', to_core)]
    ppermute x24, waiting for transfers between devices: 41.9 us -> 39 us  [hop(): moved[a] = lax.ppermute(blocks[a], ('lat', 'lev'), pairs)]
  transfers between devices with their start and end apart: 26 -> 26, of which waited for: 9 -> 11; matrix products, arithmetic and copies ran while one was open for 1% -> 0% of each run, Pallas kernels for 21% -> 22%
where the time goes in v6:
time: 110 us
  starting transfers between devices  40.8 us (37%)
  waiting for transfers between devices  39 us (35%)
  Pallas kernels  29.2 us (27%)
    ppermute x24, waiting for transfers between devices, hop(): moved[a] = lax.ppermute(blocks[a], ('lat', 'lev'), pairs)  39 us
    ppermute x24, starting transfers between devices, hop(): moved[a] = lax.ppermute(blocks[a], ('lat', 'lev'), pairs)  31.6 us
    pallas_call x2, Pallas kernels, transport(): pl.pallas_call(functools.partial(transport_kernel, part), out_shape=jax.S...  11.3 us
    pallas_call x2, Pallas kernels, remap(): pl.pallas_call(remap_kernel, out_shape=jax.ShapeDtypeStruct((GROUPS, DEPT...  9.41 us
    ppermute x1, starting transfers between devices, shards(): lax.ppermute(inside, 'lat', to_core)  7.04 us
    pallas_call x2, Pallas kernels, collect(): pl.pallas_call(functools.partial(collect_kernel, part), out_shape=jax.Sha...  6.16 us
  transfers between devices with their start and end apart: 26, of which 11 were waited for; matrix products, arithmetic and copies ran while one was open for 0% of the time, Pallas kernels for 22%

profile of v6, /device:TPU:14, one launch (start us, length us, event | category | flops | bytes accessed | tf_op | source)
XLA Modules:
  0.0 110.2 jit_solution(8236224186692153420)
XLA Ops:
  0.0 1.8 %shard_map.73 = (f32[11,2,2,1152]{3,2,1,0:T(2,128)}, f32[11,2,2,1152]{3,2,1,0:T(2,128)}) custom-call(f32[9,16,2,1152]{3,2,1,0:T(2,128)} %refs_0_.3, f32[16,2,1152]{2,1,0:T(2,128)} %refs_1_.3, f32[16,2,1152]{2,1,0:T(2,128)} %refs_3_.3), custom_call_target="tpu_custom_call" | custom-call | tf_op jit(solution)/shard_map/pallas_call | solution.py:529
  1.8 2.2 %collective-permute-start.1 = (f32[11,2,2,1152]{3,2,1,0:T(2,128)}, f32[11,2,2,1152]{3,2,1,0:T(2,128)S(1)}, u32[]{:S(2)}, u32[]{:S(2)}) collective-permute-start(f32[11,2,2,1152]{3,2,1,0:T(2,128)} %get-tuple-element.22), channel_id=1, source_target_pairs={{16,32},{48,64},{80,96},{112,128},{144,160},{176,192},{208,224},{3... | collective-permute-start | bytes 608264 | tf_op jit(solution)/shard_map/ppermute | solution.py:540
  4.0 7.0 %collective-permute-start = (f32[11,2,2,1152]{3,2,1,0:T(2,128)}, f32[11,2,2,1152]{3,2,1,0:T(2,128)S(1)}, u32[]{:S(2)}, u32[]{:S(2)}) collective-permute-start(f32[11,2,2,1152]{3,2,1,0:T(2,128)} %get-tuple-element.21.refs_4_), channel_id=1, source_target_pairs={{0,16},{16,0},{32,48},{48,32},{64,80},{80,64},{96,112},{112,96},{1... | collective-permute-start | bytes 608264 | tf_op jit(solution)/shard_map/ppermute | solution.py:540
  11.1 5.6 %shard_map.76 = f32[16,96,128]{2,1,0:T(8,128)S(1)} custom-call(f32[9,16,2,1152]{3,2,1,0:T(2,128)} %refs_0_.3, f32[16,2,1152]{2,1,0:T(2,128)} %refs_1_.3, f32[16,2,1152]{2,1,0:T(2,128)} %refs_2_.3, f32[16,2,1152]{2,1,0:T(2,128)} %refs_3_.3, f32[11,2,2,1152]{3,2,1,0:T(2,128)} %get-tuple-element.21.refs_4_), custom_call_target="tpu_custom_call" | custom-call | tf_op jit(solution)/shard_map/pallas_call | solution.py:454
  16.7 0.0 copy-start
  16.7 0.0 copy-start.1
  16.7 0.0 copy-start.2
  16.7 0.1 fusion.3
  16.8 2.0 %collective-permute-start.7 = (f32[4,96,128]{2,1,0:T(8,128)S(1)}, f32[4,96,128]{2,1,0:T(8,128)S(1)}, u32[]{:S(2)}, u32[]{:S(2)}) collective-permute-start(f32[4,96,128]{2,1,0:T(8,128)S(1)} %get-tuple-element.48), channel_id=1, source_target_pairs={{0,3},{1,2},{2,1},{3,0},{4,7},{5,6},{6,5},{7,4},{8,11},{9,10},{10,... | collective-permute-start | bytes 589832 | tf_op jit(solution)/shard_map/ppermute | solution.py:510
  18.8 0.6 collective-permute-start.6
  19.3 1.9 %collective-permute-start.5 = (f32[4,96,128]{2,1,0:T(8,128)S(1)}, f32[4,96,128]{2,1,0:T(8,128)S(1)}, u32[]{:S(2)}, u32[]{:S(2)}) collective-permute-start(f32[4,96,128]{2,1,0:T(8,128)S(1)} %get-tuple-element.50), channel_id=1, source_target_pairs={{0,1},{1,0},{2,3},{3,2},{4,5},{5,4},{6,7},{7,6},{8,9},{9,8},{10,11... | collective-permute-start | bytes 589832 | tf_op jit(solution)/shard_map/ppermute | solution.py:510
  21.2 0.5 shard_map.74
  21.7 0.0 collective-permute-done.1.refs_5_
  21.7 0.0 collective-permute-done.refs_4_
  21.7 5.7 %shard_map.75 = f32[16,96,128]{2,1,0:T(8,128)S(1)} custom-call(f32[9,16,2,1152]{3,2,1,0:T(2,128)} %refs_0_.3, f32[16,2,1152]{2,1,0:T(2,128)} %refs_1_.3, f32[16,2,1152]{2,1,0:T(2,128)} %refs_2_.3, f32[16,2,1152]{2,1,0:T(2,128)} %refs_3_.3, f32[11,2,2,1152]{3,2,1,0:T(2,128)S(1)} %collective-permute-done.refs_4_, ...), custom_call_target="tpu_custom_call" | custom-call | tf_op jit(solution)/shard_map/pallas_call | solution.py:454
  27.4 0.0 collective-permute-done.7
  27.5 1.8 %collective-permute-done.6 = f32[4,96,128]{2,1,0:T(8,128)S(1)} collective-permute-done((f32[4,96,128]{2,1,0:T(8,128)S(1)}, f32[4,96,128]{2,1,0:T(8,128)S(1)}, u32[]{:S(2)}, u32[]{:S(2)}) %collective-permute-start.6) | collective-permute-done | bytes 196640 | tf_op jit(solution)/shard_map/ppermute | solution.py:510
  29.3 0.0 collective-permute-done.5
  29.4 1.7 %collective-permute-start.8 = (f32[4,96,128]{2,1,0:T(8,128)S(1)}, f32[4,96,128]{2,1,0:T(8,128)S(1)}, u32[]{:S(2)}, u32[]{:S(2)}) collective-permute-start(f32[4,96,128]{2,1,0:T(8,128)S(1)} %pad_maximum_fusion.1), channel_id=1, source_target_pairs={{0,4},{1,5},{2,6},{3,7},{4,8},{5,9},{6,10},{7,11},{8,12},{9,13},{1... | collective-permute-start | bytes 589832 | tf_op jit(solution)/shard_map/ppermute | solution.py:510
  31.1 1.0 collective-permute-start.9
  32.1 2.5 %collective-permute-start.10 = (f32[4,96,128]{2,1,0:T(8,128)S(1)}, f32[4,96,128]{2,1,0:T(8,128)S(1)}, u32[]{:S(2)}, u32[]{:S(2)}) collective-permute-start(f32[4,96,128]{2,1,0:T(8,128)S(1)} %pad_maximum_fusion.3), channel_id=1, source_target_pairs={{0,12},{1,13},{2,14},{3,15},{4,0},{5,1},{6,2},{7,3},{8,4},{9,5},{1... | collective-permute-start | bytes 589832 | tf_op jit(solution)/shard_map/ppermute | solution.py:510
  34.6 0.1 fusion.4
  34.7 2.0 %collective-permute-start.4 = (f32[4,96,128]{2,1,0:T(8,128)S(1)}, f32[4,96,128]{2,1,0:T(8,128)S(1)}, u32[]{:S(2)}, u32[]{:S(2)}) collective-permute-start(f32[4,96,128]{2,1,0:T(8,128)S(1)} %get-tuple-element.52), channel_id=1, source_target_pairs={{0,3},{1,2},{2,1},{3,0},{4,7},{5,6},{6,5},{7,4},{8,11},{9,10},{10,... | collective-permute-start | bytes 589832 | tf_op jit(solution)/shard_map/ppermute | solution.py:510
  36.7 0.0 collective-permute-start.3
  36.7 0.0 collective-permute-done.8.refs_1_
  36.7 2.5 %collective-permute-start.2 = (f32[4,96,128]{2,1,0:T(8,128)S(1)}, f32[4,96,128]{2,1,0:T(8,128)S(1)}, u32[]{:S(2)}, u32[]{:S(2)}) collective-permute-start(f32[4,96,128]{2,1,0:T(8,128)S(1)} %get-tuple-element.54), channel_id=1, source_target_pairs={{0,1},{1,0},{2,3},{3,2},{4,5},{5,4},{6,7},{7,6},{8,9},{9,8},{10,11... | collective-permute-start | bytes 589832 | tf_op jit(solution)/shard_map/ppermute | solution.py:510
  39.2 1.4 %collective-permute-done.9.refs_2_ = f32[4,96,128]{2,1,0:T(8,128)S(1)} collective-permute-done((f32[4,96,128]{2,1,0:T(8,128)S(1)}, f32[4,96,128]{2,1,0:T(8,128)S(1)}, u32[]{:S(2)}, u32[]{:S(2)}) %collective-permute-start.9) | collective-permute-done | bytes 196640 | tf_op jit(solution)/shard_map/ppermute | solution.py:510
  40.5 1.8 %collective-permute-done.10.refs_3_ = f32[4,96,128]{2,1,0:T(8,128)S(1)} collective-permute-done((f32[4,96,128]{2,1,0:T(8,128)S(1)}, f32[4,96,128]{2,1,0:T(8,128)S(1)}, u32[]{:S(2)}, u32[]{:S(2)}) %collective-permute-start.10) | collective-permute-done | bytes 196640 | tf_op jit(solution)/shard_map/ppermute | solution.py:510
  42.3 4.7 %shard_map.77 = f32[16,96,128]{2,1,0:T(8,128)S(1)} custom-call(f32[4,96,128]{2,1,0:T(8,128)S(1)} %pad_maximum_fusion.refs_0_, f32[4,96,128]{2,1,0:T(8,128)S(1)} %collective-permute-done.8.refs_1_, f32[4,96,128]{2,1,0:T(8,128)S(1)} %collective-permute-done.9.refs_2_, f32[4,96,128]{2,1,0:T(8,128)S(1)} %collective-permute-done.10.refs_3_, ...), custom_call_target="tpu_custom_call" | custom-call | tf_op jit(solution)/shard_map/pallas_call | solution.py:474
  47.0 0.0 collective-permute-done.4
  47.0 1.6 %collective-permute-done.3 = f32[4,96,128]{2,1,0:T(8,128)S(1)} collective-permute-done((f32[4,96,128]{2,1,0:T(8,128)S(1)}, f32[4,96,128]{2,1,0:T(8,128)S(1)}, u32[]{:S(2)}, u32[]{:S(2)}) %collective-permute-start.3) | collective-permute-done | bytes 196640 | tf_op jit(solution)/shard_map/ppermute | solution.py:510
  48.7 0.4 collective-permute-start.11
  49.1 3.0 %collective-permute-start.12 = (f32[4,96,128]{2,1,0:T(8,128)S(1)}, f32[4,96,128]{2,1,0:T(8,128)S(1)}, u32[]{:S(2)}, u32[]{:S(2)}) collective-permute-start(f32[4,96,128]{2,1,0:T(8,128)S(1)} %pad_maximum_fusion.6), channel_id=1, source_target_pairs={{0,8},{1,9},{2,10},{3,11},{4,12},{5,13},{6,14},{7,15},{8,0},{9,1},... | collective-permute-start | bytes 589832 | tf_op jit(solution)/shard_map/ppermute | solution.py:510
  52.2 0.9 collective-permute-start.13
  53.1 0.1 fusion
  53.1 2.0 %collective-permute-start.22 = (f32[4,96,128]{2,1,0:T(8,128)S(1)}, f32[4,96,128]{2,1,0:T(8,128)S(1)}, u32[]{:S(2)}, u32[]{:S(2)}) collective-permute-start(f32[4,96,128]{2,1,0:T(8,128)S(1)} %get-tuple-element.37), channel_id=1, source_target_pairs={{0,3},{1,2},{2,1},{3,0},{4,7},{5,6},{6,5},{7,4},{8,11},{9,10},{10,... | collective-permute-start | bytes 589832 | tf_op jit(solution)/shard_map/ppermute | solution.py:510
  55.1 0.0 collective-permute-start.21
  55.1 0.0 collective-permute-done.11.refs_1_
  55.1 2.5 %collective-permute-start.20 = (f32[4,96,128]{2,1,0:T(8,128)S(1)}, f32[4,96,128]{2,1,0:T(8,128)S(1)}, u32[]{:S(2)}, u32[]{:S(2)}) collective-permute-start(f32[4,96,128]{2,1,0:T(8,128)S(1)} %get-tuple-element.39), channel_id=1, source_target_pairs={{0,1},{1,0},{2,3},{3,2},{4,5},{5,4},{6,7},{7,6},{8,9},{9,8},{10,11... | collective-permute-start | bytes 589832 | tf_op jit(solution)/shard_map/ppermute | solution.py:510
  57.7 0.0 collective-permute-done.12.refs_2_
  57.7 2.1 %collective-permute-done.13.refs_3_ = f32[4,96,128]{2,1,0:T(8,128)S(1)} collective-permute-done((f32[4,96,128]{2,1,0:T(8,128)S(1)}, f32[4,96,128]{2,1,0:T(8,128)S(1)}, u32[]{:S(2)}, u32[]{:S(2)}) %collective-permute-start.13) | collective-permute-done | bytes 196640 | tf_op jit(solution)/shard_map/ppermute | solution.py:510
  59.8 4.7 %shard_map.78 = f32[16,96,128]{2,1,0:T(8,128)S(1)} custom-call(f32[4,96,128]{2,1,0:T(8,128)S(1)} %pad_maximum_fusion.4.refs_0_, f32[4,96,128]{2,1,0:T(8,128)S(1)} %collective-permute-done.11.refs_1_, f32[4,96,128]{2,1,0:T(8,128)S(1)} %collective-permute-done.12.refs_2_, f32[4,96,128]{2,1,0:T(8,128)S(1)} %collective-permute-done.13.refs_3_, ...), custom_call_target="tpu_custom_call" | custom-call | tf_op jit(solution)/shard_map/pallas_call | solution.py:474
  64.6 0.0 collective-permute-done.22
  64.6 8.1 %collective-permute-done.21 = f32[4,96,128]{2,1,0:T(8,128)S(1)} collective-permute-done((f32[4,96,128]{2,1,0:T(8,128)S(1)}, f32[4,96,128]{2,1,0:T(8,128)S(1)}, u32[]{:S(2)}, u32[]{:S(2)}) %collective-permute-start.21) | collective-permute-done | bytes 196640 | tf_op jit(solution)/shard_map/ppermute | solution.py:510
  72.8 0.1 collective-permute-start.14
  72.9 2.0 %collective-permute-start.16 = (f32[4,96,128]{2,1,0:T(8,128)S(1)}, f32[4,96,128]{2,1,0:T(8,128)S(1)}, u32[]{:S(2)}, u32[]{:S(2)}) collective-permute-start(f32[4,96,128]{2,1,0:T(8,128)S(1)} %get-tuple-element.46), channel_id=1, source_target_pairs={{0,3},{1,2},{2,1},{3,0},{4,7},{5,6},{6,5},{7,4},{8,11},{9,10},{10,... | collective-permute-start | bytes 589832 | tf_op jit(solution)/shard_map/ppermute | solution.py:510
  74.9 1.5 %collective-permute-start.15 = (f32[4,96,128]{2,1,0:T(8,128)S(1)}, f32[4,96,128]{2,1,0:T(8,128)S(1)}, u32[]{:S(2)}, u32[]{:S(2)}) collective-permute-start(f32[4,96,128]{2,1,0:T(8,128)S(1)} %get-tuple-element.47), channel_id=1, source_target_pairs={{0,2},{1,3},{2,0},{3,1},{4,6},{5,7},{6,4},{7,5},{8,10},{9,11},{10,... | collective-permute-start | bytes 589832 | tf_op jit(solution)/shard_map/ppermute | solution.py:510
  76.4 0.6 collective-permute-start.23
  77.0 1.8 %collective-permute-start.24 = (f32[4,96,128]{2,1,0:T(8,128)S(1)}, f32[4,96,128]{2,1,0:T(8,128)S(1)}, u32[]{:S(2)}, u32[]{:S(2)}) collective-permute-start(f32[4,96,128]{2,1,0:T(8,128)S(1)} %pad_maximum_fusion.14), channel_id=1, source_target_pairs={{0,8},{1,9},{2,10},{3,11},{4,12},{5,13},{6,14},{7,15},{8,0},{9,1},... | collective-permute-start | bytes 589832 | tf_op jit(solution)/shard_map/ppermute | solution.py:510
  78.9 0.0 collective-permute-done.14
  78.9 0.4 collective-permute-start.25
  79.3 1.3 %collective-permute-done.16 = f32[4,96,128]{2,1,0:T(8,128)S(1)} collective-permute-done((f32[4,96,128]{2,1,0:T(8,128)S(1)}, f32[4,96,128]{2,1,0:T(8,128)S(1)}, u32[]{:S(2)}, u32[]{:S(2)}) %collective-permute-start.16) | collective-permute-done | bytes 196640 | tf_op jit(solution)/shard_map/ppermute | solution.py:510
  80.7 16.8 %collective-permute-done.15 = f32[4,96,128]{2,1,0:T(8,128)S(1)} collective-permute-done((f32[4,96,128]{2,1,0:T(8,128)S(1)}, f32[4,96,128]{2,1,0:T(8,128)S(1)}, u32[]{:S(2)}, u32[]{:S(2)}) %collective-permute-start.15) | collective-permute-done | bytes 196640 | tf_op jit(solution)/shard_map/ppermute | solution.py:510
  97.6 0.1 collective-permute-start.17
  97.7 0.1 collective-permute-start.18
  97.8 0.0 collective-permute-done.23.refs_1_
  97.8 2.1 %collective-permute-start.19 = (f32[4,96,128]{2,1,0:T(8,128)S(1)}, f32[4,96,128]{2,1,0:T(8,128)S(1)}, u32[]{:S(2)}, u32[]{:S(2)}) collective-permute-start(f32[4,96,128]{2,1,0:T(8,128)S(1)} %pad_maximum_fusion.11), channel_id=1, source_target_pairs={{0,12},{1,13},{2,14},{3,15},{4,0},{5,1},{6,2},{7,3},{8,4},{9,5},{1... | collective-permute-start | bytes 589832 | tf_op jit(solution)/shard_map/ppermute | solution.py:510
  99.9 0.0 collective-permute-done.24.refs_2_
  99.9 0.0 collective-permute-done.25.refs_3_
  99.9 3.1 %shard_map.79.refs_4_ = f32[10,16,2,1152]{3,2,1,0:T(2,128)} custom-call(f32[4,96,128]{2,1,0:T(8,128)S(1)} %pad_maximum_fusion.12.refs_0_, f32[4,96,128]{2,1,0:T(8,128)S(1)} %collective-permute-done.23.refs_1_, f32[4,96,128]{2,1,0:T(8,128)S(1)} %collective-permute-done.24.refs_2_, f32[4,96,128]{2,1,0:T(8,128)S(1)} %collective-permute-done.25.refs_3_), custom_call_target="tpu_custom_call" | custom-call | tf_op jit(solution)/shard_map/pallas_call | solution.py:485
  103.1 0.2 collective-permute-done.17.refs_1_
  103.3 1.7 %collective-permute-done.18.refs_2_ = f32[4,96,128]{2,1,0:T(8,128)S(1)} collective-permute-done((f32[4,96,128]{2,1,0:T(8,128)S(1)}, f32[4,96,128]{2,1,0:T(8,128)S(1)}, u32[]{:S(2)}, u32[]{:S(2)}) %collective-permute-start.18) | collective-permute-done | bytes 196640 | tf_op jit(solution)/shard_map/ppermute | solution.py:510
  105.0 2.0 %collective-permute-done.19.refs_3_ = f32[4,96,128]{2,1,0:T(8,128)S(1)} collective-permute-done((f32[4,96,128]{2,1,0:T(8,128)S(1)}, f32[4,96,128]{2,1,0:T(8,128)S(1)}, u32[]{:S(2)}, u32[]{:S(2)}) %collective-permute-start.19) | collective-permute-done | bytes 196640 | tf_op jit(solution)/shard_map/ppermute | solution.py:510
  107.0 3.0 %shard_map.80 = f32[10,16,2,1152]{3,2,1,0:T(2,128)} custom-call(f32[4,96,128]{2,1,0:T(8,128)S(1)} %pad_maximum_fusion.8.refs_0_, f32[4,96,128]{2,1,0:T(8,128)S(1)} %collective-permute-done.17.refs_1_, f32[4,96,128]{2,1,0:T(8,128)S(1)} %collective-permute-done.18.refs_2_, ...), custom_call_target="tpu_custom_call", output_to_operand_aliasing={{}: (4, {})} | custom-call | tf_op jit(solution)/shard_map/pallas_call | solution.py:485
  (36 shorter events, 0.5 us)
Async XLA Ops:
  1.8 19.9 %collective-permute-start.1 = (f32[11,2,2,1152]{3,2,1,0:T(2,128)}, f32[11,2,2,1152]{3,2,1,0:T(2,128)S(1)}, u32[]{:S(2)}, u32[]{:S(2)}) collective-permute-start(f32[11,2,2,1152]{3,2,1,0:T(2,128)} %get-tuple-element.22), channel_id=1, source_target_pairs={{16,32},{48,64},{80,96},{112,128},{144,160},{176,192},{208,224},{3... | collective-permute-start | bytes 608264 | tf_op jit(solution)/shard_map/ppermute | solution.py:540
  4.0 17.7 %collective-permute-start = (f32[11,2,2,1152]{3,2,1,0:T(2,128)}, f32[11,2,2,1152]{3,2,1,0:T(2,128)S(1)}, u32[]{:S(2)}, u32[]{:S(2)}) collective-permute-start(f32[11,2,2,1152]{3,2,1,0:T(2,128)} %get-tuple-element.21.refs_4_), channel_id=1, source_target_pairs={{0,16},{16,0},{32,48},{48,32},{64,80},{80,64},{96,112},{112,96},{1... | collective-permute-start | bytes 608264 | tf_op jit(solution)/shard_map/ppermute | solution.py:540
  16.7 4.6 %copy-start = (s32[31,16,72]{2,1,0:T(8,128)S(1)}, s32[31,16,72]{2,1,0:T(8,128)}, u32[]{:S(2)}) copy-start(s32[31,16,72]{2,1,0:T(8,128)} %index.1) | copy-start | bytes 428548
  16.7 4.6 %copy-start.1 = (s32[31,16,72]{2,1,0:T(8,128)S(1)}, s32[31,16,72]{2,1,0:T(8,128)}, u32[]{:S(2)}) copy-start(s32[31,16,72]{2,1,0:T(8,128)} %offset.1) | copy-start | bytes 428548
  16.7 4.5 %copy-start.2 = (f32[31,16,72]{2,1,0:T(8,128)S(1)}, f32[31,16,72]{2,1,0:T(8,128)}, u32[]{:S(2)}) copy-start(f32[31,16,72]{2,1,0:T(8,128)} %phase.1) | copy-start | bytes 428548
  16.8 10.7 %collective-permute-start.7 = (f32[4,96,128]{2,1,0:T(8,128)S(1)}, f32[4,96,128]{2,1,0:T(8,128)S(1)}, u32[]{:S(2)}, u32[]{:S(2)}) collective-permute-start(f32[4,96,128]{2,1,0:T(8,128)S(1)} %get-tuple-element.48), channel_id=1, source_target_pairs={{0,3},{1,2},{2,1},{3,0},{4,7},{5,6},{6,5},{7,4},{8,11},{9,10},{10,... | collective-permute-start | bytes 589832 | tf_op jit(solution)/shard_map/ppermute | solution.py:510
  18.8 10.5 %collective-permute-start.6 = (f32[4,96,128]{2,1,0:T(8,128)S(1)}, f32[4,96,128]{2,1,0:T(8,128)S(1)}, u32[]{:S(2)}, u32[]{:S(2)}) collective-permute-start(f32[4,96,128]{2,1,0:T(8,128)S(1)} %get-tuple-element.49), channel_id=1, source_target_pairs={{0,2},{1,3},{2,0},{3,1},{4,6},{5,7},{6,4},{7,5},{8,10},{9,11},{10,... | collective-permute-start | bytes 589832 | tf_op jit(solution)/shard_map/ppermute | solution.py:510
  19.3 10.0 %collective-permute-start.5 = (f32[4,96,128]{2,1,0:T(8,128)S(1)}, f32[4,96,128]{2,1,0:T(8,128)S(1)}, u32[]{:S(2)}, u32[]{:S(2)}) collective-permute-start(f32[4,96,128]{2,1,0:T(8,128)S(1)} %get-tuple-element.50), channel_id=1, source_target_pairs={{0,1},{1,0},{2,3},{3,2},{4,5},{5,4},{6,7},{7,6},{8,9},{9,8},{10,11... | collective-permute-start | bytes 589832 | tf_op jit(solution)/shard_map/ppermute | solution.py:510
  29.4 7.3 %collective-permute-start.8 = (f32[4,96,128]{2,1,0:T(8,128)S(1)}, f32[4,96,128]{2,1,0:T(8,128)S(1)}, u32[]{:S(2)}, u32[]{:S(2)}) collective-permute-start(f32[4,96,128]{2,1,0:T(8,128)S(1)} %pad_maximum_fusion.1), channel_id=1, source_target_pairs={{0,4},{1,5},{2,6},{3,7},{4,8},{5,9},{6,10},{7,11},{8,12},{9,13},{1... | collective-permute-start | bytes 589832 | tf_op jit(solution)/shard_map/ppermute | solution.py:510
  31.1 9.4 %collective-permute-start.9 = (f32[4,96,128]{2,1,0:T(8,128)S(1)}, f32[4,96,128]{2,1,0:T(8,128)S(1)}, u32[]{:S(2)}, u32[]{:S(2)}) collective-permute-start(f32[4,96,128]{2,1,0:T(8,128)S(1)} %pad_maximum_fusion.2), channel_id=1, source_target_pairs={{0,8},{1,9},{2,10},{3,11},{4,12},{5,13},{6,14},{7,15},{8,0},{9,1},... | collective-permute-start | bytes 589832 | tf_op jit(solution)/shard_map/ppermute | solution.py:510
  32.1 10.2 %collective-permute-start.10 = (f32[4,96,128]{2,1,0:T(8,128)S(1)}, f32[4,96,128]{2,1,0:T(8,128)S(1)}, u32[]{:S(2)}, u32[]{:S(2)}) collective-permute-start(f32[4,96,128]{2,1,0:T(8,128)S(1)} %pad_maximum_fusion.3), channel_id=1, source_target_pairs={{0,12},{1,13},{2,14},{3,15},{4,0},{5,1},{6,2},{7,3},{8,4},{9,5},{1... | collective-permute-start | bytes 589832 | tf_op jit(solution)/shard_map/ppermute | solution.py:510
  34.7 12.3 %collective-permute-start.4 = (f32[4,96,128]{2,1,0:T(8,128)S(1)}, f32[4,96,128]{2,1,0:T(8,128)S(1)}, u32[]{:S(2)}, u32[]{:S(2)}) collective-permute-start(f32[4,96,128]{2,1,0:T(8,128)S(1)} %get-tuple-element.52), channel_id=1, source_target_pairs={{0,3},{1,2},{2,1},{3,0},{4,7},{5,6},{6,5},{7,4},{8,11},{9,10},{10,... | collective-permute-start | bytes 589832 | tf_op jit(solution)/shard_map/ppermute | solution.py:510
  36.7 12.0 %collective-permute-start.3 = (f32[4,96,128]{2,1,0:T(8,128)S(1)}, f32[4,96,128]{2,1,0:T(8,128)S(1)}, u32[]{:S(2)}, u32[]{:S(2)}) collective-permute-start(f32[4,96,128]{2,1,0:T(8,128)S(1)} %get-tuple-element.53), channel_id=1, source_target_pairs={{0,2},{1,3},{2,0},{3,1},{4,6},{5,7},{6,4},{7,5},{8,10},{9,11},{10,... | collective-permute-start | bytes 589832 | tf_op jit(solution)/shard_map/ppermute | solution.py:510
  36.7 11.9 %collective-permute-start.2 = (f32[4,96,128]{2,1,0:T(8,128)S(1)}, f32[4,96,128]{2,1,0:T(8,128)S(1)}, u32[]{:S(2)}, u32[]{:S(2)}) collective-permute-start(f32[4,96,128]{2,1,0:T(8,128)S(1)} %get-tuple-element.54), channel_id=1, source_target_pairs={{0,1},{1,0},{2,3},{3,2},{4,5},{5,4},{6,7},{7,6},{8,9},{9,8},{10,11... | collective-permute-start | bytes 589832 | tf_op jit(solution)/shard_map/ppermute | solution.py:510
  48.7 6.4 %collective-permute-start.11 = (f32[4,96,128]{2,1,0:T(8,128)S(1)}, f32[4,96,128]{2,1,0:T(8,128)S(1)}, u32[]{:S(2)}, u32[]{:S(2)}) collective-permute-start(f32[4,96,128]{2,1,0:T(8,128)S(1)} %pad_maximum_fusion.5), channel_id=1, source_target_pairs={{0,4},{1,5},{2,6},{3,7},{4,8},{5,9},{6,10},{7,11},{8,12},{9,13},{1... | collective-permute-start | bytes 589832 | tf_op jit(solution)/shard_map/ppermute | solution.py:510
  49.1 8.6 %collective-permute-start.12 = (f32[4,96,128]{2,1,0:T(8,128)S(1)}, f32[4,96,128]{2,1,0:T(8,128)S(1)}, u32[]{:S(2)}, u32[]{:S(2)}) collective-permute-start(f32[4,96,128]{2,1,0:T(8,128)S(1)} %pad_maximum_fusion.6), channel_id=1, source_target_pairs={{0,8},{1,9},{2,10},{3,11},{4,12},{5,13},{6,14},{7,15},{8,0},{9,1},... | collective-permute-start | bytes 589832 | tf_op jit(solution)/shard_map/ppermute | solution.py:510
  52.2 7.6 %collective-permute-start.13 = (f32[4,96,128]{2,1,0:T(8,128)S(1)}, f32[4,96,128]{2,1,0:T(8,128)S(1)}, u32[]{:S(2)}, u32[]{:S(2)}) collective-permute-start(f32[4,96,128]{2,1,0:T(8,128)S(1)} %pad_maximum_fusion.7), channel_id=1, source_target_pairs={{0,12},{1,13},{2,14},{3,15},{4,0},{5,1},{6,2},{7,3},{8,4},{9,5},{1... | collective-permute-start | bytes 589832 | tf_op jit(solution)/shard_map/ppermute | solution.py:510
  53.1 11.5 %collective-permute-start.22 = (f32[4,96,128]{2,1,0:T(8,128)S(1)}, f32[4,96,128]{2,1,0:T(8,128)S(1)}, u32[]{:S(2)}, u32[]{:S(2)}) collective-permute-start(f32[4,96,128]{2,1,0:T(8,128)S(1)} %get-tuple-element.37), channel_id=1, source_target_pairs={{0,3},{1,2},{2,1},{3,0},{4,7},{5,6},{6,5},{7,4},{8,11},{9,10},{10,... | collective-permute-start | bytes 589832 | tf_op jit(solution)/shard_map/ppermute | solution.py:510
  55.1 17.6 %collective-permute-start.21 = (f32[4,96,128]{2,1,0:T(8,128)S(1)}, f32[4,96,128]{2,1,0:T(8,128)S(1)}, u32[]{:S(2)}, u32[]{:S(2)}) collective-permute-start(f32[4,96,128]{2,1,0:T(8,128)S(1)} %get-tuple-element.38), channel_id=1, source_target_pairs={{0,2},{1,3},{2,0},{3,1},{4,6},{5,7},{6,4},{7,5},{8,10},{9,11},{10,... | collective-permute-start | bytes 589832 | tf_op jit(solution)/shard_map/ppermute | solution.py:510
  55.1 17.6 %collective-permute-start.20 = (f32[4,96,128]{2,1,0:T(8,128)S(1)}, f32[4,96,128]{2,1,0:T(8,128)S(1)}, u32[]{:S(2)}, u32[]{:S(2)}) collective-permute-start(f32[4,96,128]{2,1,0:T(8,128)S(1)} %get-tuple-element.39), channel_id=1, source_target_pairs={{0,1},{1,0},{2,3},{3,2},{4,5},{5,4},{6,7},{7,6},{8,9},{9,8},{10,11... | collective-permute-start | bytes 589832 | tf_op jit(solution)/shard_map/ppermute | solution.py:510
  72.8 6.1 %collective-permute-start.14 = (f32[4,96,128]{2,1,0:T(8,128)S(1)}, f32[4,96,128]{2,1,0:T(8,128)S(1)}, u32[]{:S(2)}, u32[]{:S(2)}) collective-permute-start(f32[4,96,128]{2,1,0:T(8,128)S(1)} %get-tuple-element.45), channel_id=1, source_target_pairs={{0,1},{1,0},{2,3},{3,2},{4,5},{5,4},{6,7},{7,6},{8,9},{9,8},{10,11... | collective-permute-start | bytes 589832 | tf_op jit(solution)/shard_map/ppermute | solution.py:510
  72.9 7.8 %collective-permute-start.16 = (f32[4,96,128]{2,1,0:T(8,128)S(1)}, f32[4,96,128]{2,1,0:T(8,128)S(1)}, u32[]{:S(2)}, u32[]{:S(2)}) collective-permute-start(f32[4,96,128]{2,1,0:T(8,128)S(1)} %get-tuple-element.46), channel_id=1, source_target_pairs={{0,3},{1,2},{2,1},{3,0},{4,7},{5,6},{6,5},{7,4},{8,11},{9,10},{10,... | collective-permute-start | bytes 589832 | tf_op jit(solution)/shard_map/ppermute | solution.py:510
  74.9 22.6 %collective-permute-start.15 = (f32[4,96,128]{2,1,0:T(8,128)S(1)}, f32[4,96,128]{2,1,0:T(8,128)S(1)}, u32[]{:S(2)}, u32[]{:S(2)}) collective-permute-start(f32[4,96,128]{2,1,0:T(8,128)S(1)} %get-tuple-element.47), channel_id=1, source_target_pairs={{0,2},{1,3},{2,0},{3,1},{4,6},{5,7},{6,4},{7,5},{8,10},{9,11},{10,... | collective-permute-start | bytes 589832 | tf_op jit(solution)/shard_map/ppermute | solution.py:510
  76.4 21.4 %collective-permute-start.23 = (f32[4,96,128]{2,1,0:T(8,128)S(1)}, f32[4,96,128]{2,1,0:T(8,128)S(1)}, u32[]{:S(2)}, u32[]{:S(2)}) collective-permute-start(f32[4,96,128]{2,1,0:T(8,128)S(1)} %pad_maximum_fusion.13), channel_id=1, source_target_pairs={{0,4},{1,5},{2,6},{3,7},{4,8},{5,9},{6,10},{7,11},{8,12},{9,13},{1... | collective-permute-start | bytes 589832 | tf_op jit(solution)/shard_map/ppermute | solution.py:510
  77.0 22.9 %collective-permute-start.24 = (f32[4,96,128]{2,1,0:T(8,128)S(1)}, f32[4,96,128]{2,1,0:T(8,128)S(1)}, u32[]{:S(2)}, u32[]{:S(2)}) collective-permute-start(f32[4,96,128]{2,1,0:T(8,128)S(1)} %pad_maximum_fusion.14), channel_id=1, source_target_pairs={{0,8},{1,9},{2,10},{3,11},{4,12},{5,13},{6,14},{7,15},{8,0},{9,1},... | collective-permute-start | bytes 589832 | tf_op jit(solution)/shard_map/ppermute | solution.py:510
  78.9 21.0 %collective-permute-start.25 = (f32[4,96,128]{2,1,0:T(8,128)S(1)}, f32[4,96,128]{2,1,0:T(8,128)S(1)}, u32[]{:S(2)}, u32[]{:S(2)}) collective-permute-start(f32[4,96,128]{2,1,0:T(8,128)S(1)} %pad_maximum_fusion.15), channel_id=1, source_target_pairs={{0,12},{1,13},{2,14},{3,15},{4,0},{5,1},{6,2},{7,3},{8,4},{9,5},{1... | collective-permute-start | bytes 589832 | tf_op jit(solution)/shard_map/ppermute | solution.py:510
  97.6 5.7 %collective-permute-start.17 = (f32[4,96,128]{2,1,0:T(8,128)S(1)}, f32[4,96,128]{2,1,0:T(8,128)S(1)}, u32[]{:S(2)}, u32[]{:S(2)}) collective-permute-start(f32[4,96,128]{2,1,0:T(8,128)S(1)} %pad_maximum_fusion.9), channel_id=1, source_target_pairs={{0,4},{1,5},{2,6},{3,7},{4,8},{5,9},{6,10},{7,11},{8,12},{9,13},{1... | collective-permute-start | bytes 589832 | tf_op jit(solution)/shard_map/ppermute | solution.py:510
  97.7 7.4 %collective-permute-start.18 = (f32[4,96,128]{2,1,0:T(8,128)S(1)}, f32[4,96,128]{2,1,0:T(8,128)S(1)}, u32[]{:S(2)}, u32[]{:S(2)}) collective-permute-start(f32[4,96,128]{2,1,0:T(8,128)S(1)} %pad_maximum_fusion.10), channel_id=1, source_target_pairs={{0,8},{1,9},{2,10},{3,11},{4,12},{5,13},{6,14},{7,15},{8,0},{9,1},... | collective-permute-start | bytes 589832 | tf_op jit(solution)/shard_map/ppermute | solution.py:510
  97.8 9.2 %collective-permute-start.19 = (f32[4,96,128]{2,1,0:T(8,128)S(1)}, f32[4,96,128]{2,1,0:T(8,128)S(1)}, u32[]{:S(2)}, u32[]{:S(2)}) collective-permute-start(f32[4,96,128]{2,1,0:T(8,128)S(1)} %pad_maximum_fusion.11), channel_id=1, source_target_pairs={{0,12},{1,13},{2,14},{3,15},{4,0},{5,1},{6,2},{7,3},{8,4},{9,5},{1... | collective-permute-start | bytes 589832 | tf_op jit(solution)/shard_map/ppermute | solution.py:510

commit v7 on v6

--- a/solution.py
+++ b/solution.py
@@ -88,7 +88,7 @@
         tracers, thickness, courant_x, courant_y, inside, across, _, out, held, mx, ax, my, ay, fy, sem = refs
     else:
         tracers, thickness, courant_x, courant_y, _, out, held, mx, ax, my, ay, fy, sem = refs
-    chunk = slots_to()
+    chunk = slots_to(False) if part == INNER else list(range(GROUPS))
     slots = slots_of(part)
     lane, row = lane_index(), row_index()
     view = held.reshape(NTR + 3, slots // part, part, TILES, LEVS, LANES)
@@ -354,26 +354,26 @@
     lax.fori_loop(0, 4, tail, 0)
 
 
-def place_of():
+def place_of(back):
     lev = lax.axis_index("lev")
-    return lev >> 2, lev & 3, on_odd_row()
-
-
-def slots_to():
-    y, z, odd = place_of()
+    return lev >> 2, lev & 3, on_odd_row() != back
+
+
+def slots_to(back):
+    y, z, y_first = place_of(back)
     slots = []
     for g in range(GROUPS):
         j, k = ((g >> 2) - y) & 3, (g & 3) ^ z
-        slots.append(jnp.where(odd, 4 * j + k, 4 * k + j))
+        slots.append(jnp.where(y_first, 4 * j + k, 4 * k + j))
     return slots
 
 
-def gather_chunks(given, target, sem):
-    y, z, odd = place_of()
+def gather_chunks(back, given, target, sem):
+    y, z, y_first = place_of(back)
     copies = []
     for a in range(4):
         for b in range(4):
-            j, k = jnp.where(odd, a, b), jnp.where(odd, b, a)
+            j, k = jnp.where(y_first, a, b), jnp.where(y_first, b, a)
             place = ((y - j) & 3) * 4 + (z ^ k)
             copies.append(pltpu.make_async_copy(given[b].at[a], target(place), sem.at[4 * a + b]))
     for copy in copies:
@@ -388,10 +388,10 @@
     def rows(place):
         return pl.ds(pl.multiple_of(place * DEPTH, 8), DEPTH)
 
-    gather_chunks(given, lambda place: data.at[rows(place)], sem)
+    gather_chunks(False, given, lambda place: data.at[rows(place)], sem)
     remap_rows(data, table, new)
     copies = []
-    for g, slot in enumerate(slots_to()):
+    for g, slot in enumerate(slots_to(True)):
         copies.append(pltpu.make_async_copy(new.at[rows(g)], out.at[slot], sem.at[g]))
     for copy in copies:
         copy.start()
@@ -400,8 +400,11 @@
 
 
 def collect_kernel(part, *refs):
-    given, (out, data, flat, sem) = refs[:4], refs[-4:]
-    gather_chunks(given, lambda place: data.at[place], sem)
+    if part == OUTER:
+        data, _, out, flat, sem = refs
+    else:
+        given, (out, data, flat, sem) = refs[:4], refs[-4:]
+        gather_chunks(True, given, lambda place: data.at[place], sem)
     lane = lane_index()
 
     def unpack(pair, at, block, slot):
@@ -469,7 +472,17 @@
     )(*given)
 
 
-def remap(given, table):
+def remap_outer(data, table):
+    return pl.pallas_call(
+        remap_rows,
+        out_shape=jax.ShapeDtypeStruct((GROUPS * DEPTH, LANES), F32),
+        in_specs=[IN_VMEM] * 2,
+        out_specs=IN_VMEM,
+        compiler_params=PARAMS,
+    )(data.reshape(GROUPS * DEPTH, LANES), table).reshape(GROUPS, DEPTH, LANES)
+
+
+def remap_inner(given, table):
     held = pltpu.VMEM((GROUPS * DEPTH, LANES), F32)
     return pl.pallas_call(
         remap_kernel,
@@ -482,28 +495,31 @@
 
 
 def collect(part, given, *result):
+    scratch = [pltpu.VMEM((FIELDS * 8 * STEP, LANES), F32), pltpu.SemaphoreType.DMA((2 * TILES,))]
+    if part == INNER:
+        scratch = [pltpu.VMEM((GROUPS, DEPTH, LANES), F32)] + scratch
     return pl.pallas_call(
         functools.partial(collect_kernel, part),
         out_shape=jax.ShapeDtypeStruct((FIELDS, ROWS, LEVS, LONS), F32),
-        in_specs=[ANYWHERE] * (4 + len(result)),
+        in_specs=[ANYWHERE] * 4 if part == INNER else [IN_VMEM, ANYWHERE],
         out_specs=ANYWHERE,
-        scratch_shapes=[
-            pltpu.VMEM((GROUPS, DEPTH, LANES), F32),
-            pltpu.VMEM((FIELDS * 8 * STEP, LANES), F32),
-            pltpu.SemaphoreType.DMA((2 * TILES,)),
-        ],
-        input_output_aliases={4: 0} if result else {},
+        scratch_shapes=scratch,
+        input_output_aliases={} if part == INNER else {1: 0},
         compiler_params=PARAMS,
     )(*given, *result)
 
 
-def hop(blocks, first):
+def exchange(data):
+    return lax.all_to_all(data, "lev", split_axis=0, concat_axis=0, tiled=True)
+
+
+def hop(blocks, evens_along_z):
     lats = lax.axis_size("lat")
     moved = {}
     for a in (2, 3, 1):
         pairs = []
         for lat in range(lats):
-            along_z = (lat % 2 == 0) == first
+            along_z = (lat % 2 == 0) == evens_along_z
             for lev in range(GROUPS):
                 target = lev ^ a if along_z else (lev + 4 * a) % GROUPS
                 pairs.append((lat * GROUPS + lev, lat * GROUPS + target))
@@ -511,12 +527,12 @@
     return [blocks[0]] + [moved[a] for a in range(1, 4)]
 
 
-def first_hop(data):
-    return hop([data[4 * a : 4 * a + 4] for a in range(4)], True)
-
-
-def second_hop(rows):
-    return hop([jnp.stack([rows[a][b] for a in range(4)]) for b in range(4)], False)
+def first_hop(data, back=False):
+    return hop([data[4 * a : 4 * a + 4] for a in range(4)], not back)
+
+
+def second_hop(rows, back=False):
+    return hop([jnp.stack([rows[a][b] for a in range(4)]) for b in range(4)], back)
 
 
 def after(values, *others):
@@ -549,14 +565,14 @@
     )(level_index, level_offset, level_phase)
     outer = transport(OUTER, *own, inside, across, outer_table)
     inner = first_hop(inner)
-    inner, outer = second_hop(after(inner, outer)), first_hop(outer)
-    inner = remap(inner, inner_table)
-    outer = second_hop(after(outer, inner))
-    inner = first_hop(inner)
-    outer = remap(outer, outer_table)
-    inner, outer = second_hop(after(inner, outer)), first_hop(outer)
-    outer = second_hop(outer)
-    return collect(OUTER, outer, collect(INNER, inner))
+    inner = second_hop(after(inner, outer))
+    outer = exchange(after(outer, inner[2]))
+    inner = remap_inner(inner, inner_table)
+    inner = first_hop(inner, True)
+    outer = remap_outer(after(outer, inner), outer_table)
+    inner = second_hop(inner, True)
+    outer = exchange(after(outer, inner[2]))
+    return collect(OUTER, [outer], collect(INNER, inner))
 
 
 def solution(mesh):

time: 110 us -> 108 us (0.982)
  the two profiles are of different devices: /device:TPU:14 before, /device:TPU:7 now
where the time goes in v7:
time: 108 us
  waiting for transfers between devices  43.6 us (40%)
  starting transfers between devices  35.9 us (33%)
  Pallas kernels  27.5 us (25%)
    ppermute x12, waiting for transfers between devices, hop(): moved[a] = lax.ppermute(blocks[a], ('lat', 'lev'), pairs)  34.8 us
    ppermute x12, starting transfers between devices, hop(): moved[a] = lax.ppermute(blocks[a], ('lat', 'lev'), pairs)  17 us
    pallas_call x2, Pallas kernels, transport(): pl.pallas_call(functools.partial(transport_kernel, part), out_shape=jax.S...  12.1 us
    all_to_all x2, starting transfers between devices, exchange(): return lax.all_to_all(data, 'lev', split_axis=0, concat_axis=0, tiled=True)  9.47 us
    ppermute x1, starting transfers between devices, shards(): lax.ppermute(across, 'lat', to_chip)  9.29 us
    all_to_all x2, waiting for transfers between devices, exchange(): return lax.all_to_all(data, 'lev', split_axis=0, concat_axis=0, tiled=True)  8.75 us
    pallas_call x2, Pallas kernels, collect(): pl.pallas_call(functools.partial(collect_kernel, part), out_shape=jax.Sha...  5 us
    pallas_call x1, Pallas kernels, remap_inner(): pl.pallas_call(remap_kernel, out_shape=jax.ShapeDtypeStruct((GROUPS, DEPT...  4.78 us
  transfers between devices with their start and end apart: 16, of which 6 were waited for; matrix products, arithmetic and copies ran while one was open for 0% of the time, Pallas kernels for 22%

profile of v7, /device:TPU:7, one launch (start us, length us, event | category | flops | bytes accessed | tf_op | source)
XLA Modules:
  0.0 107.7 jit_solution(2964056838902203278)
XLA Ops:
  0.0 1.8 %shard_map.73 = (f32[11,2,2,1152]{3,2,1,0:T(2,128)}, f32[11,2,2,1152]{3,2,1,0:T(2,128)}) custom-call(f32[9,16,2,1152]{3,2,1,0:T(2,128)} %refs_0_.3, f32[16,2,1152]{2,1,0:T(2,128)} %refs_1_.3, f32[16,2,1152]{2,1,0:T(2,128)} %refs_3_.3), custom_call_target="tpu_custom_call" | custom-call | tf_op jit(solution)/shard_map/pallas_call | solution.py:545
  1.8 9.3 %collective-permute-start.1 = (f32[11,2,2,1152]{3,2,1,0:T(2,128)}, f32[11,2,2,1152]{3,2,1,0:T(2,128)S(1)}, u32[]{:S(2)}, u32[]{:S(2)}) collective-permute-start(f32[11,2,2,1152]{3,2,1,0:T(2,128)} %get-tuple-element.17), channel_id=1, source_target_pairs={{16,32},{48,64},{80,96},{112,128},{144,160},{176,192},{208,224},{3... | collective-permute-start | bytes 608264 | tf_op jit(solution)/shard_map/ppermute | solution.py:556
  11.1 0.1 collective-permute-start
  11.2 5.6 %shard_map.76 = f32[16,96,128]{2,1,0:T(8,128)S(1)} custom-call(f32[9,16,2,1152]{3,2,1,0:T(2,128)} %refs_0_.3, f32[16,2,1152]{2,1,0:T(2,128)} %refs_1_.3, f32[16,2,1152]{2,1,0:T(2,128)} %refs_2_.3, f32[16,2,1152]{2,1,0:T(2,128)} %refs_3_.3, f32[11,2,2,1152]{3,2,1,0:T(2,128)} %get-tuple-element.16.refs_4_), custom_call_target="tpu_custom_call" | custom-call | tf_op jit(solution)/shard_map/pallas_call | solution.py:457
  16.9 0.0 copy-start
  16.9 0.0 copy-start.1
  16.9 0.0 copy-start.2
  16.9 0.1 fusion.2
  17.0 2.8 %collective-permute-start.4 = (f32[4,96,128]{2,1,0:T(8,128)S(1)}, f32[4,96,128]{2,1,0:T(8,128)S(1)}, u32[]{:S(2)}, u32[]{:S(2)}) collective-permute-start(f32[4,96,128]{2,1,0:T(8,128)S(1)} %get-tuple-element.34), channel_id=1, source_target_pairs={{0,3},{1,2},{2,1},{3,0},{4,7},{5,6},{6,5},{7,4},{8,11},{9,10},{10,... | collective-permute-start | bytes 589832 | tf_op jit(solution)/shard_map/ppermute | solution.py:526
  19.8 0.3 collective-permute-start.3
  20.2 0.7 collective-permute-start.2
  20.8 0.0 copy-done
  20.8 0.0 copy-done.1
  20.8 0.0 copy-done.2
  20.9 0.5 shard_map.74
  21.3 0.0 collective-permute-done.1.refs_5_
  21.3 0.0 collective-permute-done.refs_4_
  21.3 6.5 %shard_map.75 = f32[16,96,128]{2,1,0:T(8,128)} custom-call(f32[9,16,2,1152]{3,2,1,0:T(2,128)} %refs_0_.3, f32[16,2,1152]{2,1,0:T(2,128)} %refs_1_.3, f32[16,2,1152]{2,1,0:T(2,128)} %refs_2_.3, f32[16,2,1152]{2,1,0:T(2,128)} %refs_3_.3, f32[11,2,2,1152]{3,2,1,0:T(2,128)S(1)} %collective-permute-done.refs_4_, ...), custom_call_target="tpu_custom_call" | custom-call | tf_op jit(solution)/shard_map/pallas_call | solution.py:457
  27.8 0.0 collective-permute-done.4
  27.8 0.0 collective-permute-done.3
  27.8 0.2 collective-permute-done.2
  28.2 1.1 %collective-permute-start.5 = (f32[4,96,128]{2,1,0:T(8,128)S(1)}, f32[4,96,128]{2,1,0:T(8,128)S(1)}, u32[]{:S(2)}, u32[]{:S(2)}) collective-permute-start(f32[4,96,128]{2,1,0:T(8,128)S(1)} %pad_maximum_fusion), channel_id=1, source_target_pairs={{0,8},{1,9},{2,10},{3,11},{4,12},{5,13},{6,14},{7,15},{8,0},{9,1},... | collective-permute-start | bytes 589832 | tf_op jit(solution)/shard_map/ppermute | solution.py:526
  29.3 1.0 collective-permute-start.6
  30.3 1.7 %collective-permute-start.7 = (f32[4,96,128]{2,1,0:T(8,128)S(1)}, f32[4,96,128]{2,1,0:T(8,128)S(1)}, u32[]{:S(2)}, u32[]{:S(2)}) collective-permute-start(f32[4,96,128]{2,1,0:T(8,128)S(1)} %pad_maximum_fusion.3), channel_id=1, source_target_pairs={{0,12},{1,13},{2,14},{3,15},{4,0},{5,1},{6,2},{7,3},{8,4},{9,5},{1... | collective-permute-start | bytes 589832 | tf_op jit(solution)/shard_map/ppermute | solution.py:526
  32.0 4.1 %collective-permute-done.5.refs_2_ = f32[4,96,128]{2,1,0:T(8,128)S(1)} collective-permute-done((f32[4,96,128]{2,1,0:T(8,128)S(1)}, f32[4,96,128]{2,1,0:T(8,128)S(1)}, u32[]{:S(2)}, u32[]{:S(2)}) %collective-permute-start.5) | collective-permute-done | bytes 196640 | tf_op jit(solution)/shard_map/ppermute | solution.py:526
  36.1 4.5 %all-to-all-start = ((f32[16,96,128]{2,1,0:T(8,128)}), f32[16,96,128]{2,1,0:T(8,128)S(1)}, u32[]{:S(2)}, u32[]{:S(2)}) async-start(f32[16,96,128]{2,1,0:T(8,128)} %shard_map.75), calls=%async_computation | async-start | bytes 1572864 | tf_op jit(solution)/shard_map/all_to_all | solution.py:513
  40.6 0.0 collective-permute-done.6.refs_1_
  40.6 0.0 collective-permute-done.7.refs_3_
  40.6 4.8 %shard_map.77 = f32[16,96,128]{2,1,0:T(8,128)S(1)} custom-call(f32[4,96,128]{2,1,0:T(8,128)S(1)} %pad_maximum_fusion.1.refs_0_, f32[4,96,128]{2,1,0:T(8,128)S(1)} %collective-permute-done.6.refs_1_, f32[4,96,128]{2,1,0:T(8,128)S(1)} %collective-permute-done.5.refs_2_, f32[4,96,128]{2,1,0:T(8,128)S(1)} %collective-permute-done.7.refs_3_, ...), custom_call_target="tpu_custom_call" | custom-call | tf_op jit(solution)/shard_map/pallas_call | solution.py:487
  45.4 3.2 %collective-permute-start.10 = (f32[4,96,128]{2,1,0:T(8,128)S(1)}, f32[4,96,128]{2,1,0:T(8,128)S(1)}, u32[]{:S(2)}, u32[]{:S(2)}) collective-permute-start(f32[4,96,128]{2,1,0:T(8,128)S(1)} %get-tuple-element.31), channel_id=1, source_target_pairs={{0,12},{1,13},{2,14},{3,15},{4,0},{5,1},{6,2},{7,3},{8,4},{9,5},{1... | collective-permute-start | bytes 589832 | tf_op jit(solution)/shard_map/ppermute | solution.py:526
  48.7 0.0 collective-permute-start.9
  48.7 0.4 collective-permute-start.8
  49.1 9.8 %collective-permute-done.10 = f32[4,96,128]{2,1,0:T(8,128)S(1)} collective-permute-done((f32[4,96,128]{2,1,0:T(8,128)S(1)}, f32[4,96,128]{2,1,0:T(8,128)S(1)}, u32[]{:S(2)}, u32[]{:S(2)}) %collective-permute-start.10) | collective-permute-done | bytes 196640 | tf_op jit(solution)/shard_map/ppermute | solution.py:526
  58.9 14.6 %collective-permute-done.9 = f32[4,96,128]{2,1,0:T(8,128)S(1)} collective-permute-done((f32[4,96,128]{2,1,0:T(8,128)S(1)}, f32[4,96,128]{2,1,0:T(8,128)S(1)}, u32[]{:S(2)}, u32[]{:S(2)}) %collective-permute-start.9) | collective-permute-done | bytes 196640 | tf_op jit(solution)/shard_map/ppermute | solution.py:526
  73.6 0.0 collective-permute-done.8
  73.6 3.0 %collective-permute-start.11 = (f32[4,96,128]{2,1,0:T(8,128)S(1)}, f32[4,96,128]{2,1,0:T(8,128)S(1)}, u32[]{:S(2)}, u32[]{:S(2)}) collective-permute-start(f32[4,96,128]{2,1,0:T(8,128)S(1)} %pad_maximum_fusion.4), channel_id=1, source_target_pairs={{0,2},{1,3},{2,0},{3,1},{4,6},{5,7},{6,4},{7,5},{8,10},{9,11},{10,... | collective-permute-start | bytes 589832 | tf_op jit(solution)/shard_map/ppermute | solution.py:526
  76.6 0.0 all-to-all-done
  76.6 3.3 %shard_map.78 = f32[1536,128]{1,0:T(8,128)} custom-call(f32[1536,128]{1,0:T(8,128)S(1)} %bitcast.2, f32[512,128]{1,0:T(8,128)S(1)} %get-tuple-element.18.refs_6_.table), custom_call_target="tpu_custom_call" | custom-call | tf_op jit(solution)/shard_map/pallas_call | solution.py:476
  79.9 0.0 collective-permute-done.11.refs_2_
  79.9 5.0 %all-to-all-start.1 = ((f32[16,96,128]{2,1,0:T(8,128)}), f32[16,96,128]{2,1,0:T(8,128)S(1)}, u32[]{:S(2)}, u32[]{:S(2)}) async-start(f32[16,96,128]{2,1,0:T(8,128)} %bitcast.1), calls=%async_computation.1 | async-start | bytes 1572864 | tf_op jit(solution)/shard_map/all_to_all | solution.py:513
  84.9 1.4 %collective-permute-start.12 = (f32[4,96,128]{2,1,0:T(8,128)S(1)}, f32[4,96,128]{2,1,0:T(8,128)S(1)}, u32[]{:S(2)}, u32[]{:S(2)}) collective-permute-start(f32[4,96,128]{2,1,0:T(8,128)S(1)} %pad_maximum_fusion.6), channel_id=1, source_target_pairs={{0,1},{1,0},{2,3},{3,2},{4,5},{5,4},{6,7},{7,6},{8,9},{9,8},{10,11... | collective-permute-start | bytes 589832 | tf_op jit(solution)/shard_map/ppermute | solution.py:526
  86.4 1.4 %collective-permute-start.13 = (f32[4,96,128]{2,1,0:T(8,128)S(1)}, f32[4,96,128]{2,1,0:T(8,128)S(1)}, u32[]{:S(2)}, u32[]{:S(2)}) collective-permute-start(f32[4,96,128]{2,1,0:T(8,128)S(1)} %pad_maximum_fusion.7), channel_id=1, source_target_pairs={{0,3},{1,2},{2,1},{3,0},{4,7},{5,6},{6,5},{7,4},{8,11},{9,10},{10,... | collective-permute-start | bytes 589832 | tf_op jit(solution)/shard_map/ppermute | solution.py:526
  87.8 6.0 %collective-permute-done.12.refs_1_ = f32[4,96,128]{2,1,0:T(8,128)S(1)} collective-permute-done((f32[4,96,128]{2,1,0:T(8,128)S(1)}, f32[4,96,128]{2,1,0:T(8,128)S(1)}, u32[]{:S(2)}, u32[]{:S(2)}) %collective-permute-start.12) | collective-permute-done | bytes 196640 | tf_op jit(solution)/shard_map/ppermute | solution.py:526
  93.8 0.0 collective-permute-done.13.refs_3_
  93.8 3.1 %shard_map.79.refs_1_ = f32[10,16,2,1152]{3,2,1,0:T(2,128)} custom-call(f32[4,96,128]{2,1,0:T(8,128)S(1)} %pad_maximum_fusion.5.refs_0_, f32[4,96,128]{2,1,0:T(8,128)S(1)} %collective-permute-done.12.refs_1_, f32[4,96,128]{2,1,0:T(8,128)S(1)} %collective-permute-done.11.refs_2_, f32[4,96,128]{2,1,0:T(8,128)S(1)} %collective-permute-done.13.refs_3_), custom_call_target="tpu_custom_call" | custom-call | tf_op jit(solution)/shard_map/pallas_call | solution.py:501
  96.9 8.7 %all-to-all-done.1.refs_0_ = f32[16,96,128]{2,1,0:T(8,128)S(1)} async-done(((f32[16,96,128]{2,1,0:T(8,128)}), f32[16,96,128]{2,1,0:T(8,128)S(1)}, u32[]{:S(2)}, u32[]{:S(2)}) %all-to-all-start.1) | async-done | bytes 786464 | tf_op jit(solution)/shard_map/all_to_all | solution.py:513
  105.6 1.9 %shard_map.80 = f32[10,16,2,1152]{3,2,1,0:T(2,128)} custom-call(f32[16,96,128]{2,1,0:T(8,128)S(1)} %all-to-all-done.1.refs_0_, f32[10,16,2,1152]{3,2,1,0:T(2,128)} %shard_map.79.refs_1_), custom_call_target="tpu_custom_call", output_to_operand_aliasing={{}: (1, {})} | custom-call | tf_op jit(solution)/shard_map/pallas_call | solution.py:501
  (15 shorter events, 0.3 us)
Async XLA Ops:
  1.8 19.5 %collective-permute-start.1 = (f32[11,2,2,1152]{3,2,1,0:T(2,128)}, f32[11,2,2,1152]{3,2,1,0:T(2,128)S(1)}, u32[]{:S(2)}, u32[]{:S(2)}) collective-permute-start(f32[11,2,2,1152]{3,2,1,0:T(2,128)} %get-tuple-element.17), channel_id=1, source_target_pairs={{16,32},{48,64},{80,96},{112,128},{144,160},{176,192},{208,224},{3... | collective-permute-start | bytes 608264 | tf_op jit(solution)/shard_map/ppermute | solution.py:556
  11.1 10.2 %collective-permute-start = (f32[11,2,2,1152]{3,2,1,0:T(2,128)}, f32[11,2,2,1152]{3,2,1,0:T(2,128)S(1)}, u32[]{:S(2)}, u32[]{:S(2)}) collective-permute-start(f32[11,2,2,1152]{3,2,1,0:T(2,128)} %get-tuple-element.16.refs_4_), channel_id=1, source_target_pairs={{0,16},{16,0},{32,48},{48,32},{64,80},{80,64},{96,112},{112,96},{1... | collective-permute-start | bytes 608264 | tf_op jit(solution)/shard_map/ppermute | solution.py:556
  16.9 4.0 %copy-start = (s32[31,16,72]{2,1,0:T(8,128)S(1)}, s32[31,16,72]{2,1,0:T(8,128)}, u32[]{:S(2)}) copy-start(s32[31,16,72]{2,1,0:T(8,128)} %index.1) | copy-start | bytes 428548
  16.9 3.9 %copy-start.1 = (s32[31,16,72]{2,1,0:T(8,128)S(1)}, s32[31,16,72]{2,1,0:T(8,128)}, u32[]{:S(2)}) copy-start(s32[31,16,72]{2,1,0:T(8,128)} %offset.1) | copy-start | bytes 428548
  16.9 3.9 %copy-start.2 = (f32[31,16,72]{2,1,0:T(8,128)S(1)}, f32[31,16,72]{2,1,0:T(8,128)}, u32[]{:S(2)}) copy-start(f32[31,16,72]{2,1,0:T(8,128)} %phase.1) | copy-start | bytes 428548
  17.0 10.8 %collective-permute-start.4 = (f32[4,96,128]{2,1,0:T(8,128)S(1)}, f32[4,96,128]{2,1,0:T(8,128)S(1)}, u32[]{:S(2)}, u32[]{:S(2)}) collective-permute-start(f32[4,96,128]{2,1,0:T(8,128)S(1)} %get-tuple-element.34), channel_id=1, source_target_pairs={{0,3},{1,2},{2,1},{3,0},{4,7},{5,6},{6,5},{7,4},{8,11},{9,10},{10,... | collective-permute-start | bytes 589832 | tf_op jit(solution)/shard_map/ppermute | solution.py:526
  19.8 8.0 %collective-permute-start.3 = (f32[4,96,128]{2,1,0:T(8,128)S(1)}, f32[4,96,128]{2,1,0:T(8,128)S(1)}, u32[]{:S(2)}, u32[]{:S(2)}) collective-permute-start(f32[4,96,128]{2,1,0:T(8,128)S(1)} %get-tuple-element.35), channel_id=1, source_target_pairs={{0,2},{1,3},{2,0},{3,1},{4,6},{5,7},{6,4},{7,5},{8,10},{9,11},{10,... | collective-permute-start | bytes 589832 | tf_op jit(solution)/shard_map/ppermute | solution.py:526
  20.2 7.9 %collective-permute-start.2 = (f32[4,96,128]{2,1,0:T(8,128)S(1)}, f32[4,96,128]{2,1,0:T(8,128)S(1)}, u32[]{:S(2)}, u32[]{:S(2)}) collective-permute-start(f32[4,96,128]{2,1,0:T(8,128)S(1)} %get-tuple-element.36), channel_id=1, source_target_pairs={{0,1},{1,0},{2,3},{3,2},{4,5},{5,4},{6,7},{7,6},{8,9},{9,8},{10,11... | collective-permute-start | bytes 589832 | tf_op jit(solution)/shard_map/ppermute | solution.py:526
  28.2 7.9 %collective-permute-start.5 = (f32[4,96,128]{2,1,0:T(8,128)S(1)}, f32[4,96,128]{2,1,0:T(8,128)S(1)}, u32[]{:S(2)}, u32[]{:S(2)}) collective-permute-start(f32[4,96,128]{2,1,0:T(8,128)S(1)} %pad_maximum_fusion), channel_id=1, source_target_pairs={{0,8},{1,9},{2,10},{3,11},{4,12},{5,13},{6,14},{7,15},{8,0},{9,1},... | collective-permute-start | bytes 589832 | tf_op jit(solution)/shard_map/ppermute | solution.py:526
  29.3 11.3 %collective-permute-start.6 = (f32[4,96,128]{2,1,0:T(8,128)S(1)}, f32[4,96,128]{2,1,0:T(8,128)S(1)}, u32[]{:S(2)}, u32[]{:S(2)}) collective-permute-start(f32[4,96,128]{2,1,0:T(8,128)S(1)} %pad_maximum_fusion.2), channel_id=1, source_target_pairs={{0,4},{1,5},{2,6},{3,7},{4,8},{5,9},{6,10},{7,11},{8,12},{9,13},{1... | collective-permute-start | bytes 589832 | tf_op jit(solution)/shard_map/ppermute | solution.py:526
  30.3 10.3 %collective-permute-start.7 = (f32[4,96,128]{2,1,0:T(8,128)S(1)}, f32[4,96,128]{2,1,0:T(8,128)S(1)}, u32[]{:S(2)}, u32[]{:S(2)}) collective-permute-start(f32[4,96,128]{2,1,0:T(8,128)S(1)} %pad_maximum_fusion.3), channel_id=1, source_target_pairs={{0,12},{1,13},{2,14},{3,15},{4,0},{5,1},{6,2},{7,3},{8,4},{9,5},{1... | collective-permute-start | bytes 589832 | tf_op jit(solution)/shard_map/ppermute | solution.py:526
  36.1 40.5 %all-to-all-start = ((f32[16,96,128]{2,1,0:T(8,128)}), f32[16,96,128]{2,1,0:T(8,128)S(1)}, u32[]{:S(2)}, u32[]{:S(2)}) async-start(f32[16,96,128]{2,1,0:T(8,128)} %shard_map.75), calls=%async_computation | async-start | bytes 1572864 | tf_op jit(solution)/shard_map/all_to_all | solution.py:513
  45.4 13.4 %collective-permute-start.10 = (f32[4,96,128]{2,1,0:T(8,128)S(1)}, f32[4,96,128]{2,1,0:T(8,128)S(1)}, u32[]{:S(2)}, u32[]{:S(2)}) collective-permute-start(f32[4,96,128]{2,1,0:T(8,128)S(1)} %get-tuple-element.31), channel_id=1, source_target_pairs={{0,12},{1,13},{2,14},{3,15},{4,0},{5,1},{6,2},{7,3},{8,4},{9,5},{1... | collective-permute-start | bytes 589832 | tf_op jit(solution)/shard_map/ppermute | solution.py:526
  48.7 24.9 %collective-permute-start.9 = (f32[4,96,128]{2,1,0:T(8,128)S(1)}, f32[4,96,128]{2,1,0:T(8,128)S(1)}, u32[]{:S(2)}, u32[]{:S(2)}) collective-permute-start(f32[4,96,128]{2,1,0:T(8,128)S(1)} %get-tuple-element.32), channel_id=1, source_target_pairs={{0,8},{1,9},{2,10},{3,11},{4,12},{5,13},{6,14},{7,15},{8,0},{9,1},... | collective-permute-start | bytes 589832 | tf_op jit(solution)/shard_map/ppermute | solution.py:526
  48.7 24.9 %collective-permute-start.8 = (f32[4,96,128]{2,1,0:T(8,128)S(1)}, f32[4,96,128]{2,1,0:T(8,128)S(1)}, u32[]{:S(2)}, u32[]{:S(2)}) collective-permute-start(f32[4,96,128]{2,1,0:T(8,128)S(1)} %get-tuple-element.33), channel_id=1, source_target_pairs={{0,4},{1,5},{2,6},{3,7},{4,8},{5,9},{6,10},{7,11},{8,12},{9,13},{1... | collective-permute-start | bytes 589832 | tf_op jit(solution)/shard_map/ppermute | solution.py:526
  73.6 6.3 %collective-permute-start.11 = (f32[4,96,128]{2,1,0:T(8,128)S(1)}, f32[4,96,128]{2,1,0:T(8,128)S(1)}, u32[]{:S(2)}, u32[]{:S(2)}) collective-permute-start(f32[4,96,128]{2,1,0:T(8,128)S(1)} %pad_maximum_fusion.4), channel_id=1, source_target_pairs={{0,2},{1,3},{2,0},{3,1},{4,6},{5,7},{6,4},{7,5},{8,10},{9,11},{10,... | collective-permute-start | bytes 589832 | tf_op jit(solution)/shard_map/ppermute | solution.py:526
  79.9 25.7 %all-to-all-start.1 = ((f32[16,96,128]{2,1,0:T(8,128)}), f32[16,96,128]{2,1,0:T(8,128)S(1)}, u32[]{:S(2)}, u32[]{:S(2)}) async-start(f32[16,96,128]{2,1,0:T(8,128)} %bitcast.1), calls=%async_computation.1 | async-start | bytes 1572864 | tf_op jit(solution)/shard_map/all_to_all | solution.py:513
  84.9 8.9 %collective-permute-start.12 = (f32[4,96,128]{2,1,0:T(8,128)S(1)}, f32[4,96,128]{2,1,0:T(8,128)S(1)}, u32[]{:S(2)}, u32[]{:S(2)}) collective-permute-start(f32[4,96,128]{2,1,0:T(8,128)S(1)} %pad_maximum_fusion.6), channel_id=1, source_target_pairs={{0,1},{1,0},{2,3},{3,2},{4,5},{5,4},{6,7},{7,6},{8,9},{9,8},{10,11... | collective-permute-start | bytes 589832 | tf_op jit(solution)/shard_map/ppermute | solution.py:526
  86.4 7.4 %collective-permute-start.13 = (f32[4,96,128]{2,1,0:T(8,128)S(1)}, f32[4,96,128]{2,1,0:T(8,128)S(1)}, u32[]{:S(2)}, u32[]{:S(2)}) collective-permute-start(f32[4,96,128]{2,1,0:T(8,128)S(1)} %pad_maximum_fusion.7), channel_id=1, source_target_pairs={{0,3},{1,2},{2,1},{3,0},{4,7},{5,6},{6,5},{7,4},{8,11},{9,10},{10,... | collective-permute-start | bytes 589832 | tf_op jit(solution)/shard_map/ppermute | solution.py:526

commit v8 on v7

--- a/solution.py
+++ b/solution.py
@@ -565,13 +565,11 @@
     )(level_index, level_offset, level_phase)
     outer = transport(OUTER, *own, inside, across, outer_table)
     inner = first_hop(inner)
-    inner = second_hop(after(inner, outer))
-    outer = exchange(after(outer, inner[2]))
+    inner, outer = second_hop(after(inner, outer)), exchange(outer)
     inner = remap_inner(inner, inner_table)
+    outer = remap_outer(after(outer, inner), outer_table)
     inner = first_hop(inner, True)
-    outer = remap_outer(after(outer, inner), outer_table)
-    inner = second_hop(inner, True)
-    outer = exchange(after(outer, inner[2]))
+    inner, outer = second_hop(after(inner, outer), True), exchange(outer)
     return collect(OUTER, [outer], collect(INNER, inner))
 
 

time: 108 us -> 106 us (0.981)
  waiting for transfers between devices: 43.6 us -> 41.2 us
    all_to_all x2, waiting for transfers between devices: 8.75 us -> 2.37 us  [exchange(): return lax.all_to_all(data, 'lev', split_axis=0, concat_axis=0, tiled=True)]
    ppermute x12, waiting for transfers between devices: 34.8 us -> 38.8 us  [hop(): moved[a] = lax.ppermute(blocks[a], ('lat', 'lev'), pairs)]
where the time goes in v8:
time: 106 us
  waiting for transfers between devices  41.2 us (39%)
  starting transfers between devices  36.1 us (34%)
  Pallas kernels  27.5 us (26%)
    ppermute x12, waiting for transfers between devices, hop(): moved[a] = lax.ppermute(blocks[a], ('lat', 'lev'), pairs)  38.8 us
    ppermute x12, starting transfers between devices, hop(): moved[a] = lax.ppermute(blocks[a], ('lat', 'lev'), pairs)  16.5 us
    pallas_call x2, Pallas kernels, transport(): pl.pallas_call(functools.partial(transport_kernel, part), out_shape=jax.S...  12.1 us
    all_to_all x2, starting transfers between devices, exchange(): return lax.all_to_all(data, 'lev', split_axis=0, concat_axis=0, tiled=True)  10.3 us
    ppermute x1, starting transfers between devices, shards(): lax.ppermute(across, 'lat', to_chip)  9.29 us
    pallas_call x2, Pallas kernels, collect(): pl.pallas_call(functools.partial(collect_kernel, part), out_shape=jax.Sha...  5 us
    pallas_call x1, Pallas kernels, remap_inner(): pl.pallas_call(remap_kernel, out_shape=jax.ShapeDtypeStruct((GROUPS, DEPT...  4.72 us
    pallas_call x1, Pallas kernels, remap_outer(): pl.pallas_call(remap_rows, out_shape=jax.ShapeDtypeStruct((GROUPS * DEPTH...  3.33 us
  transfers between devices with their start and end apart: 16, of which 6 were waited for; matrix products, arithmetic and copies ran while one was open for 0% of the time, Pallas kernels for 22%

profile of v8, /device:TPU:7, one launch (start us, length us, event | category | flops | bytes accessed | tf_op | source)
XLA Modules:
  0.0 105.5 jit_solution(3413762297019028036)
XLA Ops:
  0.0 1.8 %shard_map.73 = (f32[11,2,2,1152]{3,2,1,0:T(2,128)}, f32[11,2,2,1152]{3,2,1,0:T(2,128)}) custom-call(f32[9,16,2,1152]{3,2,1,0:T(2,128)} %refs_0_.3, f32[16,2,1152]{2,1,0:T(2,128)} %refs_1_.3, f32[16,2,1152]{2,1,0:T(2,128)} %refs_3_.3), custom_call_target="tpu_custom_call" | custom-call | tf_op jit(solution)/shard_map/pallas_call | solution.py:545
  1.8 9.3 %collective-permute-start.1 = (f32[11,2,2,1152]{3,2,1,0:T(2,128)}, f32[11,2,2,1152]{3,2,1,0:T(2,128)S(1)}, u32[]{:S(2)}, u32[]{:S(2)}) collective-permute-start(f32[11,2,2,1152]{3,2,1,0:T(2,128)} %get-tuple-element.19), channel_id=1, source_target_pairs={{16,32},{48,64},{80,96},{112,128},{144,160},{176,192},{208,224},{3... | collective-permute-start | bytes 608264 | tf_op jit(solution)/shard_map/ppermute | solution.py:556
  11.1 0.1 collective-permute-start
  11.2 5.6 %shard_map.76 = f32[16,96,128]{2,1,0:T(8,128)S(1)} custom-call(f32[9,16,2,1152]{3,2,1,0:T(2,128)} %refs_0_.3, f32[16,2,1152]{2,1,0:T(2,128)} %refs_1_.3, f32[16,2,1152]{2,1,0:T(2,128)} %refs_2_.3, f32[16,2,1152]{2,1,0:T(2,128)} %refs_3_.3, f32[11,2,2,1152]{3,2,1,0:T(2,128)} %get-tuple-element.18.refs_4_), custom_call_target="tpu_custom_call" | custom-call | tf_op jit(solution)/shard_map/pallas_call | solution.py:457
  16.9 0.0 copy-start
  16.9 0.0 copy-start.1
  16.9 0.0 copy-start.2
  16.9 0.1 fusion.1
  17.0 2.8 %collective-permute-start.4 = (f32[4,96,128]{2,1,0:T(8,128)S(1)}, f32[4,96,128]{2,1,0:T(8,128)S(1)}, u32[]{:S(2)}, u32[]{:S(2)}) collective-permute-start(f32[4,96,128]{2,1,0:T(8,128)S(1)} %get-tuple-element.35), channel_id=1, source_target_pairs={{0,3},{1,2},{2,1},{3,0},{4,7},{5,6},{6,5},{7,4},{8,11},{9,10},{10,... | collective-permute-start | bytes 589832 | tf_op jit(solution)/shard_map/ppermute | solution.py:526
  19.8 0.3 collective-permute-start.3
  20.2 0.7 collective-permute-start.2
  20.8 0.0 copy-done
  20.8 0.0 copy-done.1
  20.8 0.0 copy-done.2
  20.9 0.5 shard_map.74
  21.3 0.0 collective-permute-done.1.refs_5_
  21.3 0.0 collective-permute-done.refs_4_
  21.3 6.5 %shard_map.75 = f32[16,96,128]{2,1,0:T(8,128)} custom-call(f32[9,16,2,1152]{3,2,1,0:T(2,128)} %refs_0_.3, f32[16,2,1152]{2,1,0:T(2,128)} %refs_1_.3, f32[16,2,1152]{2,1,0:T(2,128)} %refs_2_.3, f32[16,2,1152]{2,1,0:T(2,128)} %refs_3_.3, f32[11,2,2,1152]{3,2,1,0:T(2,128)S(1)} %collective-permute-done.refs_4_, ...), custom_call_target="tpu_custom_call" | custom-call | tf_op jit(solution)/shard_map/pallas_call | solution.py:457
  27.8 4.7 %all-to-all-start = ((f32[16,96,128]{2,1,0:T(8,128)}), f32[16,96,128]{2,1,0:T(8,128)S(1)}, u32[]{:S(2)}, u32[]{:S(2)}) async-start(f32[16,96,128]{2,1,0:T(8,128)} %shard_map.75), calls=%async_computation | async-start | bytes 1572864 | tf_op jit(solution)/shard_map/all_to_all | solution.py:513
  32.6 0.0 collective-permute-done.4
  32.6 0.0 collective-permute-done.3
  32.6 0.0 collective-permute-done.2
  32.7 1.4 %collective-permute-start.5 = (f32[4,96,128]{2,1,0:T(8,128)S(1)}, f32[4,96,128]{2,1,0:T(8,128)S(1)}, u32[]{:S(2)}, u32[]{:S(2)}) collective-permute-start(f32[4,96,128]{2,1,0:T(8,128)S(1)} %pad_maximum_fusion.1), channel_id=1, source_target_pairs={{0,4},{1,5},{2,6},{3,7},{4,8},{5,9},{6,10},{7,11},{8,12},{9,13},{1... | collective-permute-start | bytes 589832 | tf_op jit(solution)/shard_map/ppermute | solution.py:526
  34.1 2.2 %collective-permute-start.6 = (f32[4,96,128]{2,1,0:T(8,128)S(1)}, f32[4,96,128]{2,1,0:T(8,128)S(1)}, u32[]{:S(2)}, u32[]{:S(2)}) collective-permute-start(f32[4,96,128]{2,1,0:T(8,128)S(1)} %pad_maximum_fusion.2), channel_id=1, source_target_pairs={{0,8},{1,9},{2,10},{3,11},{4,12},{5,13},{6,14},{7,15},{8,0},{9,1},... | collective-permute-start | bytes 589832 | tf_op jit(solution)/shard_map/ppermute | solution.py:526
  36.3 0.2 collective-permute-start.7
  36.5 12.0 %collective-permute-done.5.refs_1_ = f32[4,96,128]{2,1,0:T(8,128)S(1)} collective-permute-done((f32[4,96,128]{2,1,0:T(8,128)S(1)}, f32[4,96,128]{2,1,0:T(8,128)S(1)}, u32[]{:S(2)}, u32[]{:S(2)}) %collective-permute-start.5) | collective-permute-done | bytes 196640 | tf_op jit(solution)/shard_map/ppermute | solution.py:526
  48.5 10.7 %collective-permute-done.6.refs_2_ = f32[4,96,128]{2,1,0:T(8,128)S(1)} collective-permute-done((f32[4,96,128]{2,1,0:T(8,128)S(1)}, f32[4,96,128]{2,1,0:T(8,128)S(1)}, u32[]{:S(2)}, u32[]{:S(2)}) %collective-permute-start.6) | collective-permute-done | bytes 196640 | tf_op jit(solution)/shard_map/ppermute | solution.py:526
  59.2 0.0 collective-permute-done.7.refs_3_
  59.2 4.7 %shard_map.77 = f32[16,96,128]{2,1,0:T(8,128)S(1)} custom-call(f32[4,96,128]{2,1,0:T(8,128)S(1)} %pad_maximum_fusion.refs_0_, f32[4,96,128]{2,1,0:T(8,128)S(1)} %collective-permute-done.5.refs_1_, f32[4,96,128]{2,1,0:T(8,128)S(1)} %collective-permute-done.6.refs_2_, f32[4,96,128]{2,1,0:T(8,128)S(1)} %collective-permute-done.7.refs_3_, ...), custom_call_target="tpu_custom_call" | custom-call | tf_op jit(solution)/shard_map/pallas_call | solution.py:487
  63.9 0.1 fusion
  64.0 0.9 collective-permute-start.10
  64.9 2.7 %collective-permute-start.9 = (f32[4,96,128]{2,1,0:T(8,128)S(1)}, f32[4,96,128]{2,1,0:T(8,128)S(1)}, u32[]{:S(2)}, u32[]{:S(2)}) collective-permute-start(f32[4,96,128]{2,1,0:T(8,128)S(1)} %get-tuple-element.32), channel_id=1, source_target_pairs={{0,8},{1,9},{2,10},{3,11},{4,12},{5,13},{6,14},{7,15},{8,0},{9,1},... | collective-permute-start | bytes 589832 | tf_op jit(solution)/shard_map/ppermute | solution.py:526
  67.6 0.0 collective-permute-start.8
  67.6 0.0 all-to-all-done
  67.6 3.3 %shard_map.78 = f32[1536,128]{1,0:T(8,128)} custom-call(f32[1536,128]{1,0:T(8,128)S(1)} %bitcast.2, f32[512,128]{1,0:T(8,128)S(1)} %get-tuple-element.20.refs_6_.table), custom_call_target="tpu_custom_call" | custom-call | tf_op jit(solution)/shard_map/pallas_call | solution.py:476
  71.0 5.5 %all-to-all-start.1 = ((f32[16,96,128]{2,1,0:T(8,128)}), f32[16,96,128]{2,1,0:T(8,128)S(1)}, u32[]{:S(2)}, u32[]{:S(2)}) async-start(f32[16,96,128]{2,1,0:T(8,128)} %bitcast.1), calls=%async_computation.1 | async-start | bytes 1572864 | tf_op jit(solution)/shard_map/all_to_all | solution.py:513
  76.5 0.0 collective-permute-done.10
  76.5 11.2 %collective-permute-done.9 = f32[4,96,128]{2,1,0:T(8,128)S(1)} collective-permute-done((f32[4,96,128]{2,1,0:T(8,128)S(1)}, f32[4,96,128]{2,1,0:T(8,128)S(1)}, u32[]{:S(2)}, u32[]{:S(2)}) %collective-permute-start.9) | collective-permute-done | bytes 196640 | tf_op jit(solution)/shard_map/ppermute | solution.py:526
  87.7 0.0 collective-permute-done.8
  87.8 1.4 %collective-permute-start.11 = (f32[4,96,128]{2,1,0:T(8,128)S(1)}, f32[4,96,128]{2,1,0:T(8,128)S(1)}, u32[]{:S(2)}, u32[]{:S(2)}) collective-permute-start(f32[4,96,128]{2,1,0:T(8,128)S(1)} %pad_maximum_fusion.5), channel_id=1, source_target_pairs={{0,1},{1,0},{2,3},{3,2},{4,5},{5,4},{6,7},{7,6},{8,9},{9,8},{10,11... | collective-permute-start | bytes 589832 | tf_op jit(solution)/shard_map/ppermute | solution.py:526
  89.3 3.0 %collective-permute-start.12 = (f32[4,96,128]{2,1,0:T(8,128)S(1)}, f32[4,96,128]{2,1,0:T(8,128)S(1)}, u32[]{:S(2)}, u32[]{:S(2)}) collective-permute-start(f32[4,96,128]{2,1,0:T(8,128)S(1)} %pad_maximum_fusion.6), channel_id=1, source_target_pairs={{0,2},{1,3},{2,0},{3,1},{4,6},{5,7},{6,4},{7,5},{8,10},{9,11},{10,... | collective-permute-start | bytes 589832 | tf_op jit(solution)/shard_map/ppermute | solution.py:526
  92.3 0.7 collective-permute-start.13
  93.0 1.7 %collective-permute-done.11.refs_1_ = f32[4,96,128]{2,1,0:T(8,128)S(1)} collective-permute-done((f32[4,96,128]{2,1,0:T(8,128)S(1)}, f32[4,96,128]{2,1,0:T(8,128)S(1)}, u32[]{:S(2)}, u32[]{:S(2)}) %collective-permute-start.11) | collective-permute-done | bytes 196640 | tf_op jit(solution)/shard_map/ppermute | solution.py:526
  94.7 3.2 %collective-permute-done.12.refs_2_ = f32[4,96,128]{2,1,0:T(8,128)S(1)} collective-permute-done((f32[4,96,128]{2,1,0:T(8,128)S(1)}, f32[4,96,128]{2,1,0:T(8,128)S(1)}, u32[]{:S(2)}, u32[]{:S(2)}) %collective-permute-start.12) | collective-permute-done | bytes 196640 | tf_op jit(solution)/shard_map/ppermute | solution.py:526
  98.0 0.0 collective-permute-done.13.refs_3_
  98.0 3.1 %shard_map.79.refs_1_ = f32[10,16,2,1152]{3,2,1,0:T(2,128)} custom-call(f32[4,96,128]{2,1,0:T(8,128)S(1)} %pad_maximum_fusion.4.refs_0_, f32[4,96,128]{2,1,0:T(8,128)S(1)} %collective-permute-done.11.refs_1_, f32[4,96,128]{2,1,0:T(8,128)S(1)} %collective-permute-done.12.refs_2_, f32[4,96,128]{2,1,0:T(8,128)S(1)} %collective-permute-done.13.refs_3_), custom_call_target="tpu_custom_call" | custom-call | tf_op jit(solution)/shard_map/pallas_call | solution.py:501
  101.1 2.4 %all-to-all-done.1.refs_0_ = f32[16,96,128]{2,1,0:T(8,128)S(1)} async-done(((f32[16,96,128]{2,1,0:T(8,128)}), f32[16,96,128]{2,1,0:T(8,128)S(1)}, u32[]{:S(2)}, u32[]{:S(2)}) %all-to-all-start.1) | async-done | bytes 786464 | tf_op jit(solution)/shard_map/all_to_all | solution.py:513
  103.4 1.9 %shard_map.80 = f32[10,16,2,1152]{3,2,1,0:T(2,128)} custom-call(f32[16,96,128]{2,1,0:T(8,128)S(1)} %all-to-all-done.1.refs_0_, f32[10,16,2,1152]{3,2,1,0:T(2,128)} %shard_map.79.refs_1_), custom_call_target="tpu_custom_call", output_to_operand_aliasing={{}: (1, {})} | custom-call | tf_op jit(solution)/shard_map/pallas_call | solution.py:501
  (14 shorter events, 0.2 us)
Async XLA Ops:
  1.8 19.5 %collective-permute-start.1 = (f32[11,2,2,1152]{3,2,1,0:T(2,128)}, f32[11,2,2,1152]{3,2,1,0:T(2,128)S(1)}, u32[]{:S(2)}, u32[]{:S(2)}) collective-permute-start(f32[11,2,2,1152]{3,2,1,0:T(2,128)} %get-tuple-element.19), channel_id=1, source_target_pairs={{16,32},{48,64},{80,96},{112,128},{144,160},{176,192},{208,224},{3... | collective-permute-start | bytes 608264 | tf_op jit(solution)/shard_map/ppermute | solution.py:556
  11.1 10.2 %collective-permute-start = (f32[11,2,2,1152]{3,2,1,0:T(2,128)}, f32[11,2,2,1152]{3,2,1,0:T(2,128)S(1)}, u32[]{:S(2)}, u32[]{:S(2)}) collective-permute-start(f32[11,2,2,1152]{3,2,1,0:T(2,128)} %get-tuple-element.18.refs_4_), channel_id=1, source_target_pairs={{0,16},{16,0},{32,48},{48,32},{64,80},{80,64},{96,112},{112,96},{1... | collective-permute-start | bytes 608264 | tf_op jit(solution)/shard_map/ppermute | solution.py:556
  16.9 4.0 %copy-start = (s32[31,16,72]{2,1,0:T(8,128)S(1)}, s32[31,16,72]{2,1,0:T(8,128)}, u32[]{:S(2)}) copy-start(s32[31,16,72]{2,1,0:T(8,128)} %index.1) | copy-start | bytes 428548
  16.9 3.9 %copy-start.1 = (s32[31,16,72]{2,1,0:T(8,128)S(1)}, s32[31,16,72]{2,1,0:T(8,128)}, u32[]{:S(2)}) copy-start(s32[31,16,72]{2,1,0:T(8,128)} %offset.1) | copy-start | bytes 428548
  16.9 3.9 %copy-start.2 = (f32[31,16,72]{2,1,0:T(8,128)S(1)}, f32[31,16,72]{2,1,0:T(8,128)}, u32[]{:S(2)}) copy-start(f32[31,16,72]{2,1,0:T(8,128)} %phase.1) | copy-start | bytes 428548
  17.0 15.6 %collective-permute-start.4 = (f32[4,96,128]{2,1,0:T(8,128)S(1)}, f32[4,96,128]{2,1,0:T(8,128)S(1)}, u32[]{:S(2)}, u32[]{:S(2)}) collective-permute-start(f32[4,96,128]{2,1,0:T(8,128)S(1)} %get-tuple-element.35), channel_id=1, source_target_pairs={{0,3},{1,2},{2,1},{3,0},{4,7},{5,6},{6,5},{7,4},{8,11},{9,10},{10,... | collective-permute-start | bytes 589832 | tf_op jit(solution)/shard_map/ppermute | solution.py:526
  19.8 12.8 %collective-permute-start.3 = (f32[4,96,128]{2,1,0:T(8,128)S(1)}, f32[4,96,128]{2,1,0:T(8,128)S(1)}, u32[]{:S(2)}, u32[]{:S(2)}) collective-permute-start(f32[4,96,128]{2,1,0:T(8,128)S(1)} %get-tuple-element.36), channel_id=1, source_target_pairs={{0,2},{1,3},{2,0},{3,1},{4,6},{5,7},{6,4},{7,5},{8,10},{9,11},{10,... | collective-permute-start | bytes 589832 | tf_op jit(solution)/shard_map/ppermute | solution.py:526
  20.2 12.4 %collective-permute-start.2 = (f32[4,96,128]{2,1,0:T(8,128)S(1)}, f32[4,96,128]{2,1,0:T(8,128)S(1)}, u32[]{:S(2)}, u32[]{:S(2)}) collective-permute-start(f32[4,96,128]{2,1,0:T(8,128)S(1)} %get-tuple-element.37), channel_id=1, source_target_pairs={{0,1},{1,0},{2,3},{3,2},{4,5},{5,4},{6,7},{7,6},{8,9},{9,8},{10,11... | collective-permute-start | bytes 589832 | tf_op jit(solution)/shard_map/ppermute | solution.py:526
  27.8 39.8 %all-to-all-start = ((f32[16,96,128]{2,1,0:T(8,128)}), f32[16,96,128]{2,1,0:T(8,128)S(1)}, u32[]{:S(2)}, u32[]{:S(2)}) async-start(f32[16,96,128]{2,1,0:T(8,128)} %shard_map.75), calls=%async_computation | async-start | bytes 1572864 | tf_op jit(solution)/shard_map/all_to_all | solution.py:513
  32.7 15.9 %collective-permute-start.5 = (f32[4,96,128]{2,1,0:T(8,128)S(1)}, f32[4,96,128]{2,1,0:T(8,128)S(1)}, u32[]{:S(2)}, u32[]{:S(2)}) collective-permute-start(f32[4,96,128]{2,1,0:T(8,128)S(1)} %pad_maximum_fusion.1), channel_id=1, source_target_pairs={{0,4},{1,5},{2,6},{3,7},{4,8},{5,9},{6,10},{7,11},{8,12},{9,13},{1... | collective-permute-start | bytes 589832 | tf_op jit(solution)/shard_map/ppermute | solution.py:526
  34.1 25.1 %collective-permute-start.6 = (f32[4,96,128]{2,1,0:T(8,128)S(1)}, f32[4,96,128]{2,1,0:T(8,128)S(1)}, u32[]{:S(2)}, u32[]{:S(2)}) collective-permute-start(f32[4,96,128]{2,1,0:T(8,128)S(1)} %pad_maximum_fusion.2), channel_id=1, source_target_pairs={{0,8},{1,9},{2,10},{3,11},{4,12},{5,13},{6,14},{7,15},{8,0},{9,1},... | collective-permute-start | bytes 589832 | tf_op jit(solution)/shard_map/ppermute | solution.py:526
  36.3 22.9 %collective-permute-start.7 = (f32[4,96,128]{2,1,0:T(8,128)S(1)}, f32[4,96,128]{2,1,0:T(8,128)S(1)}, u32[]{:S(2)}, u32[]{:S(2)}) collective-permute-start(f32[4,96,128]{2,1,0:T(8,128)S(1)} %pad_maximum_fusion.3), channel_id=1, source_target_pairs={{0,12},{1,13},{2,14},{3,15},{4,0},{5,1},{6,2},{7,3},{8,4},{9,5},{1... | collective-permute-start | bytes 589832 | tf_op jit(solution)/shard_map/ppermute | solution.py:526
  64.0 12.5 %collective-permute-start.10 = (f32[4,96,128]{2,1,0:T(8,128)S(1)}, f32[4,96,128]{2,1,0:T(8,128)S(1)}, u32[]{:S(2)}, u32[]{:S(2)}) collective-permute-start(f32[4,96,128]{2,1,0:T(8,128)S(1)} %get-tuple-element.31), channel_id=1, source_target_pairs={{0,12},{1,13},{2,14},{3,15},{4,0},{5,1},{6,2},{7,3},{8,4},{9,5},{1... | collective-permute-start | bytes 589832 | tf_op jit(solution)/shard_map/ppermute | solution.py:526
  64.9 22.8 %collective-permute-start.9 = (f32[4,96,128]{2,1,0:T(8,128)S(1)}, f32[4,96,128]{2,1,0:T(8,128)S(1)}, u32[]{:S(2)}, u32[]{:S(2)}) collective-permute-start(f32[4,96,128]{2,1,0:T(8,128)S(1)} %get-tuple-element.32), channel_id=1, source_target_pairs={{0,8},{1,9},{2,10},{3,11},{4,12},{5,13},{6,14},{7,15},{8,0},{9,1},... | collective-permute-start | bytes 589832 | tf_op jit(solution)/shard_map/ppermute | solution.py:526
  67.6 20.1 %collective-permute-start.8 = (f32[4,96,128]{2,1,0:T(8,128)S(1)}, f32[4,96,128]{2,1,0:T(8,128)S(1)}, u32[]{:S(2)}, u32[]{:S(2)}) collective-permute-start(f32[4,96,128]{2,1,0:T(8,128)S(1)} %get-tuple-element.33), channel_id=1, source_target_pairs={{0,4},{1,5},{2,6},{3,7},{4,8},{5,9},{6,10},{7,11},{8,12},{9,13},{1... | collective-permute-start | bytes 589832 | tf_op jit(solution)/shard_map/ppermute | solution.py:526
  71.0 32.5 %all-to-all-start.1 = ((f32[16,96,128]{2,1,0:T(8,128)}), f32[16,96,128]{2,1,0:T(8,128)S(1)}, u32[]{:S(2)}, u32[]{:S(2)}) async-start(f32[16,96,128]{2,1,0:T(8,128)} %bitcast.1), calls=%async_computation.1 | async-start | bytes 1572864 | tf_op jit(solution)/shard_map/all_to_all | solution.py:513
  87.8 6.9 %collective-permute-start.11 = (f32[4,96,128]{2,1,0:T(8,128)S(1)}, f32[4,96,128]{2,1,0:T(8,128)S(1)}, u32[]{:S(2)}, u32[]{:S(2)}) collective-permute-start(f32[4,96,128]{2,1,0:T(8,128)S(1)} %pad_maximum_fusion.5), channel_id=1, source_target_pairs={{0,1},{1,0},{2,3},{3,2},{4,5},{5,4},{6,7},{7,6},{8,9},{9,8},{10,11... | collective-permute-start | bytes 589832 | tf_op jit(solution)/shard_map/ppermute | solution.py:526
  89.3 8.7 %collective-permute-start.12 = (f32[4,96,128]{2,1,0:T(8,128)S(1)}, f32[4,96,128]{2,1,0:T(8,128)S(1)}, u32[]{:S(2)}, u32[]{:S(2)}) collective-permute-start(f32[4,96,128]{2,1,0:T(8,128)S(1)} %pad_maximum_fusion.6), channel_id=1, source_target_pairs={{0,2},{1,3},{2,0},{3,1},{4,6},{5,7},{6,4},{7,5},{8,10},{9,11},{10,... | collective-permute-start | bytes 589832 | tf_op jit(solution)/shard_map/ppermute | solution.py:526
  92.3 5.7 %collective-permute-start.13 = (f32[4,96,128]{2,1,0:T(8,128)S(1)}, f32[4,96,128]{2,1,0:T(8,128)S(1)}, u32[]{:S(2)}, u32[]{:S(2)}) collective-permute-start(f32[4,96,128]{2,1,0:T(8,128)S(1)} %pad_maximum_fusion.7), channel_id=1, source_target_pairs={{0,3},{1,2},{2,1},{3,0},{4,7},{5,6},{6,5},{7,4},{8,11},{9,10},{10,... | collective-permute-start | bytes 589832 | tf_op jit(solution)/shard_map/ppermute | solution.py:526

commit v9 on v8

--- a/solution.py
+++ b/solution.py
@@ -75,8 +75,9 @@
     for edge, (out, first) in enumerate(((inside, jnp.where(odd, 0, ROWS - 2)), (across, jnp.where(odd, ROWS - 2, 0)))):
         rows = pl.ds(first, 2)
         copies.append(pltpu.make_async_copy(tracers.at[:, rows], out.at[pl.ds(0, NTR)], sem.at[edge, 0]))
-        copies.append(pltpu.make_async_copy(thickness.at[rows], out.at[THICK], sem.at[edge, 1]))
-        copies.append(pltpu.make_async_copy(courant_y.at[rows], out.at[NORTH], sem.at[edge, 2]))
+        row = jnp.where(first == 0, 0, ROWS - 1)
+        copies.append(pltpu.make_async_copy(thickness.at[row], out.at[NTR, 0], sem.at[edge, 1]))
+        copies.append(pltpu.make_async_copy(courant_y.at[row], out.at[NTR, 1], sem.at[edge, 2]))
     for copy in copies:
         copy.start()
     for copy in copies:
@@ -112,9 +113,11 @@
         def bring_halos(low, high):
             for c in range(TILES):
                 cut = pl.ds(LANES * c, LANES)
-                bring(low.at[pl.ds(0, NTR + 1), :, :, cut], view.at[pl.ds(0, NTR + 1), pl.ds(0, 2), 0, c])
-                bring(high.at[:, :, :, cut], view.at[pl.ds(0, NTR + 2), pl.ds(6, 2), 1, c])
-            return copies[-2 * TILES :]
+                bring(low.at[pl.ds(0, NTR), :, :, cut], view.at[pl.ds(0, NTR), pl.ds(0, 2), 0, c])
+                bring(low.at[NTR, 0, :, cut], view.at[THICK, 1, 0, c])
+                bring(high.at[pl.ds(0, NTR), :, :, cut], view.at[pl.ds(0, NTR), pl.ds(6, 2), 1, c])
+                bring(high.at[NTR, :, :, cut], view.at[pl.ds(THICK, 2), 6, 1, c])
+            return copies[-4 * TILES :]
 
         odd = on_odd_row()
 
@@ -123,7 +126,7 @@
             for copy in bring_halos(inside, across):
                 copy.start()
 
-        del copies[-2 * TILES :]
+        del copies[-4 * TILES :]
         halos = bring_halos(across, inside)
 
         @pl.when(jnp.logical_not(odd))
@@ -466,7 +469,7 @@
             factor,
             factor,
             pltpu.VMEM((STEP * 16, LANES), F32),
-            pltpu.SemaphoreType.DMA((10 * TILES,)),
+            pltpu.SemaphoreType.DMA((12 * TILES,)),
         ],
         compiler_params=PARAMS,
     )(*given)
@@ -541,7 +544,7 @@
 
 def shards(tracers, thickness, courant_x, courant_y, level_index, level_offset, level_phase):
     own = [pltpu.with_memory_space_constraint(x, pltpu.HBM) for x in (tracers, thickness, courant_x, courant_y)]
-    rim = pltpu.HBM((NTR + 2, 2, LEVS, LONS), F32)
+    rim = pltpu.HBM((NTR + 1, 2, LEVS, LONS), F32)
     inside, across = pl.pallas_call(
         halo_kernel,
         out_shape=(rim, rim),

time: 106 us -> 111 us (1.047)
  starting transfers between devices: 36.1 us -> 41.7 us
  waiting for transfers between devices: 41.2 us -> 39.8 us
    ppermute x1, waiting for transfers between devices: 0.01 us -> 4.8 us  [shards(): lax.ppermute(across, 'lat', to_chip)]
    ppermute x12, waiting for transfers between devices: 38.8 us -> 35 us  [hop(): moved[a] = lax.ppermute(blocks[a], ('lat', 'lev'), pairs)]
    all_to_all x2, starting transfers between devices: 10.3 us -> 13.2 us  [exchange(): return lax.all_to_all(data, 'lev', split_axis=0, concat_axis=0, tiled=True)]
    all_to_all x2, waiting for transfers between devices: 2.37 us -> 0.01 us  [exchange(): return lax.all_to_all(data, 'lev', split_axis=0, concat_axis=0, tiled=True)]
    ppermute x12, starting transfers between devices: 16.5 us -> 18.5 us  [hop(): moved[a] = lax.ppermute(blocks[a], ('lat', 'lev'), pairs)]
  transfers between devices with their start and end apart: 16 -> 16, of which waited for: 6 -> 6; matrix products, arithmetic and copies ran while one was open for 0% -> 0% of each run, Pallas kernels for 22% -> 17%
where the time goes in v9:
time: 111 us; the launch traced here: 110 us
  starting transfers between devices  41.7 us (38%)
  waiting for transfers between devices  39.8 us (36%)
  Pallas kernels  27.8 us (25%)
    ppermute x12, waiting for transfers between devices, hop(): moved[a] = lax.ppermute(blocks[a], ('lat', 'lev'), pairs)  35 us
    ppermute x12, starting transfers between devices, hop(): moved[a] = lax.ppermute(blocks[a], ('lat', 'lev'), pairs)  18.5 us
    all_to_all x2, starting transfers between devices, exchange(): return lax.all_to_all(data, 'lev', split_axis=0, concat_axis=0, tiled=True)  13.2 us
    pallas_call x2, Pallas kernels, transport(): pl.pallas_call(functools.partial(transport_kernel, part), out_shape=jax.S...  12.4 us
    ppermute x1, starting transfers between devices, shards(): lax.ppermute(across, 'lat', to_chip)  9.89 us
    pallas_call x2, Pallas kernels, collect(): pl.pallas_call(functools.partial(collect_kernel, part), out_shape=jax.Sha...  5 us
    ppermute x1, waiting for transfers between devices, shards(): lax.ppermute(across, 'lat', to_chip)  4.8 us
    pallas_call x1, Pallas kernels, remap_inner(): pl.pallas_call(remap_kernel, out_shape=jax.ShapeDtypeStruct((GROUPS, DEPT...  4.72 us
  transfers between devices with their start and end apart: 16, of which 6 were waited for; matrix products, arithmetic and copies ran while one was open for 0% of the time, Pallas kernels for 17%

profile of v9, /device:TPU:7, one launch (start us, length us, event | category | flops | bytes accessed | tf_op | source)
XLA Modules:
  0.0 110.1 jit_solution(9471634326053311178)
XLA Ops:
  0.0 1.8 %shard_map.73 = (f32[10,2,2,1152]{3,2,1,0:T(2,128)}, f32[10,2,2,1152]{3,2,1,0:T(2,128)}) custom-call(f32[9,16,2,1152]{3,2,1,0:T(2,128)} %refs_0_.3, f32[16,2,1152]{2,1,0:T(2,128)} %refs_1_.3, f32[16,2,1152]{2,1,0:T(2,128)} %refs_3_.3), custom_call_target="tpu_custom_call" | custom-call | tf_op jit(solution)/shard_map/pallas_call | solution.py:548
  1.8 5.8 %shard_map.76 = f32[16,96,128]{2,1,0:T(8,128)S(1)} custom-call(f32[9,16,2,1152]{3,2,1,0:T(2,128)} %refs_0_.3, f32[16,2,1152]{2,1,0:T(2,128)} %refs_1_.3, f32[16,2,1152]{2,1,0:T(2,128)} %refs_2_.3, f32[16,2,1152]{2,1,0:T(2,128)} %refs_3_.3, f32[10,2,2,1152]{3,2,1,0:T(2,128)} %get-tuple-element.18.refs_4_), custom_call_target="tpu_custom_call" | custom-call | tf_op jit(solution)/shard_map/pallas_call | solution.py:460
  7.6 0.0 copy-start.4
  7.6 0.0 copy-start.3
  7.7 0.0 copy-start
  7.7 0.0 copy-start.1
  7.7 0.0 copy-start.2
  7.7 0.1 fusion.1
  7.8 2.8 %collective-permute-start.4 = (f32[4,96,128]{2,1,0:T(8,128)S(1)}, f32[4,96,128]{2,1,0:T(8,128)S(1)}, u32[]{:S(2)}, u32[]{:S(2)}) collective-permute-start(f32[4,96,128]{2,1,0:T(8,128)S(1)} %get-tuple-element.35), channel_id=1, source_target_pairs={{0,3},{1,2},{2,1},{3,0},{4,7},{5,6},{6,5},{7,4},{8,11},{9,10},{10,... | collective-permute-start | bytes 589832 | tf_op jit(solution)/shard_map/ppermute | solution.py:529
  10.6 0.3 collective-permute-start.3
  10.9 0.7 collective-permute-start.2
  11.6 0.0 copy-done.4
  11.6 9.9 %collective-permute-start.1 = (f32[10,2,2,1152]{3,2,1,0:T(2,128)S(1)}, f32[10,2,2,1152]{3,2,1,0:T(2,128)S(1)}, u32[]{:S(2)}, u32[]{:S(2)}) collective-permute-start(f32[10,2,2,1152]{3,2,1,0:T(2,128)S(1)} %copy-done.4), channel_id=1, source_target_pairs={{16,32},{48,64},{80,96},{112,128},{144,160},{176,192},{208,224},{3... | collective-permute-start | bytes 552968 | tf_op jit(solution)/shard_map/ppermute | solution.py:559
  21.5 0.0 copy-done.3
  21.5 0.1 collective-permute-start
  21.6 0.0 copy-done
  21.6 0.0 copy-done.1
  21.6 0.0 copy-done.2
  21.7 0.5 shard_map.74
  22.1 4.8 %collective-permute-done.1.refs_5_ = f32[10,2,2,1152]{3,2,1,0:T(2,128)S(1)} collective-permute-done((f32[10,2,2,1152]{3,2,1,0:T(2,128)S(1)}, f32[10,2,2,1152]{3,2,1,0:T(2,128)S(1)}, u32[]{:S(2)}, u32[]{:S(2)}) %collective-permute-start.1) | collective-permute-done | bytes 184352 | tf_op jit(solution)/shard_map/ppermute | solution.py:559
  26.9 0.0 collective-permute-done.refs_4_
  26.9 6.6 %shard_map.75 = f32[16,96,128]{2,1,0:T(8,128)} custom-call(f32[9,16,2,1152]{3,2,1,0:T(2,128)} %refs_0_.3, f32[16,2,1152]{2,1,0:T(2,128)} %refs_1_.3, f32[16,2,1152]{2,1,0:T(2,128)} %refs_2_.3, f32[16,2,1152]{2,1,0:T(2,128)} %refs_3_.3, f32[10,2,2,1152]{3,2,1,0:T(2,128)S(1)} %collective-permute-done.refs_4_, ...), custom_call_target="tpu_custom_call" | custom-call | tf_op jit(solution)/shard_map/pallas_call | solution.py:460
  33.6 7.9 %all-to-all-start = ((f32[16,96,128]{2,1,0:T(8,128)}), f32[16,96,128]{2,1,0:T(8,128)S(1)}, u32[]{:S(2)}, u32[]{:S(2)}) async-start(f32[16,96,128]{2,1,0:T(8,128)} %shard_map.75), calls=%async_computation | async-start | bytes 1572864 | tf_op jit(solution)/shard_map/all_to_all | solution.py:516
  41.5 0.0 collective-permute-done.4
  41.5 0.0 collective-permute-done.3
  41.5 0.0 collective-permute-done.2
  41.7 1.4 %collective-permute-start.5 = (f32[4,96,128]{2,1,0:T(8,128)S(1)}, f32[4,96,128]{2,1,0:T(8,128)S(1)}, u32[]{:S(2)}, u32[]{:S(2)}) collective-permute-start(f32[4,96,128]{2,1,0:T(8,128)S(1)} %pad_maximum_fusion.1), channel_id=1, source_target_pairs={{0,4},{1,5},{2,6},{3,7},{4,8},{5,9},{6,10},{7,11},{8,12},{9,13},{1... | collective-permute-start | bytes 589832 | tf_op jit(solution)/shard_map/ppermute | solution.py:529
  43.1 2.2 %collective-permute-start.6 = (f32[4,96,128]{2,1,0:T(8,128)S(1)}, f32[4,96,128]{2,1,0:T(8,128)S(1)}, u32[]{:S(2)}, u32[]{:S(2)}) collective-permute-start(f32[4,96,128]{2,1,0:T(8,128)S(1)} %pad_maximum_fusion.2), channel_id=1, source_target_pairs={{0,8},{1,9},{2,10},{3,11},{4,12},{5,13},{6,14},{7,15},{8,0},{9,1},... | collective-permute-start | bytes 589832 | tf_op jit(solution)/shard_map/ppermute | solution.py:529
  45.3 0.2 collective-permute-start.7
  45.5 7.4 %collective-permute-done.5.refs_1_ = f32[4,96,128]{2,1,0:T(8,128)S(1)} collective-permute-done((f32[4,96,128]{2,1,0:T(8,128)S(1)}, f32[4,96,128]{2,1,0:T(8,128)S(1)}, u32[]{:S(2)}, u32[]{:S(2)}) %collective-permute-start.5) | collective-permute-done | bytes 196640 | tf_op jit(solution)/shard_map/ppermute | solution.py:529
  52.9 9.9 %collective-permute-done.6.refs_2_ = f32[4,96,128]{2,1,0:T(8,128)S(1)} collective-permute-done((f32[4,96,128]{2,1,0:T(8,128)S(1)}, f32[4,96,128]{2,1,0:T(8,128)S(1)}, u32[]{:S(2)}, u32[]{:S(2)}) %collective-permute-start.6) | collective-permute-done | bytes 196640 | tf_op jit(solution)/shard_map/ppermute | solution.py:529
  62.8 0.0 collective-permute-done.7.refs_3_
  62.8 4.7 %shard_map.77 = f32[16,96,128]{2,1,0:T(8,128)S(1)} custom-call(f32[4,96,128]{2,1,0:T(8,128)S(1)} %pad_maximum_fusion.refs_0_, f32[4,96,128]{2,1,0:T(8,128)S(1)} %collective-permute-done.5.refs_1_, f32[4,96,128]{2,1,0:T(8,128)S(1)} %collective-permute-done.6.refs_2_, f32[4,96,128]{2,1,0:T(8,128)S(1)} %collective-permute-done.7.refs_3_, ...), custom_call_target="tpu_custom_call" | custom-call | tf_op jit(solution)/shard_map/pallas_call | solution.py:490
  67.6 0.1 fusion
  67.6 0.8 collective-permute-start.10
  68.4 3.1 %collective-permute-start.9 = (f32[4,96,128]{2,1,0:T(8,128)S(1)}, f32[4,96,128]{2,1,0:T(8,128)S(1)}, u32[]{:S(2)}, u32[]{:S(2)}) collective-permute-start(f32[4,96,128]{2,1,0:T(8,128)S(1)} %get-tuple-element.32), channel_id=1, source_target_pairs={{0,8},{1,9},{2,10},{3,11},{4,12},{5,13},{6,14},{7,15},{8,0},{9,1},... | collective-permute-start | bytes 589832 | tf_op jit(solution)/shard_map/ppermute | solution.py:529
  71.5 0.0 collective-permute-start.8
  71.6 0.0 all-to-all-done
  71.6 3.3 %shard_map.78 = f32[1536,128]{1,0:T(8,128)} custom-call(f32[1536,128]{1,0:T(8,128)S(1)} %bitcast.2, f32[512,128]{1,0:T(8,128)S(1)} %get-tuple-element.20.refs_6_.table), custom_call_target="tpu_custom_call" | custom-call | tf_op jit(solution)/shard_map/pallas_call | solution.py:479
  74.9 5.3 %all-to-all-start.1 = ((f32[16,96,128]{2,1,0:T(8,128)}), f32[16,96,128]{2,1,0:T(8,128)S(1)}, u32[]{:S(2)}, u32[]{:S(2)}) async-start(f32[16,96,128]{2,1,0:T(8,128)} %bitcast.1), calls=%async_computation.1 | async-start | bytes 1572864 | tf_op jit(solution)/shard_map/all_to_all | solution.py:516
  80.2 0.0 collective-permute-done.10
  80.2 13.8 %collective-permute-done.9 = f32[4,96,128]{2,1,0:T(8,128)S(1)} collective-permute-done((f32[4,96,128]{2,1,0:T(8,128)S(1)}, f32[4,96,128]{2,1,0:T(8,128)S(1)}, u32[]{:S(2)}, u32[]{:S(2)}) %collective-permute-start.9) | collective-permute-done | bytes 196640 | tf_op jit(solution)/shard_map/ppermute | solution.py:529
  94.0 0.0 collective-permute-done.8
  94.1 3.2 %collective-permute-start.11 = (f32[4,96,128]{2,1,0:T(8,128)S(1)}, f32[4,96,128]{2,1,0:T(8,128)S(1)}, u32[]{:S(2)}, u32[]{:S(2)}) collective-permute-start(f32[4,96,128]{2,1,0:T(8,128)S(1)} %pad_maximum_fusion.5), channel_id=1, source_target_pairs={{0,1},{1,0},{2,3},{3,2},{4,5},{5,4},{6,7},{7,6},{8,9},{9,8},{10,11... | collective-permute-start | bytes 589832 | tf_op jit(solution)/shard_map/ppermute | solution.py:529
  97.3 2.5 %collective-permute-start.12 = (f32[4,96,128]{2,1,0:T(8,128)S(1)}, f32[4,96,128]{2,1,0:T(8,128)S(1)}, u32[]{:S(2)}, u32[]{:S(2)}) collective-permute-start(f32[4,96,128]{2,1,0:T(8,128)S(1)} %pad_maximum_fusion.6), channel_id=1, source_target_pairs={{0,2},{1,3},{2,0},{3,1},{4,6},{5,7},{6,4},{7,5},{8,10},{9,11},{10,... | collective-permute-start | bytes 589832 | tf_op jit(solution)/shard_map/ppermute | solution.py:529
  99.8 1.3 %collective-permute-start.13 = (f32[4,96,128]{2,1,0:T(8,128)S(1)}, f32[4,96,128]{2,1,0:T(8,128)S(1)}, u32[]{:S(2)}, u32[]{:S(2)}) collective-permute-start(f32[4,96,128]{2,1,0:T(8,128)S(1)} %pad_maximum_fusion.7), channel_id=1, source_target_pairs={{0,3},{1,2},{2,1},{3,0},{4,7},{5,6},{6,5},{7,4},{8,11},{9,10},{10,... | collective-permute-start | bytes 589832 | tf_op jit(solution)/shard_map/ppermute | solution.py:529
  101.1 1.0 collective-permute-done.11.refs_1_
  102.1 2.8 %collective-permute-done.12.refs_2_ = f32[4,96,128]{2,1,0:T(8,128)S(1)} collective-permute-done((f32[4,96,128]{2,1,0:T(8,128)S(1)}, f32[4,96,128]{2,1,0:T(8,128)S(1)}, u32[]{:S(2)}, u32[]{:S(2)}) %collective-permute-start.12) | collective-permute-done | bytes 196640 | tf_op jit(solution)/shard_map/ppermute | solution.py:529
  104.9 0.0 collective-permute-done.13.refs_3_
  104.9 3.1 %shard_map.79.refs_1_ = f32[10,16,2,1152]{3,2,1,0:T(2,128)} custom-call(f32[4,96,128]{2,1,0:T(8,128)S(1)} %pad_maximum_fusion.4.refs_0_, f32[4,96,128]{2,1,0:T(8,128)S(1)} %collective-permute-done.11.refs_1_, f32[4,96,128]{2,1,0:T(8,128)S(1)} %collective-permute-done.12.refs_2_, f32[4,96,128]{2,1,0:T(8,128)S(1)} %collective-permute-done.13.refs_3_), custom_call_target="tpu_custom_call" | custom-call | tf_op jit(solution)/shard_map/pallas_call | solution.py:504
  108.0 0.0 all-to-all-done.1.refs_0_
  108.0 1.9 %shard_map.80 = f32[10,16,2,1152]{3,2,1,0:T(2,128)} custom-call(f32[16,96,128]{2,1,0:T(8,128)S(1)} %all-to-all-done.1.refs_0_, f32[10,16,2,1152]{3,2,1,0:T(2,128)} %shard_map.79.refs_1_), custom_call_target="tpu_custom_call", output_to_operand_aliasing={{}: (1, {})} | custom-call | tf_op jit(solution)/shard_map/pallas_call | solution.py:504
  (14 shorter events, 0.2 us)
Async XLA Ops:
  7.6 4.0 %copy-start.4 = (f32[10,2,2,1152]{3,2,1,0:T(2,128)S(1)}, f32[10,2,2,1152]{3,2,1,0:T(2,128)}, u32[]{:S(2)}) copy-start(f32[10,2,2,1152]{3,2,1,0:T(2,128)} %get-tuple-element.19) | copy-start | bytes 552964
  7.6 13.9 %copy-start.3 = (f32[10,2,2,1152]{3,2,1,0:T(2,128)S(1)}, f32[10,2,2,1152]{3,2,1,0:T(2,128)}, u32[]{:S(2)}) copy-start(f32[10,2,2,1152]{3,2,1,0:T(2,128)} %get-tuple-element.18.refs_4_) | copy-start | bytes 552964
  7.7 14.0 %copy-start = (s32[31,16,72]{2,1,0:T(8,128)S(1)}, s32[31,16,72]{2,1,0:T(8,128)}, u32[]{:S(2)}) copy-start(s32[31,16,72]{2,1,0:T(8,128)} %index.1) | copy-start | bytes 428548
  7.7 14.0 %copy-start.1 = (s32[31,16,72]{2,1,0:T(8,128)S(1)}, s32[31,16,72]{2,1,0:T(8,128)}, u32[]{:S(2)}) copy-start(s32[31,16,72]{2,1,0:T(8,128)} %offset.1) | copy-start | bytes 428548
  7.7 14.0 %copy-start.2 = (f32[31,16,72]{2,1,0:T(8,128)S(1)}, f32[31,16,72]{2,1,0:T(8,128)}, u32[]{:S(2)}) copy-start(f32[31,16,72]{2,1,0:T(8,128)} %phase.1) | copy-start | bytes 428548
  7.8 33.8 %collective-permute-start.4 = (f32[4,96,128]{2,1,0:T(8,128)S(1)}, f32[4,96,128]{2,1,0:T(8,128)S(1)}, u32[]{:S(2)}, u32[]{:S(2)}) collective-permute-start(f32[4,96,128]{2,1,0:T(8,128)S(1)} %get-tuple-element.35), channel_id=1, source_target_pairs={{0,3},{1,2},{2,1},{3,0},{4,7},{5,6},{6,5},{7,4},{8,11},{9,10},{10,... | collective-permute-start | bytes 589832 | tf_op jit(solution)/shard_map/ppermute | solution.py:529
  10.6 31.0 %collective-permute-start.3 = (f32[4,96,128]{2,1,0:T(8,128)S(1)}, f32[4,96,128]{2,1,0:T(8,128)S(1)}, u32[]{:S(2)}, u32[]{:S(2)}) collective-permute-start(f32[4,96,128]{2,1,0:T(8,128)S(1)} %get-tuple-element.36), channel_id=1, source_target_pairs={{0,2},{1,3},{2,0},{3,1},{4,6},{5,7},{6,4},{7,5},{8,10},{9,11},{10,... | collective-permute-start | bytes 589832 | tf_op jit(solution)/shard_map/ppermute | solution.py:529
  10.9 30.6 %collective-permute-start.2 = (f32[4,96,128]{2,1,0:T(8,128)S(1)}, f32[4,96,128]{2,1,0:T(8,128)S(1)}, u32[]{:S(2)}, u32[]{:S(2)}) collective-permute-start(f32[4,96,128]{2,1,0:T(8,128)S(1)} %get-tuple-element.37), channel_id=1, source_target_pairs={{0,1},{1,0},{2,3},{3,2},{4,5},{5,4},{6,7},{7,6},{8,9},{9,8},{10,11... | collective-permute-start | bytes 589832 | tf_op jit(solution)/shard_map/ppermute | solution.py:529
  11.6 15.3 %collective-permute-start.1 = (f32[10,2,2,1152]{3,2,1,0:T(2,128)S(1)}, f32[10,2,2,1152]{3,2,1,0:T(2,128)S(1)}, u32[]{:S(2)}, u32[]{:S(2)}) collective-permute-start(f32[10,2,2,1152]{3,2,1,0:T(2,128)S(1)} %copy-done.4), channel_id=1, source_target_pairs={{16,32},{48,64},{80,96},{112,128},{144,160},{176,192},{208,224},{3... | collective-permute-start | bytes 552968 | tf_op jit(solution)/shard_map/ppermute | solution.py:559
  21.5 5.4 %collective-permute-start = (f32[10,2,2,1152]{3,2,1,0:T(2,128)S(1)}, f32[10,2,2,1152]{3,2,1,0:T(2,128)S(1)}, u32[]{:S(2)}, u32[]{:S(2)}) collective-permute-start(f32[10,2,2,1152]{3,2,1,0:T(2,128)S(1)} %copy-done.3), channel_id=1, source_target_pairs={{0,16},{16,0},{32,48},{48,32},{64,80},{80,64},{96,112},{112,96},{1... | collective-permute-start | bytes 552968 | tf_op jit(solution)/shard_map/ppermute | solution.py:559
  33.6 38.0 %all-to-all-start = ((f32[16,96,128]{2,1,0:T(8,128)}), f32[16,96,128]{2,1,0:T(8,128)S(1)}, u32[]{:S(2)}, u32[]{:S(2)}) async-start(f32[16,96,128]{2,1,0:T(8,128)} %shard_map.75), calls=%async_computation | async-start | bytes 1572864 | tf_op jit(solution)/shard_map/all_to_all | solution.py:516
  41.7 11.2 %collective-permute-start.5 = (f32[4,96,128]{2,1,0:T(8,128)S(1)}, f32[4,96,128]{2,1,0:T(8,128)S(1)}, u32[]{:S(2)}, u32[]{:S(2)}) collective-permute-start(f32[4,96,128]{2,1,0:T(8,128)S(1)} %pad_maximum_fusion.1), channel_id=1, source_target_pairs={{0,4},{1,5},{2,6},{3,7},{4,8},{5,9},{6,10},{7,11},{8,12},{9,13},{1... | collective-permute-start | bytes 589832 | tf_op jit(solution)/shard_map/ppermute | solution.py:529
  43.1 19.7 %collective-permute-start.6 = (f32[4,96,128]{2,1,0:T(8,128)S(1)}, f32[4,96,128]{2,1,0:T(8,128)S(1)}, u32[]{:S(2)}, u32[]{:S(2)}) collective-permute-start(f32[4,96,128]{2,1,0:T(8,128)S(1)} %pad_maximum_fusion.2), channel_id=1, source_target_pairs={{0,8},{1,9},{2,10},{3,11},{4,12},{5,13},{6,14},{7,15},{8,0},{9,1},... | collective-permute-start | bytes 589832 | tf_op jit(solution)/shard_map/ppermute | solution.py:529
  45.3 17.5 %collective-permute-start.7 = (f32[4,96,128]{2,1,0:T(8,128)S(1)}, f32[4,96,128]{2,1,0:T(8,128)S(1)}, u32[]{:S(2)}, u32[]{:S(2)}) collective-permute-start(f32[4,96,128]{2,1,0:T(8,128)S(1)} %pad_maximum_fusion.3), channel_id=1, source_target_pairs={{0,12},{1,13},{2,14},{3,15},{4,0},{5,1},{6,2},{7,3},{8,4},{9,5},{1... | collective-permute-start | bytes 589832 | tf_op jit(solution)/shard_map/ppermute | solution.py:529
  67.6 12.6 %collective-permute-start.10 = (f32[4,96,128]{2,1,0:T(8,128)S(1)}, f32[4,96,128]{2,1,0:T(8,128)S(1)}, u32[]{:S(2)}, u32[]{:S(2)}) collective-permute-start(f32[4,96,128]{2,1,0:T(8,128)S(1)} %get-tuple-element.31), channel_id=1, source_target_pairs={{0,12},{1,13},{2,14},{3,15},{4,0},{5,1},{6,2},{7,3},{8,4},{9,5},{1... | collective-permute-start | bytes 589832 | tf_op jit(solution)/shard_map/ppermute | solution.py:529
  68.4 25.6 %collective-permute-start.9 = (f32[4,96,128]{2,1,0:T(8,128)S(1)}, f32[4,96,128]{2,1,0:T(8,128)S(1)}, u32[]{:S(2)}, u32[]{:S(2)}) collective-permute-start(f32[4,96,128]{2,1,0:T(8,128)S(1)} %get-tuple-element.32), channel_id=1, source_target_pairs={{0,8},{1,9},{2,10},{3,11},{4,12},{5,13},{6,14},{7,15},{8,0},{9,1},... | collective-permute-start | bytes 589832 | tf_op jit(solution)/shard_map/ppermute | solution.py:529
  71.5 22.5 %collective-permute-start.8 = (f32[4,96,128]{2,1,0:T(8,128)S(1)}, f32[4,96,128]{2,1,0:T(8,128)S(1)}, u32[]{:S(2)}, u32[]{:S(2)}) collective-permute-start(f32[4,96,128]{2,1,0:T(8,128)S(1)} %get-tuple-element.33), channel_id=1, source_target_pairs={{0,4},{1,5},{2,6},{3,7},{4,8},{5,9},{6,10},{7,11},{8,12},{9,13},{1... | collective-permute-start | bytes 589832 | tf_op jit(solution)/shard_map/ppermute | solution.py:529
  74.9 33.1 %all-to-all-start.1 = ((f32[16,96,128]{2,1,0:T(8,128)}), f32[16,96,128]{2,1,0:T(8,128)S(1)}, u32[]{:S(2)}, u32[]{:S(2)}) async-start(f32[16,96,128]{2,1,0:T(8,128)} %bitcast.1), calls=%async_computation.1 | async-start | bytes 1572864 | tf_op jit(solution)/shard_map/all_to_all | solution.py:516
  94.1 8.0 %collective-permute-start.11 = (f32[4,96,128]{2,1,0:T(8,128)S(1)}, f32[4,96,128]{2,1,0:T(8,128)S(1)}, u32[]{:S(2)}, u32[]{:S(2)}) collective-permute-start(f32[4,96,128]{2,1,0:T(8,128)S(1)} %pad_maximum_fusion.5), channel_id=1, source_target_pairs={{0,1},{1,0},{2,3},{3,2},{4,5},{5,4},{6,7},{7,6},{8,9},{9,8},{10,11... | collective-permute-start | bytes 589832 | tf_op jit(solution)/shard_map/ppermute | solution.py:529
  97.3 7.6 %collective-permute-start.12 = (f32[4,96,128]{2,1,0:T(8,128)S(1)}, f32[4,96,128]{2,1,0:T(8,128)S(1)}, u32[]{:S(2)}, u32[]{:S(2)}) collective-permute-start(f32[4,96,128]{2,1,0:T(8,128)S(1)} %pad_maximum_fusion.6), channel_id=1, source_target_pairs={{0,2},{1,3},{2,0},{3,1},{4,6},{5,7},{6,4},{7,5},{8,10},{9,11},{10,... | collective-permute-start | bytes 589832 | tf_op jit(solution)/shard_map/ppermute | solution.py:529
  99.8 5.1 %collective-permute-start.13 = (f32[4,96,128]{2,1,0:T(8,128)S(1)}, f32[4,96,128]{2,1,0:T(8,128)S(1)}, u32[]{:S(2)}, u32[]{:S(2)}) collective-permute-start(f32[4,96,128]{2,1,0:T(8,128)S(1)} %pad_maximum_fusion.7), channel_id=1, source_target_pairs={{0,3},{1,2},{2,1},{3,0},{4,7},{5,6},{6,5},{7,4},{8,11},{9,10},{10,... | collective-permute-start | bytes 589832 | tf_op jit(solution)/shard_map/ppermute | solution.py:529

commit v10 on v9

--- a/solution.py
+++ b/solution.py
@@ -567,7 +567,7 @@
         compiler_params=PARAMS,
     )(level_index, level_offset, level_phase)
     outer = transport(OUTER, *own, inside, across, outer_table)
-    inner = first_hop(inner)
+    inner = first_hop(after(inner, inside, across))
     inner, outer = second_hop(after(inner, outer)), exchange(outer)
     inner = remap_inner(inner, inner_table)
     outer = remap_outer(after(outer, inner), outer_table)

time: 111 us -> 107 us (0.964)
  starting transfers between devices: 41.7 us -> 36.9 us
    ppermute x1, waiting for transfers between devices: 4.8 us -> 0.01 us  [shards(): lax.ppermute(across, 'lat', to_chip)]
    ppermute x12, waiting for transfers between devices: 35 us -> 39.6 us  [hop(): moved[a] = lax.ppermute(blocks[a], ('lat', 'lev'), pairs)]
    all_to_all x2, starting transfers between devices: 13.2 us -> 10.6 us  [exchange(): return lax.all_to_all(data, 'lev', split_axis=0, concat_axis=0, tiled=True)]
    ppermute x12, starting transfers between devices: 18.5 us -> 16.9 us  [hop(): moved[a] = lax.ppermute(blocks[a], ('lat', 'lev'), pairs)]
    all_to_all x2, waiting for transfers between devices: 0.01 us -> 1.25 us  [exchange(): return lax.all_to_all(data, 'lev', split_axis=0, concat_axis=0, tiled=True)]
  transfers between devices with their start and end apart: 16 -> 16, of which waited for: 6 -> 6; matrix products, arithmetic and copies ran while one was open for 0% -> 0% of each run, Pallas kernels for 17% -> 23%
where the time goes in v10:
time: 107 us; the launch traced here: 106 us
  waiting for transfers between devices  40.8 us (38%)
  starting transfers between devices  36.9 us (34%)
  Pallas kernels  27.9 us (26%)
    ppermute x12, waiting for transfers between devices, hop(): moved[a] = lax.ppermute(blocks[a], ('lat', 'lev'), pairs)  39.6 us
    ppermute x12, starting transfers between devices, hop(): moved[a] = lax.ppermute(blocks[a], ('lat', 'lev'), pairs)  16.9 us
    pallas_call x2, Pallas kernels, transport(): pl.pallas_call(functools.partial(transport_kernel, part), out_shape=jax.S...  12.6 us
    all_to_all x2, starting transfers between devices, exchange(): return lax.all_to_all(data, 'lev', split_axis=0, concat_axis=0, tiled=True)  10.6 us
    ppermute x1, starting transfers between devices, shards(): lax.ppermute(across, 'lat', to_chip)  9.29 us
    pallas_call x2, Pallas kernels, collect(): pl.pallas_call(functools.partial(collect_kernel, part), out_shape=jax.Sha...  5 us
    pallas_call x1, Pallas kernels, remap_inner(): pl.pallas_call(remap_kernel, out_shape=jax.ShapeDtypeStruct((GROUPS, DEPT...  4.72 us
    pallas_call x1, Pallas kernels, remap_outer(): pl.pallas_call(remap_rows, out_shape=jax.ShapeDtypeStruct((GROUPS * DEPTH...  3.33 us
  transfers between devices with their start and end apart: 16, of which 6 were waited for; matrix products, arithmetic and copies ran while one was open for 0% of the time, Pallas kernels for 23%

profile of v10, /device:TPU:7, one launch (start us, length us, event | category | flops | bytes accessed | tf_op | source)
XLA Modules:
  0.0 106.5 jit_solution(11379043947207511536)
XLA Ops:
  0.0 1.8 %shard_map.73 = (f32[10,2,2,1152]{3,2,1,0:T(2,128)}, f32[10,2,2,1152]{3,2,1,0:T(2,128)}) custom-call(f32[9,16,2,1152]{3,2,1,0:T(2,128)} %refs_0_.3, f32[16,2,1152]{2,1,0:T(2,128)} %refs_1_.3, f32[16,2,1152]{2,1,0:T(2,128)} %refs_3_.3), custom_call_target="tpu_custom_call" | custom-call | tf_op jit(solution)/shard_map/pallas_call | solution.py:548
  1.8 9.3 %collective-permute-start.1 = (f32[10,2,2,1152]{3,2,1,0:T(2,128)}, f32[10,2,2,1152]{3,2,1,0:T(2,128)S(1)}, u32[]{:S(2)}, u32[]{:S(2)}) collective-permute-start(f32[10,2,2,1152]{3,2,1,0:T(2,128)} %get-tuple-element.20), channel_id=1, source_target_pairs={{16,32},{48,64},{80,96},{112,128},{144,160},{176,192},{208,224},{3... | collective-permute-start | bytes 552968 | tf_op jit(solution)/shard_map/ppermute | solution.py:559
  11.1 0.0 copy-start
  11.1 0.0 copy-start.1
  11.1 0.0 copy-start.2
  11.2 0.1 collective-permute-start
  11.3 6.0 %shard_map.76 = f32[16,96,128]{2,1,0:T(8,128)S(1)} custom-call(f32[9,16,2,1152]{3,2,1,0:T(2,128)} %refs_0_.3, f32[16,2,1152]{2,1,0:T(2,128)} %refs_1_.3, f32[16,2,1152]{2,1,0:T(2,128)} %refs_2_.3, f32[16,2,1152]{2,1,0:T(2,128)} %refs_3_.3, f32[10,2,2,1152]{3,2,1,0:T(2,128)} %get-tuple-element.19.refs_4_), custom_call_target="tpu_custom_call" | custom-call | tf_op jit(solution)/shard_map/pallas_call | solution.py:460
  17.2 0.0 collective-permute-done.1.refs_5_
  17.2 0.0 collective-permute-done.refs_4_
  17.2 0.1 fusion.1
  17.3 2.8 %collective-permute-start.4 = (f32[4,96,128]{2,1,0:T(8,128)S(1)}, f32[4,96,128]{2,1,0:T(8,128)S(1)}, u32[]{:S(2)}, u32[]{:S(2)}) collective-permute-start(f32[4,96,128]{2,1,0:T(8,128)S(1)} %get-tuple-element.37), channel_id=1, source_target_pairs={{0,3},{1,2},{2,1},{3,0},{4,7},{5,6},{6,5},{7,4},{8,11},{9,10},{10,... | collective-permute-start | bytes 589832 | tf_op jit(solution)/shard_map/ppermute | solution.py:529
  20.1 0.3 collective-permute-start.3
  20.5 0.7 collective-permute-start.2
  21.2 0.0 copy-done
  21.2 0.0 copy-done.1
  21.2 0.0 copy-done.2
  21.2 0.5 shard_map.74
  21.6 6.6 %shard_map.75 = f32[16,96,128]{2,1,0:T(8,128)} custom-call(f32[9,16,2,1152]{3,2,1,0:T(2,128)} %refs_0_.3, f32[16,2,1152]{2,1,0:T(2,128)} %refs_1_.3, f32[16,2,1152]{2,1,0:T(2,128)} %refs_2_.3, f32[16,2,1152]{2,1,0:T(2,128)} %refs_3_.3, f32[10,2,2,1152]{3,2,1,0:T(2,128)S(1)} %collective-permute-done.refs_4_, ...), custom_call_target="tpu_custom_call" | custom-call | tf_op jit(solution)/shard_map/pallas_call | solution.py:460
  28.3 5.1 %all-to-all-start = ((f32[16,96,128]{2,1,0:T(8,128)}), f32[16,96,128]{2,1,0:T(8,128)S(1)}, u32[]{:S(2)}, u32[]{:S(2)}) async-start(f32[16,96,128]{2,1,0:T(8,128)} %shard_map.75), calls=%async_computation | async-start | bytes 1572864 | tf_op jit(solution)/shard_map/all_to_all | solution.py:516
  33.4 0.0 collective-permute-done.4
  33.4 0.0 collective-permute-done.3
  33.4 0.0 collective-permute-done.2
  33.5 1.4 %collective-permute-start.5 = (f32[4,96,128]{2,1,0:T(8,128)S(1)}, f32[4,96,128]{2,1,0:T(8,128)S(1)}, u32[]{:S(2)}, u32[]{:S(2)}) collective-permute-start(f32[4,96,128]{2,1,0:T(8,128)S(1)} %pad_maximum_fusion.1), channel_id=1, source_target_pairs={{0,4},{1,5},{2,6},{3,7},{4,8},{5,9},{6,10},{7,11},{8,12},{9,13},{1... | collective-permute-start | bytes 589832 | tf_op jit(solution)/shard_map/ppermute | solution.py:529
  35.0 2.2 %collective-permute-start.6 = (f32[4,96,128]{2,1,0:T(8,128)S(1)}, f32[4,96,128]{2,1,0:T(8,128)S(1)}, u32[]{:S(2)}, u32[]{:S(2)}) collective-permute-start(f32[4,96,128]{2,1,0:T(8,128)S(1)} %pad_maximum_fusion.2), channel_id=1, source_target_pairs={{0,8},{1,9},{2,10},{3,11},{4,12},{5,13},{6,14},{7,15},{8,0},{9,1},... | collective-permute-start | bytes 589832 | tf_op jit(solution)/shard_map/ppermute | solution.py:529
  37.2 0.2 collective-permute-start.7
  37.4 12.0 %collective-permute-done.5.refs_1_ = f32[4,96,128]{2,1,0:T(8,128)S(1)} collective-permute-done((f32[4,96,128]{2,1,0:T(8,128)S(1)}, f32[4,96,128]{2,1,0:T(8,128)S(1)}, u32[]{:S(2)}, u32[]{:S(2)}) %collective-permute-start.5) | collective-permute-done | bytes 196640 | tf_op jit(solution)/shard_map/ppermute | solution.py:529
  49.4 10.6 %collective-permute-done.6.refs_2_ = f32[4,96,128]{2,1,0:T(8,128)S(1)} collective-permute-done((f32[4,96,128]{2,1,0:T(8,128)S(1)}, f32[4,96,128]{2,1,0:T(8,128)S(1)}, u32[]{:S(2)}, u32[]{:S(2)}) %collective-permute-start.6) | collective-permute-done | bytes 196640 | tf_op jit(solution)/shard_map/ppermute | solution.py:529
  60.0 0.0 collective-permute-done.7.refs_3_
  60.0 4.7 %shard_map.77 = f32[16,96,128]{2,1,0:T(8,128)S(1)} custom-call(f32[4,96,128]{2,1,0:T(8,128)S(1)} %pad_maximum_fusion.refs_0_, f32[4,96,128]{2,1,0:T(8,128)S(1)} %collective-permute-done.5.refs_1_, f32[4,96,128]{2,1,0:T(8,128)S(1)} %collective-permute-done.6.refs_2_, f32[4,96,128]{2,1,0:T(8,128)S(1)} %collective-permute-done.7.refs_3_, ...), custom_call_target="tpu_custom_call" | custom-call | tf_op jit(solution)/shard_map/pallas_call | solution.py:490
  64.7 0.1 fusion
  64.8 1.0 collective-permute-start.10
  65.8 2.6 %collective-permute-start.9 = (f32[4,96,128]{2,1,0:T(8,128)S(1)}, f32[4,96,128]{2,1,0:T(8,128)S(1)}, u32[]{:S(2)}, u32[]{:S(2)}) collective-permute-start(f32[4,96,128]{2,1,0:T(8,128)S(1)} %get-tuple-element.34), channel_id=1, source_target_pairs={{0,8},{1,9},{2,10},{3,11},{4,12},{5,13},{6,14},{7,15},{8,0},{9,1},... | collective-permute-start | bytes 589832 | tf_op jit(solution)/shard_map/ppermute | solution.py:529
  68.4 0.0 collective-permute-start.8
  68.4 0.0 all-to-all-done
  68.4 3.3 %shard_map.78 = f32[1536,128]{1,0:T(8,128)} custom-call(f32[1536,128]{1,0:T(8,128)S(1)} %bitcast.2, f32[512,128]{1,0:T(8,128)S(1)} %get-tuple-element.21.refs_6_.table), custom_call_target="tpu_custom_call" | custom-call | tf_op jit(solution)/shard_map/pallas_call | solution.py:479
  71.8 5.5 %all-to-all-start.1 = ((f32[16,96,128]{2,1,0:T(8,128)}), f32[16,96,128]{2,1,0:T(8,128)S(1)}, u32[]{:S(2)}, u32[]{:S(2)}) async-start(f32[16,96,128]{2,1,0:T(8,128)} %bitcast.1), calls=%async_computation.1 | async-start | bytes 1572864 | tf_op jit(solution)/shard_map/all_to_all | solution.py:516
  77.3 0.0 collective-permute-done.10
  77.3 11.5 %collective-permute-done.9 = f32[4,96,128]{2,1,0:T(8,128)S(1)} collective-permute-done((f32[4,96,128]{2,1,0:T(8,128)S(1)}, f32[4,96,128]{2,1,0:T(8,128)S(1)}, u32[]{:S(2)}, u32[]{:S(2)}) %collective-permute-start.9) | collective-permute-done | bytes 196640 | tf_op jit(solution)/shard_map/ppermute | solution.py:529
  88.8 0.0 collective-permute-done.8
  88.9 1.4 %collective-permute-start.11 = (f32[4,96,128]{2,1,0:T(8,128)S(1)}, f32[4,96,128]{2,1,0:T(8,128)S(1)}, u32[]{:S(2)}, u32[]{:S(2)}) collective-permute-start(f32[4,96,128]{2,1,0:T(8,128)S(1)} %pad_maximum_fusion.5), channel_id=1, source_target_pairs={{0,1},{1,0},{2,3},{3,2},{4,5},{5,4},{6,7},{7,6},{8,9},{9,8},{10,11... | collective-permute-start | bytes 589832 | tf_op jit(solution)/shard_map/ppermute | solution.py:529
  90.4 4.1 %collective-permute-start.12 = (f32[4,96,128]{2,1,0:T(8,128)S(1)}, f32[4,96,128]{2,1,0:T(8,128)S(1)}, u32[]{:S(2)}, u32[]{:S(2)}) collective-permute-start(f32[4,96,128]{2,1,0:T(8,128)S(1)} %pad_maximum_fusion.6), channel_id=1, source_target_pairs={{0,2},{1,3},{2,0},{3,1},{4,6},{5,7},{6,4},{7,5},{8,10},{9,11},{10,... | collective-permute-start | bytes 589832 | tf_op jit(solution)/shard_map/ppermute | solution.py:529
  94.5 0.1 collective-permute-start.13
  94.6 2.3 %collective-permute-done.11.refs_1_ = f32[4,96,128]{2,1,0:T(8,128)S(1)} collective-permute-done((f32[4,96,128]{2,1,0:T(8,128)S(1)}, f32[4,96,128]{2,1,0:T(8,128)S(1)}, u32[]{:S(2)}, u32[]{:S(2)}) %collective-permute-start.11) | collective-permute-done | bytes 196640 | tf_op jit(solution)/shard_map/ppermute | solution.py:529
  96.9 3.2 %collective-permute-done.12.refs_2_ = f32[4,96,128]{2,1,0:T(8,128)S(1)} collective-permute-done((f32[4,96,128]{2,1,0:T(8,128)S(1)}, f32[4,96,128]{2,1,0:T(8,128)S(1)}, u32[]{:S(2)}, u32[]{:S(2)}) %collective-permute-start.12) | collective-permute-done | bytes 196640 | tf_op jit(solution)/shard_map/ppermute | solution.py:529
  100.1 0.0 collective-permute-done.13.refs_3_
  100.1 3.1 %shard_map.79.refs_1_ = f32[10,16,2,1152]{3,2,1,0:T(2,128)} custom-call(f32[4,96,128]{2,1,0:T(8,128)S(1)} %pad_maximum_fusion.4.refs_0_, f32[4,96,128]{2,1,0:T(8,128)S(1)} %collective-permute-done.11.refs_1_, f32[4,96,128]{2,1,0:T(8,128)S(1)} %collective-permute-done.12.refs_2_, f32[4,96,128]{2,1,0:T(8,128)S(1)} %collective-permute-done.13.refs_3_), custom_call_target="tpu_custom_call" | custom-call | tf_op jit(solution)/shard_map/pallas_call | solution.py:504
  103.1 1.2 %all-to-all-done.1.refs_0_ = f32[16,96,128]{2,1,0:T(8,128)S(1)} async-done(((f32[16,96,128]{2,1,0:T(8,128)}), f32[16,96,128]{2,1,0:T(8,128)S(1)}, u32[]{:S(2)}, u32[]{:S(2)}) %all-to-all-start.1) | async-done | bytes 786464 | tf_op jit(solution)/shard_map/all_to_all | solution.py:516
  104.4 1.9 %shard_map.80 = f32[10,16,2,1152]{3,2,1,0:T(2,128)} custom-call(f32[16,96,128]{2,1,0:T(8,128)S(1)} %all-to-all-done.1.refs_0_, f32[10,16,2,1152]{3,2,1,0:T(2,128)} %shard_map.79.refs_1_), custom_call_target="tpu_custom_call", output_to_operand_aliasing={{}: (1, {})} | custom-call | tf_op jit(solution)/shard_map/pallas_call | solution.py:504
  (14 shorter events, 0.2 us)
Async XLA Ops:
  1.8 15.4 %collective-permute-start.1 = (f32[10,2,2,1152]{3,2,1,0:T(2,128)}, f32[10,2,2,1152]{3,2,1,0:T(2,128)S(1)}, u32[]{:S(2)}, u32[]{:S(2)}) collective-permute-start(f32[10,2,2,1152]{3,2,1,0:T(2,128)} %get-tuple-element.20), channel_id=1, source_target_pairs={{16,32},{48,64},{80,96},{112,128},{144,160},{176,192},{208,224},{3... | collective-permute-start | bytes 552968 | tf_op jit(solution)/shard_map/ppermute | solution.py:559
  11.1 10.0 %copy-start = (s32[31,16,72]{2,1,0:T(8,128)S(1)}, s32[31,16,72]{2,1,0:T(8,128)}, u32[]{:S(2)}) copy-start(s32[31,16,72]{2,1,0:T(8,128)} %index.1) | copy-start | bytes 428548
  11.1 10.0 %copy-start.1 = (s32[31,16,72]{2,1,0:T(8,128)S(1)}, s32[31,16,72]{2,1,0:T(8,128)}, u32[]{:S(2)}) copy-start(s32[31,16,72]{2,1,0:T(8,128)} %offset.1) | copy-start | bytes 428548
  11.1 10.0 %copy-start.2 = (f32[31,16,72]{2,1,0:T(8,128)S(1)}, f32[31,16,72]{2,1,0:T(8,128)}, u32[]{:S(2)}) copy-start(f32[31,16,72]{2,1,0:T(8,128)} %phase.1) | copy-start | bytes 428548
  11.2 6.1 %collective-permute-start = (f32[10,2,2,1152]{3,2,1,0:T(2,128)}, f32[10,2,2,1152]{3,2,1,0:T(2,128)S(1)}, u32[]{:S(2)}, u32[]{:S(2)}) collective-permute-start(f32[10,2,2,1152]{3,2,1,0:T(2,128)} %get-tuple-element.19.refs_4_), channel_id=1, source_target_pairs={{0,16},{16,0},{32,48},{48,32},{64,80},{80,64},{96,112},{112,96},{1... | collective-permute-start | bytes 552968 | tf_op jit(solution)/shard_map/ppermute | solution.py:559
  17.3 16.1 %collective-permute-start.4 = (f32[4,96,128]{2,1,0:T(8,128)S(1)}, f32[4,96,128]{2,1,0:T(8,128)S(1)}, u32[]{:S(2)}, u32[]{:S(2)}) collective-permute-start(f32[4,96,128]{2,1,0:T(8,128)S(1)} %get-tuple-element.37), channel_id=1, source_target_pairs={{0,3},{1,2},{2,1},{3,0},{4,7},{5,6},{6,5},{7,4},{8,11},{9,10},{10,... | collective-permute-start | bytes 589832 | tf_op jit(solution)/shard_map/ppermute | solution.py:529
  20.1 13.3 %collective-permute-start.3 = (f32[4,96,128]{2,1,0:T(8,128)S(1)}, f32[4,96,128]{2,1,0:T(8,128)S(1)}, u32[]{:S(2)}, u32[]{:S(2)}) collective-permute-start(f32[4,96,128]{2,1,0:T(8,128)S(1)} %get-tuple-element.38), channel_id=1, source_target_pairs={{0,2},{1,3},{2,0},{3,1},{4,6},{5,7},{6,4},{7,5},{8,10},{9,11},{10,... | collective-permute-start | bytes 589832 | tf_op jit(solution)/shard_map/ppermute | solution.py:529
  20.5 13.0 %collective-permute-start.2 = (f32[4,96,128]{2,1,0:T(8,128)S(1)}, f32[4,96,128]{2,1,0:T(8,128)S(1)}, u32[]{:S(2)}, u32[]{:S(2)}) collective-permute-start(f32[4,96,128]{2,1,0:T(8,128)S(1)} %get-tuple-element.39), channel_id=1, source_target_pairs={{0,1},{1,0},{2,3},{3,2},{4,5},{5,4},{6,7},{7,6},{8,9},{9,8},{10,11... | collective-permute-start | bytes 589832 | tf_op jit(solution)/shard_map/ppermute | solution.py:529
  28.3 40.1 %all-to-all-start = ((f32[16,96,128]{2,1,0:T(8,128)}), f32[16,96,128]{2,1,0:T(8,128)S(1)}, u32[]{:S(2)}, u32[]{:S(2)}) async-start(f32[16,96,128]{2,1,0:T(8,128)} %shard_map.75), calls=%async_computation | async-start | bytes 1572864 | tf_op jit(solution)/shard_map/all_to_all | solution.py:516
  33.5 15.9 %collective-permute-start.5 = (f32[4,96,128]{2,1,0:T(8,128)S(1)}, f32[4,96,128]{2,1,0:T(8,128)S(1)}, u32[]{:S(2)}, u32[]{:S(2)}) collective-permute-start(f32[4,96,128]{2,1,0:T(8,128)S(1)} %pad_maximum_fusion.1), channel_id=1, source_target_pairs={{0,4},{1,5},{2,6},{3,7},{4,8},{5,9},{6,10},{7,11},{8,12},{9,13},{1... | collective-permute-start | bytes 589832 | tf_op jit(solution)/shard_map/ppermute | solution.py:529
  35.0 25.0 %collective-permute-start.6 = (f32[4,96,128]{2,1,0:T(8,128)S(1)}, f32[4,96,128]{2,1,0:T(8,128)S(1)}, u32[]{:S(2)}, u32[]{:S(2)}) collective-permute-start(f32[4,96,128]{2,1,0:T(8,128)S(1)} %pad_maximum_fusion.2), channel_id=1, source_target_pairs={{0,8},{1,9},{2,10},{3,11},{4,12},{5,13},{6,14},{7,15},{8,0},{9,1},... | collective-permute-start | bytes 589832 | tf_op jit(solution)/shard_map/ppermute | solution.py:529
  37.2 22.8 %collective-permute-start.7 = (f32[4,96,128]{2,1,0:T(8,128)S(1)}, f32[4,96,128]{2,1,0:T(8,128)S(1)}, u32[]{:S(2)}, u32[]{:S(2)}) collective-permute-start(f32[4,96,128]{2,1,0:T(8,128)S(1)} %pad_maximum_fusion.3), channel_id=1, source_target_pairs={{0,12},{1,13},{2,14},{3,15},{4,0},{5,1},{6,2},{7,3},{8,4},{9,5},{1... | collective-permute-start | bytes 589832 | tf_op jit(solution)/shard_map/ppermute | solution.py:529
  64.8 12.5 %collective-permute-start.10 = (f32[4,96,128]{2,1,0:T(8,128)S(1)}, f32[4,96,128]{2,1,0:T(8,128)S(1)}, u32[]{:S(2)}, u32[]{:S(2)}) collective-permute-start(f32[4,96,128]{2,1,0:T(8,128)S(1)} %get-tuple-element.33), channel_id=1, source_target_pairs={{0,12},{1,13},{2,14},{3,15},{4,0},{5,1},{6,2},{7,3},{8,4},{9,5},{1... | collective-permute-start | bytes 589832 | tf_op jit(solution)/shard_map/ppermute | solution.py:529
  65.8 23.0 %collective-permute-start.9 = (f32[4,96,128]{2,1,0:T(8,128)S(1)}, f32[4,96,128]{2,1,0:T(8,128)S(1)}, u32[]{:S(2)}, u32[]{:S(2)}) collective-permute-start(f32[4,96,128]{2,1,0:T(8,128)S(1)} %get-tuple-element.34), channel_id=1, source_target_pairs={{0,8},{1,9},{2,10},{3,11},{4,12},{5,13},{6,14},{7,15},{8,0},{9,1},... | collective-permute-start | bytes 589832 | tf_op jit(solution)/shard_map/ppermute | solution.py:529
  68.4 20.4 %collective-permute-start.8 = (f32[4,96,128]{2,1,0:T(8,128)S(1)}, f32[4,96,128]{2,1,0:T(8,128)S(1)}, u32[]{:S(2)}, u32[]{:S(2)}) collective-permute-start(f32[4,96,128]{2,1,0:T(8,128)S(1)} %get-tuple-element.35), channel_id=1, source_target_pairs={{0,4},{1,5},{2,6},{3,7},{4,8},{5,9},{6,10},{7,11},{8,12},{9,13},{1... | collective-permute-start | bytes 589832 | tf_op jit(solution)/shard_map/ppermute | solution.py:529
  71.8 32.6 %all-to-all-start.1 = ((f32[16,96,128]{2,1,0:T(8,128)}), f32[16,96,128]{2,1,0:T(8,128)S(1)}, u32[]{:S(2)}, u32[]{:S(2)}) async-start(f32[16,96,128]{2,1,0:T(8,128)} %bitcast.1), calls=%async_computation.1 | async-start | bytes 1572864 | tf_op jit(solution)/shard_map/all_to_all | solution.py:516
  88.9 8.0 %collective-permute-start.11 = (f32[4,96,128]{2,1,0:T(8,128)S(1)}, f32[4,96,128]{2,1,0:T(8,128)S(1)}, u32[]{:S(2)}, u32[]{:S(2)}) collective-permute-start(f32[4,96,128]{2,1,0:T(8,128)S(1)} %pad_maximum_fusion.5), channel_id=1, source_target_pairs={{0,1},{1,0},{2,3},{3,2},{4,5},{5,4},{6,7},{7,6},{8,9},{9,8},{10,11... | collective-permute-start | bytes 589832 | tf_op jit(solution)/shard_map/ppermute | solution.py:529
  90.4 9.7 %collective-permute-start.12 = (f32[4,96,128]{2,1,0:T(8,128)S(1)}, f32[4,96,128]{2,1,0:T(8,128)S(1)}, u32[]{:S(2)}, u32[]{:S(2)}) collective-permute-start(f32[4,96,128]{2,1,0:T(8,128)S(1)} %pad_maximum_fusion.6), channel_id=1, source_target_pairs={{0,2},{1,3},{2,0},{3,1},{4,6},{5,7},{6,4},{7,5},{8,10},{9,11},{10,... | collective-permute-start | bytes 589832 | tf_op jit(solution)/shard_map/ppermute | solution.py:529
  94.5 5.6 %collective-permute-start.13 = (f32[4,96,128]{2,1,0:T(8,128)S(1)}, f32[4,96,128]{2,1,0:T(8,128)S(1)}, u32[]{:S(2)}, u32[]{:S(2)}) collective-permute-start(f32[4,96,128]{2,1,0:T(8,128)S(1)} %pad_maximum_fusion.7), channel_id=1, source_target_pairs={{0,3},{1,2},{2,1},{3,0},{4,7},{5,6},{6,5},{7,4},{8,11},{9,10},{10,... | collective-permute-start | bytes 589832 | tf_op jit(solution)/shard_map/ppermute | solution.py:529
